TPU v7x, 128 devices: a whole 4x4x4 slice. The times are simulated.
128 devices in a mesh: band: 4 (over y), grid: 32 (over z, x, core).
Axes of the slice: x: 4, y: 4, z: 4, core: 2. Of those that a mesh axis runs over, the one named last changes fastest.
Arguments:
- orbitals: float32 [2, 8, 256, 256, 256], P(None, 'band', 'grid'), may hold values from -6 to 6
- potential: float32 [256, 256, 256], P('grid'), may hold values from -6 to 6
- projectors: float32 [4, 16384, 128], P(None, 'grid'), may hold values from -0.375 to 0.375
- entry_atom: int32 [16384], P('grid'), may hold values from 0 to 511
- entry_block: int32 [16384], P('grid'), may hold values from 0 to 4095
- entry_count: int32 [16384], P('grid'), may hold values from 1 to 128
- owner_slot: int32 [512], replicated, may hold values from 0 to 511, each once
- strength: float32 [512], replicated, may hold values from 0.1 to 1
Outputs:
- propagated: float32 [2, 8, 256, 256, 256], P(None, 'band', 'grid')
- density: float32 [256, 256, 256], P('grid')
- forces: float32 [3, 512], P(None, 'grid')
Inputs may be any that keep to these rules, and one draw needn't show every extreme that they name: `owner_slot`: a permutation: owner slot s belongs to grid device s // 16.
All inputs are finite; a program needn't handle non-finite values.
Results may differ from a plain program's by a relative error of at most 0.00013.
Values sent between devices are 32-bit elements; how exact they have to be, the bound alone decides.
No kernel may reach another device: no remote copies, remote signals or barrier semaphores. Data moves between devices by JAX's collectives and lax.ppermute only.
A program may use at most 128 MiB of HBM per device.

v0:
```python
import math

import jax
import jax.numpy as jnp
from jax import lax
from jax.sharding import PartitionSpec as P

NX = 256
NY = 256
NZ = 256


TIME_STEP = 4.0
HIGHEST = lax.Precision.HIGHEST


def wave_square(index, size):
    freq = jnp.where(index < size // 2, index, index - size).astype(jnp.float32)
    wave = freq * (2.0 * math.pi / size)
    return wave * wave


def turn(real_part, imag_part, cosine, sine):
    return (cosine * real_part + sine * imag_part, cosine * imag_part - sine * real_part)


def couple(values, strength):
    theta = TIME_STEP * strength
    less_one = jnp.cos(theta) - 1.0
    sine = jnp.sin(theta)
    return jnp.stack(
        [less_one * values[0] + sine * values[1], less_one * values[1] - sine * values[0]]
    )


def transform(field, form, length, sign):
    index = jnp.arange(length, dtype=jnp.int32)
    product = index[:, None] * index[None, :] % length
    angle = product.astype(jnp.float32) * (2.0 * math.pi / length)
    cos_table = jnp.cos(angle)
    sin_table = jnp.sin(angle)
    cos_real = jnp.einsum(form, field[0], cos_table, precision=HIGHEST)
    cos_imag = jnp.einsum(form, field[1], cos_table, precision=HIGHEST)
    sin_real = jnp.einsum(form, field[0], sin_table, precision=HIGHEST)
    sin_imag = jnp.einsum(form, field[1], sin_table, precision=HIGHEST)
    real_part = cos_real - sign * sin_imag
    imag_part = cos_imag + sign * sin_real
    if sign > 0:
        real_part = real_part / length
        imag_part = imag_part / length
    return jnp.stack([real_part, imag_part])


def line_section(lines, first_row):
    lines = transform(lines, "anyz,kn->akyz", NX, -1)
    rows_here = lines.shape[3]
    kinetic = (
        0.5
        * TIME_STEP
        * (
            wave_square(jnp.arange(NX, dtype=jnp.int32), NX)[:, None, None]
            + wave_square(first_row + jnp.arange(rows_here, dtype=jnp.int32), NY)[None, :, None]
            + wave_square(jnp.arange(NZ, dtype=jnp.int32), NZ)[None, None, :]
        )
    )
    real_part, imag_part = turn(lines[0], lines[1], jnp.cos(kinetic), jnp.sin(kinetic))
    return transform(jnp.stack([real_part, imag_part]), "anyz,kn->akyz", NX, 1)


def body(
    orbitals, potential, projectors, entry_atom, entry_block, entry_count, owner_slot, strength
):
    orbs = orbitals.shape[1]
    planes = orbitals.shape[2]
    depth = orbitals.shape[4]
    width = projectors.shape[2]
    angle = 0.5 * TIME_STEP * potential
    cosine = jnp.cos(angle)
    sine = jnp.sin(angle)
    real_part, imag_part = turn(orbitals[0], orbitals[1], cosine, sine)
    shifted = jnp.stack([real_part, imag_part])
    blocks = planes * NY * depth // width
    flat = shifted.reshape(2, orbs, blocks, width)
    points = jnp.arange(width, dtype=jnp.int32)
    masked = projectors * (points[None, :] < entry_count[:, None]).astype(jnp.float32)[None]
    gathered = jnp.take(flat, entry_block, axis=2)
    intersections = jnp.einsum("fep,coep->fcoe", masked, gathered, precision=HIGHEST)
    atoms = owner_slot.shape[0]
    atom_ids = jnp.arange(atoms, dtype=jnp.int32)
    entry_slot = jnp.sum(
        jnp.where(entry_atom[:, None] == atom_ids[None, :], owner_slot[None, :], 0), axis=1
    )
    to_slot = (entry_slot[:, None] == atom_ids[None, :]).astype(jnp.float32)
    partials = jnp.einsum("fcoe,es->fcos", intersections, to_slot, precision=HIGHEST)
    owned = atoms // lax.axis_size("grid")
    begin = lax.axis_index("grid") * owned
    strength_mine = lax.dynamic_slice_in_dim(strength, begin, owned)
    mine = lax.psum_scatter(partials, "grid", scatter_dimension=3, tiled=True)
    coef_all = lax.all_gather(couple(mine[0], strength_mine), "grid", axis=2, tiled=True)
    force_local = -2.0 * strength_mine * jnp.sum(mine[0][None] * mine[1:], axis=(1, 2))
    forces = lax.psum(force_local, "band")
    entry_coef = jnp.einsum("cos,es->coe", coef_all, to_slot, precision=HIGHEST)
    flat = flat.at[:, :, entry_block, :].add(entry_coef[..., None] * masked[0][None, None])
    field = flat.reshape(shifted.shape)
    field = transform(field, "abcn,kn->abck", NZ, -1)
    field = transform(field, "abnd,kn->abkd", NY, -1)
    items = lax.all_to_all(field, "grid", split_axis=3, concat_axis=2, tiled=True)
    first_row = lax.axis_index("grid") * items.shape[3]
    done = line_section(items, first_row)
    field = lax.all_to_all(done, "grid", split_axis=2, concat_axis=3, tiled=True)
    field = transform(field, "abnd,kn->abkd", NY, 1)
    field = transform(field, "abcn,kn->abck", NZ, 1)
    real_part, imag_part = turn(field[0], field[1], cosine, sine)
    density_local = jnp.sum(real_part * real_part + imag_part * imag_part, axis=0)
    density = lax.psum(density_local, "band")
    return (jnp.stack([real_part, imag_part]), density, forces)


def solution(mesh):
    in_specs = (
        P(None, "band", "grid", None, None),
        P("grid", None, None),
        P(None, "grid", None),
        P("grid"),
        P("grid"),
        P("grid"),
        P(),
        P(),
    )
    out_specs = (P(None, "band", "grid", None, None), P("grid", None, None), P(None, "grid"))
    return jax.shard_map(body, mesh=mesh, in_specs=in_specs, out_specs=out_specs, check_vma=False)
```

profile of v0, /device:TPU:0, one launch (start us, length us, event | category | flops | bytes accessed | tf_op | source)
XLA Modules:
  0.0 697.0 jit_solution(4358139962994286035)
XLA Ops:
  8.6 10.5 %broadcast_multiply_fusion.1 = (f32[8,256,256]{2,1,0:T(8,128)}, f32[8,256,256]{2,1,0:T(8,128)}, f32[8,256,256]{2,1,0:T(8,128)S(1)}, f32[8,256,256]{2,1,0:T(8,128)S(1)}) fusion(f32[8,256,256]{2,1,0:T(8,128)} %param.9), kind=kLoop, calls=%fused_computation.68 | loop fusion | flops 1572864 | bytes 10485760 | tf_op jit(solution)/shard_map/mul | solution.py:24
  22.9 4.8 stack.41
  27.7 8.7 %copy_dynamic-update-slice_fusion.1 = f32[2,2,4096,128]{3,1,2,0:T(2,128)} fusion(f32[1,2,4096,128]{3,2,1,0:T(8,128)} %stack.41), kind=kLoop, calls=%fused_computation.28 | loop fusion | bytes 8388608
  36.4 4.8 stack.42
  41.4 8.8 %copy_dynamic-update-slice_fusion = f32[2,2,4096,128]{3,1,2,0:T(2,128)} fusion(f32[2,2,4096,128]{3,1,2,0:T(2,128)} %copy_dynamic-update-slice_fusion.1, f32[1,2,4096,128]{3,2,1,0:T(8,128)} %stack.42), kind=kLoop, calls=%fused_computation.27 | loop fusion | bytes 8388608 | tf_op jit(solution)/shard_map/stack | solution.py:81
  50.2 5.6 gather_fusion
  56.2 7.1 %convolution_bitcast_fusion = f32[4,2,2,512]{0,2,1,3:T(2,128)S(1)} fusion(f32[4,512,128,1]{2,1,0,3:T(8,128)S(1)} %fusion.231, f32[512,2,2,128]{3,2,1,0:T(2,128)S(1)} %gather_fusion, pred[512]{0:T(512)(128)(4,1)S(1)} %compare_and_fusion), kind=kOutput, calls=%fused_computation.61 | convolution fusion | flops 12845056 | bytes 2130432 | tf_op jit(solution)/shard_map/fep,coep->fcoe/dot_general | solution.py:87
  67.5 78.7 %reduce-scatter.4.cloned.1.call-done = f32[16,16]{1,0:T(8,128)} async-done(((f32[512,16]{1,0:T(8,128)}), f32[16,16]{1,0:T(8,128)}) %reduce-scatter.4.cloned.1.call-update) | async-done | bytes 1040
  147.3 24.6 %all_gather.3 = f32[2,2,512]{1,0,2:T(2,128)S(1)} all-gather(f32[2,2,16]{1,0,2:T(2,128)S(1)} %copy.44), channel_id=1, replica_groups=mesh['band'=4,'grid'=32] {'grid'}, dimensions={2}, use_global_device_ids=true | all-gather | bytes 8448 | tf_op jit(solution)/shard_map/all_gather | solution.py:99
  176.0 53.8 %scatter_fusion = f32[2,2,4096,128]{3,1,2,0:T(2,128)} fusion(f32[2,2,4096,128]{3,1,2,0:T(2,128)} %copy_dynamic-update-slice_fusion, s32[512]{0:T(512)S(1)} %compare_select_fusion, f32[512,2,2,128]{3,2,1,0:T(2,128)S(1)} %multiply_bitcast_fusion.2), kind=kCustom, calls=%fused_computation.1 | custom fusion | flops 262144 | bytes 3147776 | tf_op jit(solution)/shard_map/scatter-add | solution.py:103
  229.8 5.8 fusion.217
  237.9 5.2 squeeze.18
  243.1 8.7 %fusion.80 = f32[2,8,256,256]{3,2,1,0:T(8,128)} fusion(f32[2,8,256,256]{3,2,1,0:T(8,128)} %squeeze.18), kind=kOutput, calls=%fused_computation.115 | convolution fusion | flops 3222142976 | bytes 8388608 | tf_op jit(solution)/shard_map/abcn,kn->abck/dot_general | solution.py:42
  254.1 5.2 squeeze.38
  259.4 7.5 %fusion.76 = f32[2,8,256,256]{3,2,1,0:T(8,128)S(1)} fusion(f32[2,8,256,256]{3,2,1,0:T(8,128)} %squeeze.38), kind=kOutput, calls=%fused_computation.111 | convolution fusion | flops 3222142976 | bytes 8388608 | tf_op jit(solution)/shard_map/abcn,kn->abck/dot_general | solution.py:43
  266.9 4.4 multiply_subtract_fusion.3
  271.4 4.7 fusion.78
  276.1 4.8 multiply_add_fusion.3
  281.0 4.7 fusion.74
  285.7 5.5 subtract_bitcast_fusion
  291.2 5.7 add_bitcast_fusion
  297.8 8.3 %copy.49 = f32[2,2,8,256,256]{4,2,1,0,3:T(8,128)} copy(f32[2,2,8,256,256]{4,3,2,1,0:T(8,128)S(1)} %pad_maximum_fusion) | data formatting | bytes 16777216 | tf_op jit(solution)/shard_map/stack | solution.py:51
  306.0 5.0 all-to-all-start
  311.1 9.2 %fusion.35 = (f32[256,8,256]{2,0,1:T(8,128)S(1)}, f32[256,8,256]{2,0,1:T(8,128)}) fusion(f32[256]{0:T(256)S(1)} %fusion.114, f32[256,8]{0,1:T(8,128)S(1)} %broadcast_add_fusion), kind=kLoop, calls=%fused_computation.58 | loop fusion | flops 1048576 | bytes 4203520 | tf_op jit(solution)/shard_map/cos | solution.py:66
  320.3 96.5 %all-to-all-done = f32[2,2,8,256,256]{4,2,1,0,3:T(8,128)} async-done(((f32[2,2,8,256,256]{4,2,1,0,3:T(8,128)}), f32[2,2,8,256,256]{4,2,1,0,3:T(8,128)}, u32[]{:S(2)}, u32[]{:S(2)}) %all-to-all-start) | async-done | bytes 8388640 | tf_op jit(solution)/shard_map/all_to_all | solution.py:107
  416.9 4.5 copy.76
  421.4 4.8 fusion.16
  426.1 4.7 fusion.17
  430.9 5.2 multiply_add_fusion.2
  436.1 5.0 multiply_subtract_fusion.2
  441.1 7.2 %fusion.10 = f32[256,2,8,256]{3,0,2,1:T(8,128)} fusion(f32[256,2,8,256]{3,0,2,1:T(8,128)S(1)} %multiply_subtract_fusion.2, f32[256,2,8,256]{3,0,2,1:T(8,128)S(1)} %multiply_add_fusion.2, f32[256,8,256]{2,0,1:T(8,128)S(1)} %copy-done, f32[256,8,256]{2,0,1:T(8,128)S(1)} %get-tuple-element.16), kind=kOutput, calls=%fused_computation.21 | convolution fusion | flops 3225288704 | bytes 16777216 | tf_op jit(solution)/shard_map/anyz,kn->akyz/dot_general | solution.py:45
  448.4 5.4 fusion.8
  453.8 7.9 %multiply_bitcast_fusion.1 = f32[1,2,256,8,256]{4,2,3,1,0:T(8,128)S(1)} fusion(f32[256,2,8,256]{3,0,2,1:T(8,128)} %fusion.10, f32[256,2,8,256]{3,0,2,1:T(8,128)S(1)} %multiply_add_fusion.2, f32[256,2,8,256]{3,0,2,1:T(8,128)S(1)} %multiply_subtract_fusion.2, f32[256,8,256]{2,0,1:T(8,128)S(1)} %copy-done, f32[256,8,256]{2,0,1:T(8,128)S(1)} %get-tuple-element.16), kind=kOutput, calls=%fused_computation.35 | convolution fusion | flops 3227385856 | bytes 20971520 | tf_op jit(solution)/shard_map/anyz,kn->akyz/dot_general | solution.py:42
  461.7 7.8 %multiply_bitcast_fusion = f32[1,2,256,8,256]{4,2,3,1,0:T(8,128)} fusion(f32[256,2,8,256]{3,0,2,1:T(8,128)S(1)} %fusion.8, f32[256,2,8,256]{3,0,2,1:T(8,128)S(1)} %multiply_add_fusion.2, f32[256,2,8,256]{3,0,2,1:T(8,128)S(1)} %multiply_subtract_fusion.2, f32[256,8,256]{2,0,1:T(8,128)S(1)} %copy-done, f32[256,8,256]{2,0,1:T(8,128)S(1)} %get-tuple-element.16), kind=kOutput, calls=%fused_computation.34 | convolution fusion | flops 3227385856 | bytes 20971520 | tf_op jit(solution)/shard_map/anyz,kn->akyz/dot_general | solution.py:44
  472.4 4.9 copy.51
  477.3 99.8 %all_to_all.30 = f32[2,2,256,8,256]{4,3,1,0,2:T(8,128)} all-to-all(f32[2,2,256,8,256]{4,3,1,0,2:T(8,128)S(1)} %copy.51), channel_id=1, replica_groups=mesh['band'=4,'grid'=32] {'grid'}, dimensions={2} | all-to-all | bytes 16777216 | tf_op jit(solution)/shard_map/all_to_all | solution.py:110
  577.0 4.3 copy.75
  581.4 5.2 fusion.21
  586.6 5.2 fusion.20
  591.8 5.5 add_multiply_fusion
  597.3 4.4 fusion.2
  601.7 5.0 fusion
  606.7 5.6 subtract_multiply_fusion
  612.4 4.7 fusion.28
  617.1 11.2 %add_reduce_fusion = (f32[8,256,256]{2,1,0:T(8,128)}, f32[1,2,8,256,256]{4,3,2,1,0:T(8,128)}, f32[1,2,8,256,256]{4,3,2,1,0:T(8,128)}) fusion(f32[8,256,256]{2,1,0:T(8,128)S(1)} %copy-done.4, f32[2,8,256,256]{3,2,1,0:T(8,128)S(1)} %fusion.28, f32[8,256,256]{2,1,0:T(8,128)S(1)} %copy-done.3, f32[2,8,256,256]{3,2,1,0:T(8,128)S(1)} %fusion, ...), kind=kOutput, calls=%fused_computation.29 | convolution fusion | flops 3233153024 | bytes 27262976 | tf_op jit(solution)/shard_map/abcn,kn->abck/dot_general | solution.py:44
  628.6 11.0 %psum.15 = f32[3,16]{1,0:T(4,128)} all-reduce(f32[3,16]{1,0:T(4,128)S(1)} %broadcast_multiply_fusion.3), channel_id=1, replica_groups=mesh['band'=4,'grid'=32] {'band'}, use_global_device_ids=true, to_apply=%region_6.7 | all-reduce | flops 48 | bytes 384 | tf_op jit(solution)/shard_map/psum | solution.py:101
  639.6 7.8 %pad_maximum_fusion.2 = f32[2,2,8,256,256]{4,3,2,1,0:T(8,128)} fusion(f32[1,2,8,256,256]{4,3,2,1,0:T(8,128)} %get-tuple-element.4, f32[1,2,8,256,256]{4,3,2,1,0:T(8,128)} %get-tuple-element.5), kind=kLoop, calls=%fused_computation.4 | loop fusion | flops 2097152 | bytes 16777216 | tf_op jit(solution)/shard_map/stack | solution.py:116
  647.4 39.5 %all-reduce.2.cloned.1.call-done = f32[8,256,256]{2,1,0:T(8,128)} async-done(((f32[8,256,256]{2,1,0:T(8,128)}), f32[8,256,256]{2,1,0:T(8,128)}) %all-reduce.2.cloned.1.call-update) | async-done | bytes 2097168 | tf_op jit(solution)/shard_map/psum | solution.py:115
  (64 shorter events, 27.1 us)
Async XLA Ops:
  7.2 139.0 %reduce-scatter.4.cloned.1.call-start = ((), (), s32[]{:S(2)}) async-start(), calls=%async_computation.4 | async-start | bytes 270336
  8.6 10.5 %copy-start.7 = (f32[2,2,8,256,256]{4,3,2,1,0:T(8,128)S(1)}, f32[2,2,8,256,256]{4,3,2,1,0:T(8,128)}, u32[]{:S(2)}) copy-start(f32[2,2,8,256,256]{4,3,2,1,0:T(8,128)} %param.8) | copy-start | bytes 25165828
  36.4 4.8 copy-start.9
  41.4 14.4 %copy-start.8 = (f32[4,512,128]{2,1,0:T(8,128)S(1)}, f32[4,512,128]{2,1,0:T(8,128)}, u32[]{:S(2)}) copy-start(f32[4,512,128]{2,1,0:T(8,128)} %param.10) | copy-start | bytes 3145732
  50.2 5.7 copy-start.10
  50.2 5.7 copy-start.11
  243.1 8.7 %copy-start.6 = (f32[1,2,4096,128]{3,1,2,0:T(2,128)S(1)}, f32[1,2,4096,128]{3,1,2,0:T(2,128)}, u32[]{:S(2)}) copy-start(f32[1,2,4096,128]{3,1,2,0:T(2,128)} %get-tuple-element.9) | copy-start | bytes 12582916
  259.4 7.5 %copy-start.2 = (f32[2,8,256,256]{3,2,1,0:T(8,128)S(1)}, f32[2,8,256,256]{3,2,1,0:T(8,128)}, u32[]{:S(2)}) copy-start(f32[2,8,256,256]{3,2,1,0:T(8,128)} %squeeze.38) | copy-start | bytes 12582916
  259.4 7.5 %copy-start.5 = (f32[2,8,256,256]{3,2,1,0:T(8,128)S(1)}, f32[2,8,256,256]{3,2,1,0:T(8,128)}, u32[]{:S(2)}) copy-start(f32[2,8,256,256]{3,2,1,0:T(8,128)} %fusion.80) | copy-start | bytes 12582916
  271.3 4.8 copy-start.1
  306.0 110.8 %all-to-all-start = ((f32[2,2,8,256,256]{4,2,1,0,3:T(8,128)}), f32[2,2,8,256,256]{4,2,1,0,3:T(8,128)}, u32[]{:S(2)}, u32[]{:S(2)}) async-start(f32[2,2,8,256,256]{4,2,1,0,3:T(8,128)} %copy.49), calls=%async_computation | async-start | bytes 16777216 | tf_op jit(solution)/shard_map/all_to_all | solution.py:107
  311.0 375.9 %all-reduce.2.cloned.1.call-start = ((), (), s32[]{:S(2)}) async-start(), calls=%async_computation.3 | async-start | bytes 4194304 | tf_op jit(solution)/shard_map/psum | solution.py:115
  436.1 5.0 copy-start
  612.4 4.7 copy-start.3
  612.4 4.7 copy-start.4
Sparse Core Ops, SparseCore 0:
  66.7 79.4 reduce-scatter.3
  628.4 58.5 all-reduce.1
where the time goes:
time: 708 us; the launch traced here: 697 us
  waiting for transfers between devices  215 us (30%)
  matrix products  150 us (21%)
  blocking collectives  135 us (19%)
  other arithmetic  94.5 us (13%)
  local copies, waits for them, and re-layouts  82.4 us (12%)
  between operations  14.7 us (2%)
    all_to_all x1, blocking collectives, body(): lax.all_to_all(done, 'grid', split_axis=2, concat_axis=3, tiled=True)  99.8 us
    all_to_all x1, waiting for transfers between devices, body(): lax.all_to_all(field, 'grid', split_axis=3, concat_axis=2, tiled=True)  96.5 us
    unnamed x3, waiting for transfers between devices  78.7 us
    scatter-add x1, other arithmetic, body(): flat.at[:, :, entry_block, :]  53.8 us
    psum x1, waiting for transfers between devices, body(): density = lax.psum(density_local, 'band')  39.5 us
    dot_general x6, matrix products, transform(): sin_real = jnp.einsum(form, field[0], sin_table, precision=HIGHEST)  39.5 us
    dot_general x6, matrix products, transform(): cos_real = jnp.einsum(form, field[0], cos_table, precision=HIGHEST)  36 us
    dot_general x6, matrix products, transform(): cos_imag = jnp.einsum(form, field[1], cos_table, precision=HIGHEST)  33.3 us
  transfers between devices with their start and end apart: 3, of which 3 were waited for; matrix products, arithmetic and copies ran while one was open for 3% of the time, Pallas kernels for 0%

commit v1 on v0

v1 whole, which is shorter than its diff:
```python
import functools
import math

import jax
import jax.numpy as jnp
import ml_dtypes
import numpy as np
from jax import lax
from jax.experimental import pallas as pl
from jax.experimental.pallas import tpu as pltpu
from jax.sharding import PartitionSpec as P

SIZE = 256
HALF = SIZE // 2
LANES = 128
TIME_STEP = 4.0
HIGHEST = lax.Precision.HIGHEST
ORBS = 2
PLANES = 8
GROUPS = 32
ENTRIES = 512
ATOMS = 512
FIRST = 6
MIB = 1 << 20


def propagator_tables():
    index = np.arange(SIZE)
    freq = np.where(index < HALF, index, index - SIZE)
    wave = freq * (2.0 * math.pi / SIZE)
    line = np.fft.ifft(np.exp(-0.5j * TIME_STEP * wave * wave))
    full = line[(index[:, None] - index[None, :]) % SIZE]
    parts = []
    for sign in (1.0, -1.0):
        half = 0.5 * (full[:HALF, :HALF] + sign * full[:HALF, HALF:])
        real = np.block([[half.real, -half.imag], [half.imag, half.real]]).astype(np.float32)
        high = real.astype(ml_dtypes.bfloat16)
        low = (real - high.astype(np.float32)).astype(ml_dtypes.bfloat16)
        parts += [high, low]
    left = np.stack(parts)
    return left, np.ascontiguousarray(np.swapaxes(left, 1, 2))


def cos_sin(angle):
    turns = jnp.floor(angle * (2.0 / math.pi) + 0.5)
    rest = angle - turns * 1.5703125
    rest = rest - turns * 4.837512969970703125e-4
    rest = rest - turns * 7.54978995489188216e-8
    square = rest * rest
    sine = ((-1.9515295891e-4 * square + 8.3321608736e-3) * square - 1.6666654611e-1) * square * rest + rest
    cosine = ((2.443315711809948e-5 * square - 1.388731625493765e-3) * square + 4.166664568298827e-2) * (
        square * square
    ) - 0.5 * square + 1.0
    quarter = turns.astype(jnp.int32)
    odd = (quarter & 1) == 1
    cos_out = jnp.where(odd, sine, cosine)
    sin_out = jnp.where(odd, cosine, sine)
    cos_out = jnp.where(((quarter + 1) & 2) == 2, -cos_out, cos_out)
    sin_out = jnp.where((quarter & 2) == 2, -sin_out, sin_out)
    return cos_out, sin_out


def two_parts(values):
    high = values.astype(jnp.bfloat16)
    low = (values - high.astype(jnp.float32)).astype(jnp.bfloat16)
    return high, low


def three_parts(values):
    high = values.astype(jnp.bfloat16)
    rest = values - high.astype(jnp.float32)
    middle = rest.astype(jnp.bfloat16)
    low = (rest - middle.astype(jnp.float32)).astype(jnp.bfloat16)
    return jnp.concatenate([high, middle, low], axis=0)


def dot(left, right):
    return jnp.dot(left, right, preferred_element_type=jnp.float32)


def left_product(table, at, values):
    high, low = two_parts(values)
    return dot(table[at], high) + dot(table[at], low) + dot(table[at + 1], high)


def right_product(table, at, values):
    high, low = two_parts(values)
    return dot(high, table[at]) + dot(low, table[at]) + dot(high, table[at + 1])


def propagate_rows(table, real, imag):
    plus = jnp.concatenate([real[:HALF] + real[HALF:], imag[:HALF] + imag[HALF:]], axis=0)
    minus = jnp.concatenate([real[:HALF] - real[HALF:], imag[:HALF] - imag[HALF:]], axis=0)
    plus = left_product(table, 0, plus)
    minus = left_product(table, 2, minus)
    low, high = plus + minus, plus - minus
    return (
        jnp.concatenate([low[:HALF], high[:HALF]], axis=0),
        jnp.concatenate([low[HALF:], high[HALF:]], axis=0),
    )


def propagate_lanes(table, real, imag):
    plus = jnp.concatenate([real[0] + real[1], imag[0] + imag[1]], axis=1)
    minus = jnp.concatenate([real[0] - real[1], imag[0] - imag[1]], axis=1)
    plus = right_product(table, 0, plus)
    minus = right_product(table, 2, minus)
    low, high = plus + minus, plus - minus
    return (
        jnp.concatenate([low[:, :HALF], high[:, :HALF]], axis=1),
        jnp.concatenate([low[:, HALF:], high[:, HALF:]], axis=1),
    )


def atom_matrix(atom_ref):
    atoms = lax.broadcasted_iota(jnp.int32, (ATOMS, ENTRIES), 0)
    return jnp.where(atoms == atom_ref[...], 1.0, 0.0).astype(jnp.bfloat16)


def project_kernel(
    block, count, atom_ref, orbs_hbm, potential_hbm, projectors, sent, partial_ref, masked_ref,
    orbs, potential, rows, counts, table, packed, sems,
):
    half_rows = PLANES * SIZE

    def load(source, into, sem):
        return [
            pltpu.make_async_copy(
                source.at[:, pl.ds(z * LANES, LANES)], into.at[pl.ds(z * half_rows, half_rows)], sem.at[z]
            )
            for z in range(2)
        ]

    copies = [load(potential_hbm, potential, sems.at[4])]
    copies += [load(orbs_hbm.at[k], orbs.at[k], sems.at[k]) for k in range(4)]
    for pair in copies:
        for copy in pair:
            copy.start()

    def arrived(pair):
        for copy in pair:
            copy.wait()

    def place(entry):
        at = block[entry]
        return (at & 1) * half_rows + lax.shift_right_logical(at, 1)

    arrived(copies[0])

    def first(entry, carry):
        rows[4, pl.ds(entry, 1), :] = potential[pl.ds(place(entry), 1), :]
        counts[pl.ds(entry, 1), :] = jnp.full((1, LANES), count[entry], jnp.int32)
        return carry

    lax.fori_loop(0, ENTRIES, first, 0, unroll=8)
    for k in range(4):
        arrived(copies[k + 1])

        def step(entry, carry):
            rows[k, pl.ds(entry, 1), :] = orbs[k, pl.ds(place(entry), 1), :]
            return carry

        lax.fori_loop(0, ENTRIES, step, 0, unroll=8)

    piece = 64

    def reduce(index, carry):
        at = pl.ds(pl.multiple_of(index * piece, piece), piece)
        lane = lax.broadcasted_iota(jnp.int32, (piece, LANES), 1)
        cosine, sine = cos_sin((0.5 * TIME_STEP) * rows[4, at, :])
        inside = lane < counts[at, :]
        fields = []
        for n in range(ORBS):
            real, imag = rows[n, at, :], rows[ORBS + n, at, :]
            fields += [(n, cosine * real + sine * imag), (ORBS + n, cosine * imag - sine * real)]
        out = jnp.zeros((piece, LANES), jnp.float32)
        for f in range(4):
            masked = jnp.where(inside, projectors[f, at, :], 0.0)
            if f == 0:
                masked_ref[at, :] = masked
            for k, field in fields:
                total = jnp.sum(masked * field, axis=1, keepdims=True)
                out = jnp.where(lane == f * 4 + k, total, out)
        table[at, :] = out
        return carry

    lax.fori_loop(0, ENTRIES // piece, reduce, 0)
    turned = jnp.transpose(table[...])[:16]
    sums = lax.dot_general(
        three_parts(turned), atom_matrix(atom_ref), (((1,), (1,)), ((), ())), preferred_element_type=jnp.float32
    )
    sums = sums[:16] + sums[16:32] + sums[32:]
    partial_ref[...] = sums
    for k in range(4):
        for q in range(4):
            packed[k * 4 + q : k * 4 + q + 1, :] = sums[k : k + 1, q * LANES : (q + 1) * LANES]
    for d in range(GROUPS):
        sent[d] = packed[...]


def project(orbs, potential, projectors, entry_atom, entry_block, entry_count):
    smem = pl.BlockSpec(memory_space=pltpu.SMEM)
    vmem = pl.BlockSpec(memory_space=pltpu.VMEM)
    hbm = pl.BlockSpec(memory_space=pl.ANY)
    rows = PLANES * SIZE
    return pl.pallas_call(
        project_kernel,
        out_shape=(
            jax.ShapeDtypeStruct((GROUPS, 16, LANES), jnp.float32),
            jax.ShapeDtypeStruct((16, ATOMS), jnp.float32),
            jax.ShapeDtypeStruct((ENTRIES, LANES), jnp.float32),
        ),
        in_specs=[smem, smem, vmem, hbm, hbm, vmem],
        out_specs=(vmem, vmem, vmem),
        scratch_shapes=[
            pltpu.VMEM((4, 2 * rows, LANES), jnp.float32),
            pltpu.VMEM((2 * rows, LANES), jnp.float32),
            pltpu.VMEM((5, ENTRIES, LANES), jnp.float32),
            pltpu.VMEM((ENTRIES, LANES), jnp.int32),
            pltpu.VMEM((ENTRIES, LANES), jnp.float32),
            pltpu.VMEM((16, LANES), jnp.float32),
            pltpu.SemaphoreType.DMA((5, 2)),
        ],
        compiler_params=pltpu.CompilerParams(vmem_limit_bytes=32 * MIB),
        cost_estimate=pl.CostEstimate(flops=10**9, bytes_accessed=36 * 10**6, transcendentals=0),
        name="project",
    )(entry_block, entry_count, entry_atom.reshape(1, ENTRIES), orbs, potential, projectors)


SHIFT_STEP = 4


def shift_kernel(orbs, potential, first, second):
    for x in range(PLANES):
        cosine, sine = cos_sin((0.5 * TIME_STEP) * potential[x])
        for n, out in enumerate((first, second)):
            real, imag = orbs[0, n, x], orbs[1, n, x]
            both = (cosine * real + sine * imag, cosine * imag - sine * real)
            for c in range(2):
                for d in range(SHIFT_STEP):
                    for z in range(2):
                        tile = both[c][d * 8 : d * 8 + 8, z * LANES : (z + 1) * LANES]
                        out[d, pl.ds(c * 128 + z * 64 + x, 8, stride=8), :] = tile


def shift(orbitals, potential):
    width = SHIFT_STEP * 8
    shape = jax.ShapeDtypeStruct((GROUPS, 256, LANES), jnp.float32)
    spec = pl.BlockSpec((SHIFT_STEP, 256, LANES), lambda i: (i, 0, 0))
    return pl.pallas_call(
        shift_kernel,
        grid=(GROUPS // SHIFT_STEP,),
        out_shape=(shape, shape),
        in_specs=[
            pl.BlockSpec((2, ORBS, PLANES, width, SIZE), lambda i: (0, 0, 0, i, 0)),
            pl.BlockSpec((PLANES, width, SIZE), lambda i: (0, i, 0)),
        ],
        out_specs=(spec, spec),
        compiler_params=pltpu.CompilerParams(vmem_limit_bytes=32 * MIB),
        cost_estimate=pl.CostEstimate(flops=10**8, bytes_accessed=19 * 10**6, transcendentals=0),
        name="shift",
    )(orbitals, potential)


def correct_kernel(n, place, received, strength, atom_ref, masked, before, after, field, coefs, updates, sems):
    load = pltpu.make_async_copy(before, field, sems.at[0])
    load.start()
    sums = jnp.sum(received[...], axis=0)
    real = sums[n * 4 : n * 4 + 4]
    imag = sums[(ORBS + n) * 4 : (ORBS + n) * 4 + 4]
    cosine, sine = cos_sin(TIME_STEP * strength[...])
    less_one = cosine - 1.0
    both = (less_one * real + sine * imag, less_one * imag - sine * real)
    coefs[...] = jnp.zeros_like(coefs)
    for c in range(2):
        for q in range(4):
            coefs[c : c + 1, q * LANES : (q + 1) * LANES] = both[c][q : q + 1]
    spread = dot(three_parts(coefs[...]), atom_matrix(atom_ref))
    spread = jnp.transpose(spread[:16] + spread[16:32] + spread[32:])
    for c in range(2):
        updates[c] = spread[:, c : c + 1] * masked[...]
    load.wait()

    def step(entry, carry):
        row = place[entry]
        for c in range(2):
            at = pl.ds(row + c * 128, 1)
            field[at, :] = field[at, :] + updates[c, pl.ds(entry, 1), :]
        return carry

    lax.fori_loop(0, ENTRIES, step, 0, unroll=8)
    store = pltpu.make_async_copy(field, after, sems.at[1])
    store.start()
    store.wait()


def correct(n, place, received, strength, atoms, masked, before):
    smem = pl.BlockSpec(memory_space=pltpu.SMEM)
    vmem = pl.BlockSpec(memory_space=pltpu.VMEM)
    hbm = pl.BlockSpec(memory_space=pl.ANY)
    return pl.pallas_call(
        functools.partial(correct_kernel, n),
        out_shape=jax.ShapeDtypeStruct((GROUPS * 256, LANES), jnp.float32),
        in_specs=[smem, vmem, vmem, vmem, vmem, hbm],
        out_specs=hbm,
        scratch_shapes=[
            pltpu.VMEM((GROUPS * 256, LANES), jnp.float32),
            pltpu.VMEM((16, ATOMS), jnp.float32),
            pltpu.VMEM((2, ENTRIES, LANES), jnp.float32),
            pltpu.SemaphoreType.DMA((2,)),
        ],
        input_output_aliases={5: 0},
        compiler_params=pltpu.CompilerParams(vmem_limit_bytes=24 * MIB),
        cost_estimate=pl.CostEstimate(flops=5 * 10**8, bytes_accessed=20 * 10**6, transcendentals=0),
        name=f"correct{n}",
    )(place, received, strength, atoms, masked, before.reshape(GROUPS * 256, LANES))


def lines_kernel(n, field, left, right, *rest):
    head, tail, turned, sems = rest[-4:]
    y = pl.program_id(0)
    real = [field[:, 0, z, 0].reshape(SIZE, LANES) for z in range(2)]
    imag = [field[:, 1, z, 0].reshape(SIZE, LANES) for z in range(2)]
    real, imag = propagate_lanes(right, real, imag)
    both = propagate_rows(left, real, imag)
    for c in range(2):
        for z in range(2):
            for d in range(GROUPS):
                tile = both[c][d * 8 : d * 8 + 8, z * LANES : (z + 1) * LANES]
                turned[d, c, z, pl.ds(y, 8, stride=8), :] = tile

    @pl.when(y == pl.num_programs(0) - 1)
    def _():
        cut = FIRST * 8
        copies = [
            pltpu.make_async_copy(turned.at[:, :, :, pl.ds(0, cut)], head.at[:, :, n], sems.at[0]),
            pltpu.make_async_copy(turned.at[:, :, :, pl.ds(cut, 64 - cut)], tail.at[:, :, n], sems.at[1]),
        ]
        for copy in copies:
            copy.start()
        for copy in copies:
            copy.wait()


def lines(n, field, left, right, *before):
    hbm = pl.BlockSpec(memory_space=pl.ANY)
    table = pl.BlockSpec((4, SIZE, SIZE), lambda i: (0, 0, 0))
    return pl.pallas_call(
        functools.partial(lines_kernel, n),
        grid=(8,),
        out_shape=(
            jax.ShapeDtypeStruct((GROUPS, 2, ORBS, 2, FIRST * 8, LANES), jnp.float32),
            jax.ShapeDtypeStruct((GROUPS, 2, ORBS, 2, (PLANES - FIRST) * 8, LANES), jnp.float32),
        ),
        in_specs=[
            pl.BlockSpec((GROUPS, 2, 2, 1, 8, LANES), lambda i: (0, 0, 0, i, 0, 0)),
            table,
            table,
            *[hbm for _ in before],
        ],
        out_specs=(hbm, hbm),
        scratch_shapes=[
            pltpu.VMEM((GROUPS, 2, 2, 64, LANES), jnp.float32),
            pltpu.SemaphoreType.DMA((2,)),
        ],
        input_output_aliases={3 + k: k for k in range(len(before))},
        compiler_params=pltpu.CompilerParams(vmem_limit_bytes=32 * MIB),
        cost_estimate=pl.CostEstimate(flops=5 * 10**9, bytes_accessed=10 * 10**6, transcendentals=0),
        name=f"lines{n}",
    )(field.reshape(GROUPS, 2, 2, 8, 8, LANES), left, right, *before)


def finish_kernel(field, potential, left, *rest):
    out, density = rest[-2:]
    cosine, sine = cos_sin((0.5 * TIME_STEP) * potential[0])
    total = None
    for n in range(ORBS):
        real, imag = (
            jnp.concatenate([field[:, c, n, z].reshape(SIZE, LANES) for z in range(2)], axis=1) for c in range(2)
        )
        real, imag = propagate_rows(left, real, imag)
        real, imag = cosine * real + sine * imag, cosine * imag - sine * real
        out[0, n, 0] = real
        out[1, n, 0] = imag
        square = real * real + imag * imag
        total = square if total is None else total + square
    density[0] = total


def finish(planes, begin, field, potential, left, *before):
    hbm = pl.BlockSpec(memory_space=pl.ANY)
    return pl.pallas_call(
        finish_kernel,
        grid=(planes,),
        out_shape=(
            jax.ShapeDtypeStruct((2, ORBS, PLANES, SIZE, SIZE), jnp.float32),
            jax.ShapeDtypeStruct((planes, SIZE, SIZE), jnp.float32),
        ),
        in_specs=[
            pl.BlockSpec((GROUPS, 2, ORBS, 2, 8, LANES), lambda i: (0, 0, 0, 0, i, 0)),
            pl.BlockSpec((1, SIZE, SIZE), lambda i: (i + begin, 0, 0)),
            pl.BlockSpec((4, SIZE, SIZE), lambda i: (0, 0, 0)),
            *[hbm for _ in before],
        ],
        out_specs=(
            pl.BlockSpec((2, ORBS, 1, SIZE, SIZE), lambda i: (0, 0, i + begin, 0, 0)),
            pl.BlockSpec((1, SIZE, SIZE), lambda i: (i, 0, 0)),
        ),
        input_output_aliases={3 + k: k for k in range(len(before))},
        compiler_params=pltpu.CompilerParams(vmem_limit_bytes=32 * MIB),
        cost_estimate=pl.CostEstimate(flops=10**9 * planes, bytes_accessed=3 * 10**6 * planes, transcendentals=0),
        name=f"finish{begin}",
    )(field, potential, left, *before)


def exchange(array):
    return lax.all_to_all(array, "grid", split_axis=0, concat_axis=0, tiled=True)


def body(left, right, orbitals, potential, projectors, entry_atom, entry_block, entry_count, owner_slot, strength):
    atom_ids = jnp.arange(ATOMS, dtype=jnp.int32)
    rows = PLANES * SIZE
    sent, partials, masked = project(
        orbitals.reshape(2 * ORBS, rows, SIZE), potential.reshape(rows, SIZE), projectors,
        entry_atom, entry_block, entry_count,
    )
    received = exchange(sent)
    shifted = shift(orbitals, potential)
    x, y, z = entry_block // 512, (entry_block // 2) % SIZE, entry_block % 2
    place = (y // 8) * 256 + z * 64 + (y % 8) * 8 + x
    in_slot = owner_slot[:, None] == atom_ids[None, :]
    strength_atom = jnp.sum(jnp.where(in_slot, strength[None, :], 0.0), axis=1).reshape(4, LANES)
    atoms = entry_atom.reshape(1, ENTRIES)
    pencils = [
        exchange(correct(n, place, received, strength_atom, atoms, masked, shifted[n]).reshape(GROUPS, 256, LANES))
        for n in range(ORBS)
    ]
    in_slots = jnp.einsum("ka,as->ks", partials, in_slot.astype(jnp.float32), precision=HIGHEST)
    owned = ATOMS // GROUPS
    mine = lax.psum_scatter(in_slots, "grid", scatter_dimension=1, tiled=True).reshape(4, 2 * ORBS, owned)
    strength_mine = lax.dynamic_slice_in_dim(strength, lax.axis_index("grid") * owned, owned)
    force_local = -2.0 * strength_mine * jnp.sum(mine[0][None] * mine[1:], axis=1)
    forces = lax.psum(force_local, "band")

    back = lines(0, pencils[0], left, right)
    back = lines(1, pencils[1], left, right, *back)
    head = exchange(back[0])
    tail = exchange(back[1])
    out, density_head = finish(FIRST, 0, head, potential, left)
    out, density_tail = finish(PLANES - FIRST, FIRST, tail, potential, left, out)
    density = jnp.concatenate([lax.psum(density_head, "band"), lax.psum(density_tail, "band")], axis=0)
    return out, density, forces


def solution(mesh):
    left, right = propagator_tables()
    in_specs = (
        P(None, "band", "grid", None, None),
        P("grid", None, None),
        P(None, "grid", None),
        P("grid"),
        P("grid"),
        P("grid"),
        P(),
        P(),
    )
    out_specs = (P(None, "band", "grid", None, None), P("grid", None, None), P(None, "grid"))

    def run(*args):
        return body(jnp.asarray(left), jnp.asarray(right), *args)

    return jax.shard_map(run, mesh=mesh, in_specs=in_specs, out_specs=out_specs, check_vma=False)
```

time: 708 us -> 380 us (0.54); the launches traced: 697 us -> 378 us
  matrix products: 150 us -> 1.8 us
  other arithmetic: 94.5 us -> 3.42 us
  waiting for transfers between devices: 215 us -> 152 us
  Pallas kernels: 0 us -> 53.7 us
  blocking collectives: 135 us -> 88.3 us
  local copies, waits for them, and re-layouts: 82.4 us -> 38 us
  starting transfers between devices: 5.05 us -> 25.9 us
    dot_general x27 -> x0, matrix products: 150 us -> none  [the longest x6 39.5 us: transform(): sin_real = jnp.einsum(form, field[0], sin_table, precision=HIGHEST)]
    scatter-add x1 -> x0, other arithmetic: 53.8 us -> none  [body(): flat.at[:, :, entry_block, :]]
    pallas_call x0 -> x8, Pallas kernels: none -> 53.7 us  [the longest x2 18.6 us: lines(): pl.pallas_call(functools.partial(lines_kernel, n), grid=(8,), out_shape=(...]
    psum x1, waiting for transfers between devices: 39.5 us -> 0.01 us  [body(): lax.psum(density_tail, 'band')]
    another operation x6 -> x0, local copies, waits for them, and re-layouts: 31.6 us -> none  [the longest x3 18.4 us: body(): shifted = jnp.stack([real_part, imag_part])]
    unnamed x3, waiting for transfers between devices: 78.7 us -> 49 us
    all_gather x1 -> x0, blocking collectives: 24.6 us -> none  [body(): lax.all_gather(couple(mine[0], strength_mine), 'grid', axis=2, tiled=True)]
    all_to_all x1, blocking collectives: 99.8 us -> 77.3 us  [exchange(): lax.all_to_all(array, 'grid', split_axis=0, concat_axis=0, tiled=True)]
  transfers between devices with their start and end apart: 3 -> 6, of which waited for: 3 -> 4; matrix products, arithmetic and copies ran while one was open for 3% -> 1% of each run, Pallas kernels for 0% -> 8%
where the time goes in v1:
time: 380 us; the launch traced here: 378 us
  waiting for transfers between devices  152 us (40%)
  blocking collectives  88.3 us (23%)
  Pallas kernels  53.7 us (14%)
  local copies, waits for them, and re-layouts  38 us (10%)
  starting transfers between devices  25.9 us (7%)
  between operations  15.7 us (4%)
    all_to_all x4, waiting for transfers between devices, exchange(): lax.all_to_all(array, 'grid', split_axis=0, concat_axis=0, tiled=True)  103 us
    all_to_all x1, blocking collectives, exchange(): lax.all_to_all(array, 'grid', split_axis=0, concat_axis=0, tiled=True)  77.3 us
    unnamed x3, waiting for transfers between devices  49 us
    unnamed x56, local copies, waits for them, and re-layouts  37.2 us
    all_to_all x4, starting transfers between devices, exchange(): lax.all_to_all(array, 'grid', split_axis=0, concat_axis=0, tiled=True)  25.8 us
    pallas_call x2, Pallas kernels, lines(): pl.pallas_call(functools.partial(lines_kernel, n), grid=(8,), out_shape=(...  18.6 us
    pallas_call x2, Pallas kernels, finish(): pl.pallas_call(finish_kernel, grid=(planes,), out_shape=(jax.ShapeDtypeSt...  11.4 us
    psum x1, blocking collectives, body(): forces = lax.psum(force_local, 'band')  11 us
  transfers between devices with their start and end apart: 6, of which 4 were waited for; matrix products, arithmetic and copies ran while one was open for 1% of the time, Pallas kernels for 8%

profile of v1, /device:TPU:0, one launch (start us, length us, event | category | flops | bytes accessed | tf_op | source)
XLA Modules:
  0.0 378.3 jit_solution(12533423481019889897)
XLA Ops:
  8.0 3.4 copy-done
  11.4 1.6 copy-done.2
  13.0 1.2 copy-done.17
  14.2 0.7 copy-done.19
  14.9 0.7 copy-done.21
  15.6 0.7 copy-done.23
  16.3 10.9 %project.1 = (f32[32,16,128]{2,1,0:T(8,128)}, f32[16,512]{1,0:T(8,128)S(1)}, f32[512,128]{1,0:T(8,128)S(1)}) custom-call(s32[512]{0:T(512)S(1)} %copy-done.21, s32[512]{0:T(512)S(1)} %copy-done.23, s32[1,512]{1,0:T(1,128)S(1)} %bitcast.21, f32[4,2048,256]{2,1,0:T(8,128)S(1)} %bitcast.15, f32[2048,256]{1,0:T(8,128)S(1)} %bitcast.16, f32[4,512,128]{2,1,0:T(8,128)S(1)} %copy-done.17), custom_call_target="tpu_custom_call" | custom-call | flops 1000000000 | bytes 36000000 | tf_op jit(solution)/shard_map/project/pallas_call | solution.py:206
  27.2 8.3 %all-to-all-start = ((f32[32,16,128]{2,1,0:T(8,128)}), f32[32,16,128]{2,1,0:T(8,128)S(1)}, u32[]{:S(2)}, u32[]{:S(2)}) async-start(f32[32,16,128]{2,1,0:T(8,128)} %get-tuple-element.16), calls=%async_computation | async-start | bytes 524288 | tf_op jit(solution)/shard_map/all_to_all | solution.py:417
  35.5 0.2 select_reduce_fusion
  35.7 3.4 copy-done.1
  39.1 5.5 %shift.1 = (f32[32,256,128]{2,1,0:T(8,128)S(1)}, f32[32,256,128]{2,1,0:T(8,128)S(1)}) custom-call(f32[2,2,8,256,256]{4,3,2,1,0:T(8,128)S(1)} %copy-done.1, f32[8,256,256]{2,1,0:T(8,128)S(1)} %copy-done.3), custom_call_target="tpu_custom_call" | custom-call | flops 100000000 | bytes 19000000 | tf_op jit(solution)/shard_map/shift/pallas_call | solution.py:250
  44.6 2.0 copy-done.4
  46.6 2.0 copy-done.7
  48.7 2.2 copy-done.8
  50.8 3.6 correct0.1
  54.5 2.0 copy-done.9
  56.5 7.5 %all-to-all-start.2 = ((f32[32,256,128]{2,1,0:T(8,128)}), f32[32,256,128]{2,1,0:T(8,128)}, u32[]{:S(2)}, u32[]{:S(2)}) async-start(f32[32,256,128]{2,1,0:T(8,128)} %bitcast.20), calls=%async_computation.2 | async-start | bytes 8388608 | tf_op jit(solution)/shard_map/all_to_all | solution.py:417
  64.0 2.2 copy-done.5
  66.2 3.6 correct1.1
  69.9 2.0 copy-done.6
  71.9 45.6 %all-to-all-done.2 = f32[32,256,128]{2,1,0:T(8,128)} async-done(((f32[32,256,128]{2,1,0:T(8,128)}), f32[32,256,128]{2,1,0:T(8,128)}, u32[]{:S(2)}, u32[]{:S(2)}) %all-to-all-start.2) | async-done | bytes 4194336 | tf_op jit(solution)/shard_map/all_to_all | solution.py:417
  117.5 5.0 %all-to-all-start.1 = ((f32[32,256,128]{2,1,0:T(8,128)}), f32[32,256,128]{2,1,0:T(8,128)}, u32[]{:S(2)}, u32[]{:S(2)}) async-start(f32[32,256,128]{2,1,0:T(8,128)} %bitcast.18), calls=%async_computation.1 | async-start | bytes 8388608 | tf_op jit(solution)/shard_map/all_to_all | solution.py:417
  122.5 9.3 %lines0.1 = (f32[32,2,2,2,48,128]{5,4,3,2,1,0:T(8,128)S(1)}, f32[32,2,2,2,16,128]{5,4,3,2,1,0:T(8,128)S(1)}) custom-call(f32[32,2,2,8,8,128]{5,4,3,2,1,0:T(8,128)} %bitcast.9.field, bf16[4,256,256]{2,1,0:T(8,128)(2,1)S(1)} %copy-done.18, bf16[4,256,256]{2,1,0:T(8,128)(2,1)S(1)} %copy-done.24), custom_call_target="tpu_custom_call" | custom-call | flops 5000000000 | bytes 10000000 | tf_op jit(solution)/shard_map/lines0/pallas_call | solution.py:348
  131.9 2.7 copy-done.11
  134.6 1.3 copy-done.13
  135.9 40.1 %all-to-all-done.1 = f32[32,256,128]{2,1,0:T(8,128)} async-done(((f32[32,256,128]{2,1,0:T(8,128)}), f32[32,256,128]{2,1,0:T(8,128)}, u32[]{:S(2)}, u32[]{:S(2)}) %all-to-all-start.1) | async-done | bytes 4194336 | tf_op jit(solution)/shard_map/all_to_all | solution.py:417
  176.0 2.8 copy-done.12
  178.8 1.6 copy-done.14
  180.3 9.2 %lines1.1 = (f32[32,2,2,2,48,128]{5,4,3,2,1,0:T(8,128)S(1)}, f32[32,2,2,2,16,128]{5,4,3,2,1,0:T(8,128)S(1)}) custom-call(f32[32,2,2,8,8,128]{5,4,3,2,1,0:T(8,128)} %bitcast.6.field, bf16[4,256,256]{2,1,0:T(8,128)(2,1)S(1)} %copy-done.18, bf16[4,256,256]{2,1,0:T(8,128)(2,1)S(1)} %copy-done.24, ...), custom_call_target="tpu_custom_call", output_to_operand_aliasing={{0}: (3, {}), {1}: (4, {})} | custom-call | flops 5000000000 | bytes 10000000 | tf_op jit(solution)/shard_map/lines1/pallas_call | solution.py:348
  189.6 77.3 %all_to_all.25.field = f32[32,2,2,2,48,128]{5,4,3,2,1,0:T(8,128)} all-to-all(f32[32,2,2,2,48,128]{5,4,3,2,1,0:T(8,128)S(1)} %get-tuple-element.23), channel_id=1, replica_groups=mesh['band'=4,'grid'=32] {'grid'}, dimensions={0} | all-to-all | bytes 12582912 | tf_op jit(solution)/shard_map/all_to_all | solution.py:417
  266.9 5.1 %all-to-all-start.3 = ((f32[32,2,2,2,16,128]{5,4,3,2,1,0:T(8,128)}), f32[32,2,2,2,16,128]{5,4,3,2,1,0:T(8,128)}, u32[]{:S(2)}, u32[]{:S(2)}) async-start(f32[32,2,2,2,16,128]{5,4,3,2,1,0:T(8,128)} %copy-done.15), calls=%async_computation.3 | async-start | bytes 4194304 | tf_op jit(solution)/shard_map/all_to_all | solution.py:417
  271.9 0.0 reduce-scatter.4.cloned.1.call-start
  272.0 1.8 convolution_bitcast_fusion
  273.8 0.0 reduce-scatter.4.cloned.1.call-update
  273.8 0.0 all-reduce.3.cloned.1.call-start
  273.9 2.8 copy-done.10
  276.6 7.2 %finish0.1 = (f32[2,2,8,256,256]{4,3,2,1,0:T(8,128)}, f32[6,256,256]{2,1,0:T(8,128)S(1)}) custom-call(f32[32,2,2,2,48,128]{5,4,3,2,1,0:T(8,128)S(1)} %copy-done.10, f32[8,256,256]{2,1,0:T(8,128)S(1)} %copy-done.3, bf16[4,256,256]{2,1,0:T(8,128)(2,1)S(1)} %copy-done.18), custom_call_target="tpu_custom_call" | custom-call | flops 6000000000 | bytes 18000000 | tf_op jit(solution)/shard_map/finish0/pallas_call | solution.py:392
  283.8 1.2 copy-done.16
  285.0 16.9 %all-to-all-done.3.field = f32[32,2,2,2,16,128]{5,4,3,2,1,0:T(8,128)} async-done(((f32[32,2,2,2,16,128]{5,4,3,2,1,0:T(8,128)}), f32[32,2,2,2,16,128]{5,4,3,2,1,0:T(8,128)}, u32[]{:S(2)}, u32[]{:S(2)}) %all-to-all-start.3) | async-done | bytes 2097184 | tf_op jit(solution)/shard_map/all_to_all | solution.py:417
  301.9 4.2 %finish6.1 = (f32[2,2,8,256,256]{4,3,2,1,0:T(8,128)}, f32[2,256,256]{2,1,0:T(8,128)}) custom-call(f32[32,2,2,2,16,128]{5,4,3,2,1,0:T(8,128)} %all-to-all-done.3.field, f32[8,256,256]{2,1,0:T(8,128)S(1)} %copy-done.3, bf16[4,256,256]{2,1,0:T(8,128)(2,1)S(1)} %copy-done.18, ...), custom_call_target="tpu_custom_call", output_to_operand_aliasing={{0}: (3, {})} | custom-call | flops 2000000000 | bytes 6000000 | tf_op jit(solution)/shard_map/finish6/pallas_call | solution.py:392
  306.1 0.0 all-reduce.3.cloned.1.call-update
  306.1 0.1 dynamic-slice_multiply_fusion
  306.2 48.9 %reduce-scatter.4.cloned.1.call-done = f32[16,16]{1,0:T(8,128)} async-done(((f32[512,16]{1,0:T(8,128)}), f32[16,16]{1,0:T(8,128)}) %reduce-scatter.4.cloned.1.call-update) | async-done | bytes 1040
  355.2 0.8 slice.14
  355.9 0.8 copy.20
  356.7 0.1 copy.21
  356.8 11.0 %psum.23 = f32[3,16]{1,0:T(4,128)} all-reduce(f32[3,16]{1,0:T(4,128)S(1)} %broadcast_multiply_fusion), channel_id=1, replica_groups=mesh['band'=4,'grid'=32] {'band'}, use_global_device_ids=true, to_apply=%region_5.6 | all-reduce | flops 48 | bytes 384 | tf_op jit(solution)/shard_map/psum | solution.py:443
  367.9 3.0 pad_maximum_fusion
  (41 shorter events, 0.2 us)
Async XLA Ops:
  8.0 3.4 copy-start
  11.4 1.6 copy-start.2
  13.0 1.2 copy-start.17
  14.2 0.7 copy-start.19
  14.9 0.7 copy-start.21
  15.6 0.7 copy-start.23
  16.2 19.2 %copy-start.25 = (s32[512]{0:T(512)S(1)}, s32[512]{0:T(512)}, u32[]{:S(2)}) copy-start(s32[512]{0:T(512)} %param.16) | copy-start | bytes 6148
  16.2 19.2 %copy-start.26 = (f32[512]{0:T(512)S(1)}, f32[512]{0:T(512)}, u32[]{:S(2)}) copy-start(f32[512]{0:T(512)} %param.17) | copy-start | bytes 6148
  16.3 19.5 %copy-start.3 = (f32[8,256,256]{2,1,0:T(8,128)S(1)}, f32[8,256,256]{2,1,0:T(8,128)}, u32[]{:S(2)}) copy-start(f32[8,256,256]{2,1,0:T(8,128)} %potential.5) | copy-start | bytes 6291460
  27.2 21.5 %all-to-all-start = ((f32[32,16,128]{2,1,0:T(8,128)}), f32[32,16,128]{2,1,0:T(8,128)S(1)}, u32[]{:S(2)}, u32[]{:S(2)}) async-start(f32[32,16,128]{2,1,0:T(8,128)} %get-tuple-element.16), calls=%async_computation | async-start | bytes 524288 | tf_op jit(solution)/shard_map/all_to_all | solution.py:417
  35.7 3.4 copy-start.1
  39.1 9.5 %copy-start.22 = (s32[512]{0:T(512)S(1)}, s32[512]{0:T(512)}, u32[]{:S(2)}) copy-start(s32[512]{0:T(512)} %block.1) | copy-start | bytes 6148
  39.1 9.5 %copy-start.20 = (s32[512]{0:T(512)S(1)}, s32[512]{0:T(512)}, u32[]{:S(2)}) copy-start(s32[512]{0:T(512)} %param.13) | copy-start | bytes 6148
  44.6 2.0 copy-start.4
  46.6 2.0 copy-start.7
  48.7 2.2 copy-start.8
  54.5 2.0 copy-start.9
  56.5 61.0 %all-to-all-start.2 = ((f32[32,256,128]{2,1,0:T(8,128)}), f32[32,256,128]{2,1,0:T(8,128)}, u32[]{:S(2)}, u32[]{:S(2)}) async-start(f32[32,256,128]{2,1,0:T(8,128)} %bitcast.20), calls=%async_computation.2 | async-start | bytes 8388608 | tf_op jit(solution)/shard_map/all_to_all | solution.py:417
  64.0 2.2 copy-start.5
  69.9 2.0 copy-start.6
  117.5 5.0 %copy-start.18 = (bf16[4,256,256]{2,1,0:T(8,128)(2,1)S(1)}, bf16[4,256,256]{2,1,0:T(8,128)(2,1)}, u32[]{:S(2)}) copy-start(bf16[4,256,256]{2,1,0:T(8,128)(2,1)} %constant.88.clone.left) | copy-start | bytes 1572868
  117.5 5.0 %copy-start.24 = (bf16[4,256,256]{2,1,0:T(8,128)(2,1)S(1)}, bf16[4,256,256]{2,1,0:T(8,128)(2,1)}, u32[]{:S(2)}) copy-start(bf16[4,256,256]{2,1,0:T(8,128)(2,1)} %constant.89.clone.right) | copy-start | bytes 1572868
  117.5 58.5 %all-to-all-start.1 = ((f32[32,256,128]{2,1,0:T(8,128)}), f32[32,256,128]{2,1,0:T(8,128)}, u32[]{:S(2)}, u32[]{:S(2)}) async-start(f32[32,256,128]{2,1,0:T(8,128)} %bitcast.18), calls=%async_computation.1 | async-start | bytes 8388608 | tf_op jit(solution)/shard_map/all_to_all | solution.py:417
  131.9 2.7 copy-start.11
  134.6 1.3 copy-start.13
  176.0 2.8 copy-start.12
  178.8 1.6 copy-start.14
  189.6 77.3 %copy-start.15 = (f32[32,2,2,2,16,128]{5,4,3,2,1,0:T(8,128)}, f32[32,2,2,2,16,128]{5,4,3,2,1,0:T(8,128)S(1)}, u32[]{:S(2)}) copy-start(f32[32,2,2,2,16,128]{5,4,3,2,1,0:T(8,128)S(1)} %get-tuple-element.22) | copy-start | bytes 6291460
  266.9 35.0 %all-to-all-start.3 = ((f32[32,2,2,2,16,128]{5,4,3,2,1,0:T(8,128)}), f32[32,2,2,2,16,128]{5,4,3,2,1,0:T(8,128)}, u32[]{:S(2)}, u32[]{:S(2)}) async-start(f32[32,2,2,2,16,128]{5,4,3,2,1,0:T(8,128)} %copy-done.15), calls=%async_computation.3 | async-start | bytes 4194304 | tf_op jit(solution)/shard_map/all_to_all | solution.py:417
  271.9 83.2 %reduce-scatter.4.cloned.1.call-start = ((), (), s32[]{:S(2)}) async-start(), calls=%async_computation.6 | async-start | bytes 270336
  273.8 94.1 %all-reduce.3.cloned.1.call-start = ((), (), s32[]{:S(2)}) async-start(), calls=%async_computation.7 | async-start | bytes 4194304 | tf_op jit(solution)/shard_map/psum | solution.py:451
  273.9 2.8 copy-start.10
  283.8 1.2 copy-start.16
Sparse Core Ops, SparseCore 0:
  276.6 78.5 reduce-scatter.3
Sparse Core Ops, SparseCore 1:
  306.2 55.9 all-reduce.2

commit v2 on v1

--- a/solution.py
+++ b/solution.py
@@ -16,12 +16,15 @@
 TIME_STEP = 4.0
 HIGHEST = lax.Precision.HIGHEST
 ORBS = 2
+BANDS = 4
 PLANES = 8
 GROUPS = 32
 ENTRIES = 512
 ATOMS = 512
-FIRST = 6
-MIB = 1 << 20
+OWNED = ATOMS // GROUPS
+CHUNKS = (5, 3)
+VMEM = 56 << 20
+SENT = 24
 
 
 def propagator_tables():
@@ -30,14 +33,14 @@
     wave = freq * (2.0 * math.pi / SIZE)
     line = np.fft.ifft(np.exp(-0.5j * TIME_STEP * wave * wave))
     full = line[(index[:, None] - index[None, :]) % SIZE]
-    parts = []
+    left = []
     for sign in (1.0, -1.0):
         half = 0.5 * (full[:HALF, :HALF] + sign * full[:HALF, HALF:])
         real = np.block([[half.real, -half.imag], [half.imag, half.real]]).astype(np.float32)
         high = real.astype(ml_dtypes.bfloat16)
         low = (real - high.astype(np.float32)).astype(ml_dtypes.bfloat16)
-        parts += [high, low]
-    left = np.stack(parts)
+        left.append(np.concatenate([high, high, low], axis=1))
+    left = np.stack(left)
     return left, np.ascontiguousarray(np.swapaxes(left, 1, 2))
 
 
@@ -60,10 +63,10 @@
     return cos_out, sin_out
 
 
-def two_parts(values):
+def split(values, axis):
     high = values.astype(jnp.bfloat16)
     low = (values - high.astype(jnp.float32)).astype(jnp.bfloat16)
-    return high, low
+    return jnp.concatenate([high, low, high], axis=axis)
 
 
 def three_parts(values):
@@ -78,21 +81,11 @@
     return jnp.dot(left, right, preferred_element_type=jnp.float32)
 
 
-def left_product(table, at, values):
-    high, low = two_parts(values)
-    return dot(table[at], high) + dot(table[at], low) + dot(table[at + 1], high)
-
-
-def right_product(table, at, values):
-    high, low = two_parts(values)
-    return dot(high, table[at]) + dot(low, table[at]) + dot(high, table[at + 1])
-
-
 def propagate_rows(table, real, imag):
     plus = jnp.concatenate([real[:HALF] + real[HALF:], imag[:HALF] + imag[HALF:]], axis=0)
     minus = jnp.concatenate([real[:HALF] - real[HALF:], imag[:HALF] - imag[HALF:]], axis=0)
-    plus = left_product(table, 0, plus)
-    minus = left_product(table, 2, minus)
+    plus = dot(table[0], split(plus, 0))
+    minus = dot(table[1], split(minus, 0))
     low, high = plus + minus, plus - minus
     return (
         jnp.concatenate([low[:HALF], high[:HALF]], axis=0),
@@ -103,8 +96,8 @@
 def propagate_lanes(table, real, imag):
     plus = jnp.concatenate([real[0] + real[1], imag[0] + imag[1]], axis=1)
     minus = jnp.concatenate([real[0] - real[1], imag[0] - imag[1]], axis=1)
-    plus = right_product(table, 0, plus)
-    minus = right_product(table, 2, minus)
+    plus = dot(split(plus, 1), table[0])
+    minus = dot(split(minus, 1), table[1])
     low, high = plus + minus, plus - minus
     return (
         jnp.concatenate([low[:, :HALF], high[:, :HALF]], axis=1),
@@ -118,7 +111,7 @@
 
 
 def project_kernel(
-    block, count, atom_ref, orbs_hbm, potential_hbm, projectors, sent, partial_ref, masked_ref,
+    block, count, atom_ref, slot_ref, orbs_hbm, potential_hbm, projectors, sent, masked_ref,
     orbs, potential, rows, counts, table, packed, sems,
 ):
     half_rows = PLANES * SIZE
@@ -190,28 +183,36 @@
         three_parts(turned), atom_matrix(atom_ref), (((1,), (1,)), ((), ())), preferred_element_type=jnp.float32
     )
     sums = sums[:16] + sums[16:32] + sums[32:]
-    partial_ref[...] = sums
     for k in range(4):
         for q in range(4):
             packed[k * 4 + q : k * 4 + q + 1, :] = sums[k : k + 1, q * LANES : (q + 1) * LANES]
+    slots = lax.dot_general(
+        three_parts(sums), atom_matrix(slot_ref), (((1,), (1,)), ((), ())), preferred_element_type=jnp.float32
+    )
+    slots = slots[:16] + slots[16:32] + slots[32:]
+    lane = lax.broadcasted_iota(jnp.int32, (8, LANES), 1)
     for d in range(GROUPS):
-        sent[d] = packed[...]
-
-
-def project(orbs, potential, projectors, entry_atom, entry_block, entry_count):
+        tile = slots[:, d // 8 * LANES : (d // 8 + 1) * LANES]
+        begin = d % 8 * OWNED
+        upper = pltpu.roll(tile[:8], (LANES - begin) % LANES, 1)
+        lower = pltpu.roll(tile[8:], (LANES - begin + OWNED) % LANES, 1)
+        sent[d, 0:16, :] = packed[...]
+        sent[d, 16:24, :] = jnp.where(lane < OWNED, upper, lower)
+
+
+def project(orbs, potential, projectors, entry_atom, entry_block, entry_count, owner_slot):
     smem = pl.BlockSpec(memory_space=pltpu.SMEM)
     vmem = pl.BlockSpec(memory_space=pltpu.VMEM)
-    hbm = pl.BlockSpec(memory_space=pl.ANY)
+    hbm = pl.BlockSpec(memory_space=pltpu.HBM)
     rows = PLANES * SIZE
     return pl.pallas_call(
         project_kernel,
         out_shape=(
-            jax.ShapeDtypeStruct((GROUPS, 16, LANES), jnp.float32),
-            jax.ShapeDtypeStruct((16, ATOMS), jnp.float32),
+            jax.ShapeDtypeStruct((GROUPS, SENT, LANES), jnp.float32),
             jax.ShapeDtypeStruct((ENTRIES, LANES), jnp.float32),
         ),
-        in_specs=[smem, smem, vmem, hbm, hbm, vmem],
-        out_specs=(vmem, vmem, vmem),
+        in_specs=[smem, smem, vmem, vmem, hbm, hbm, vmem],
+        out_specs=(vmem, vmem),
         scratch_shapes=[
             pltpu.VMEM((4, 2 * rows, LANES), jnp.float32),
             pltpu.VMEM((2 * rows, LANES), jnp.float32),
@@ -221,51 +222,52 @@
             pltpu.VMEM((16, LANES), jnp.float32),
             pltpu.SemaphoreType.DMA((5, 2)),
         ],
-        compiler_params=pltpu.CompilerParams(vmem_limit_bytes=32 * MIB),
+        compiler_params=pltpu.CompilerParams(vmem_limit_bytes=VMEM),
         cost_estimate=pl.CostEstimate(flops=10**9, bytes_accessed=36 * 10**6, transcendentals=0),
         name="project",
-    )(entry_block, entry_count, entry_atom.reshape(1, ENTRIES), orbs, potential, projectors)
+    )(
+        entry_block, entry_count, entry_atom.reshape(1, ENTRIES), owner_slot.reshape(1, ATOMS), orbs, potential, projectors
+    )
 
 
 SHIFT_STEP = 4
 
 
-def shift_kernel(orbs, potential, first, second):
+def shift_kernel(orbs, potential, *rest):
+    out = rest[-1]
     for x in range(PLANES):
         cosine, sine = cos_sin((0.5 * TIME_STEP) * potential[x])
-        for n, out in enumerate((first, second)):
-            real, imag = orbs[0, n, x], orbs[1, n, x]
-            both = (cosine * real + sine * imag, cosine * imag - sine * real)
-            for c in range(2):
-                for d in range(SHIFT_STEP):
-                    for z in range(2):
-                        tile = both[c][d * 8 : d * 8 + 8, z * LANES : (z + 1) * LANES]
-                        out[d, pl.ds(c * 128 + z * 64 + x, 8, stride=8), :] = tile
-
-
-def shift(orbitals, potential):
+        real, imag = orbs[0, 0, x], orbs[1, 0, x]
+        both = (cosine * real + sine * imag, cosine * imag - sine * real)
+        for c in range(2):
+            for d in range(SHIFT_STEP):
+                for z in range(2):
+                    tile = both[c][d * 8 : d * 8 + 8, z * LANES : (z + 1) * LANES]
+                    out[d, pl.ds(c * 128 + z * 64 + x, 8, stride=8), :] = tile
+
+
+def shift(n, orbitals, potential, *first):
     width = SHIFT_STEP * 8
-    shape = jax.ShapeDtypeStruct((GROUPS, 256, LANES), jnp.float32)
-    spec = pl.BlockSpec((SHIFT_STEP, 256, LANES), lambda i: (i, 0, 0))
     return pl.pallas_call(
         shift_kernel,
         grid=(GROUPS // SHIFT_STEP,),
-        out_shape=(shape, shape),
+        out_shape=jax.ShapeDtypeStruct((GROUPS, 256, LANES), jnp.float32),
         in_specs=[
-            pl.BlockSpec((2, ORBS, PLANES, width, SIZE), lambda i: (0, 0, 0, i, 0)),
+            pl.BlockSpec((2, 1, PLANES, width, SIZE), lambda i: (0, n, 0, i, 0)),
             pl.BlockSpec((PLANES, width, SIZE), lambda i: (0, i, 0)),
-        ],
-        out_specs=(spec, spec),
-        compiler_params=pltpu.CompilerParams(vmem_limit_bytes=32 * MIB),
-        cost_estimate=pl.CostEstimate(flops=10**8, bytes_accessed=19 * 10**6, transcendentals=0),
-        name="shift",
-    )(orbitals, potential)
+            *[pl.BlockSpec(memory_space=pl.ANY) for _ in first],
+        ],
+        out_specs=pl.BlockSpec((SHIFT_STEP, 256, LANES), lambda i: (i, 0, 0)),
+        compiler_params=pltpu.CompilerParams(vmem_limit_bytes=VMEM),
+        cost_estimate=pl.CostEstimate(flops=10**8, bytes_accessed=11 * 10**6, transcendentals=0),
+        name=f"shift{n}",
+    )(orbitals, potential, *first)
 
 
 def correct_kernel(n, place, received, strength, atom_ref, masked, before, after, field, coefs, updates, sems):
     load = pltpu.make_async_copy(before, field, sems.at[0])
     load.start()
-    sums = jnp.sum(received[...], axis=0)
+    sums = jnp.sum(received[:, 0:16, :], axis=0)
     real = sums[n * 4 : n * 4 + 4]
     imag = sums[(ORBS + n) * 4 : (ORBS + n) * 4 + 4]
     cosine, sine = cos_sin(TIME_STEP * strength[...])
@@ -297,7 +299,7 @@
 def correct(n, place, received, strength, atoms, masked, before):
     smem = pl.BlockSpec(memory_space=pltpu.SMEM)
     vmem = pl.BlockSpec(memory_space=pltpu.VMEM)
-    hbm = pl.BlockSpec(memory_space=pl.ANY)
+    hbm = pl.BlockSpec(memory_space=pltpu.HBM)
     return pl.pallas_call(
         functools.partial(correct_kernel, n),
         out_shape=jax.ShapeDtypeStruct((GROUPS * 256, LANES), jnp.float32),
@@ -310,14 +312,14 @@
             pltpu.SemaphoreType.DMA((2,)),
         ],
         input_output_aliases={5: 0},
-        compiler_params=pltpu.CompilerParams(vmem_limit_bytes=24 * MIB),
+        compiler_params=pltpu.CompilerParams(vmem_limit_bytes=VMEM),
         cost_estimate=pl.CostEstimate(flops=5 * 10**8, bytes_accessed=20 * 10**6, transcendentals=0),
         name=f"correct{n}",
     )(place, received, strength, atoms, masked, before.reshape(GROUPS * 256, LANES))
 
 
 def lines_kernel(n, field, left, right, *rest):
-    head, tail, turned, sems = rest[-4:]
+    *chunks, turned, sems = rest[-2 - len(CHUNKS) :]
     y = pl.program_id(0)
     real = [field[:, 0, z, 0].reshape(SIZE, LANES) for z in range(2)]
     imag = [field[:, 1, z, 0].reshape(SIZE, LANES) for z in range(2)]
@@ -331,47 +333,45 @@
 
     @pl.when(y == pl.num_programs(0) - 1)
     def _():
-        cut = FIRST * 8
-        copies = [
-            pltpu.make_async_copy(turned.at[:, :, :, pl.ds(0, cut)], head.at[:, :, n], sems.at[0]),
-            pltpu.make_async_copy(turned.at[:, :, :, pl.ds(cut, 64 - cut)], tail.at[:, :, n], sems.at[1]),
-        ]
+        copies, begin = [], 0
+        for k, (chunk, planes) in enumerate(zip(chunks, CHUNKS)):
+            part = turned.at[:, :, :, pl.ds(begin * 8, planes * 8)]
+            copies.append(pltpu.make_async_copy(part, chunk.at[:, :, n], sems.at[k]))
+            begin += planes
         for copy in copies:
             copy.start()
         for copy in copies:
             copy.wait()
 
 
-def lines(n, field, left, right, *before):
-    hbm = pl.BlockSpec(memory_space=pl.ANY)
-    table = pl.BlockSpec((4, SIZE, SIZE), lambda i: (0, 0, 0))
+def lines(n, field, left, right, before=(), first=()):
+    hbm = pl.BlockSpec(memory_space=pltpu.HBM)
     return pl.pallas_call(
         functools.partial(lines_kernel, n),
         grid=(8,),
-        out_shape=(
-            jax.ShapeDtypeStruct((GROUPS, 2, ORBS, 2, FIRST * 8, LANES), jnp.float32),
-            jax.ShapeDtypeStruct((GROUPS, 2, ORBS, 2, (PLANES - FIRST) * 8, LANES), jnp.float32),
+        out_shape=tuple(
+            jax.ShapeDtypeStruct((GROUPS, 2, ORBS, 2, planes * 8, LANES), jnp.float32) for planes in CHUNKS
         ),
         in_specs=[
             pl.BlockSpec((GROUPS, 2, 2, 1, 8, LANES), lambda i: (0, 0, 0, i, 0, 0)),
-            table,
-            table,
-            *[hbm for _ in before],
-        ],
-        out_specs=(hbm, hbm),
+            pl.BlockSpec(left.shape, lambda i: (0, 0, 0)),
+            pl.BlockSpec(right.shape, lambda i: (0, 0, 0)),
+            *[hbm for _ in (*before, *first)],
+        ],
+        out_specs=tuple(hbm for _ in CHUNKS),
         scratch_shapes=[
             pltpu.VMEM((GROUPS, 2, 2, 64, LANES), jnp.float32),
-            pltpu.SemaphoreType.DMA((2,)),
+            pltpu.SemaphoreType.DMA((len(CHUNKS),)),
         ],
         input_output_aliases={3 + k: k for k in range(len(before))},
-        compiler_params=pltpu.CompilerParams(vmem_limit_bytes=32 * MIB),
+        compiler_params=pltpu.CompilerParams(vmem_limit_bytes=VMEM),
         cost_estimate=pl.CostEstimate(flops=5 * 10**9, bytes_accessed=10 * 10**6, transcendentals=0),
         name=f"lines{n}",
-    )(field.reshape(GROUPS, 2, 2, 8, 8, LANES), left, right, *before)
-
-
-def finish_kernel(field, potential, left, *rest):
-    out, density = rest[-2:]
+    )(field.reshape(GROUPS, 2, 2, 8, 8, LANES), left, right, *before, *first)
+
+
+def finish_kernel(band, field, potential, left, *rest):
+    out, *pieces, whole = rest[-6:]
     cosine, sine = cos_sin((0.5 * TIME_STEP) * potential[0])
     total = None
     for n in range(ORBS):
@@ -384,33 +384,92 @@
         out[1, n, 0] = imag
         square = real * real + imag * imag
         total = square if total is None else total + square
-    density[0] = total
-
-
-def finish(planes, begin, field, potential, left, *before):
-    hbm = pl.BlockSpec(memory_space=pl.ANY)
+    whole[...] = total
+    rows = SIZE // BANDS
+    for k, piece in enumerate(pieces):
+        begin = pl.multiple_of((band[0] + k) % BANDS * rows, rows)
+        piece[0] = whole[pl.ds(begin, rows), :]
+
+
+def finish(planes, begin, band, field, potential, left, before=(), first=()):
+    rows = SIZE // BANDS
     return pl.pallas_call(
         finish_kernel,
         grid=(planes,),
         out_shape=(
             jax.ShapeDtypeStruct((2, ORBS, PLANES, SIZE, SIZE), jnp.float32),
-            jax.ShapeDtypeStruct((planes, SIZE, SIZE), jnp.float32),
+            *[jax.ShapeDtypeStruct((planes, rows, SIZE), jnp.float32) for _ in range(BANDS)],
         ),
         in_specs=[
+            pl.BlockSpec(memory_space=pltpu.SMEM),
             pl.BlockSpec((GROUPS, 2, ORBS, 2, 8, LANES), lambda i: (0, 0, 0, 0, i, 0)),
             pl.BlockSpec((1, SIZE, SIZE), lambda i: (i + begin, 0, 0)),
-            pl.BlockSpec((4, SIZE, SIZE), lambda i: (0, 0, 0)),
-            *[hbm for _ in before],
+            pl.BlockSpec(left.shape, lambda i: (0, 0, 0)),
+            *[pl.BlockSpec(memory_space=pl.ANY) for _ in (*before, *first)],
         ],
         out_specs=(
             pl.BlockSpec((2, ORBS, 1, SIZE, SIZE), lambda i: (0, 0, i + begin, 0, 0)),
-            pl.BlockSpec((1, SIZE, SIZE), lambda i: (i, 0, 0)),
+            *[pl.BlockSpec((1, rows, SIZE), lambda i: (i, 0, 0)) for _ in range(BANDS)],
         ),
-        input_output_aliases={3 + k: k for k in range(len(before))},
-        compiler_params=pltpu.CompilerParams(vmem_limit_bytes=32 * MIB),
+        scratch_shapes=[pltpu.VMEM((SIZE, SIZE), jnp.float32)],
+        input_output_aliases={4 + k: k for k in range(len(before))},
+        compiler_params=pltpu.CompilerParams(vmem_limit_bytes=VMEM),
         cost_estimate=pl.CostEstimate(flops=10**9 * planes, bytes_accessed=3 * 10**6 * planes, transcendentals=0),
         name=f"finish{begin}",
-    )(field, potential, left, *before)
+    )(band, field, potential, left, *before, *first)
+
+
+def collect_kernel(owners, band, *refs):
+    out = refs[-1]
+    rows = SIZE // BANDS
+    for piece, (owner, offset) in zip(refs, owners):
+        row = pl.multiple_of((band[0] + owner) % BANDS * rows, rows)
+        out[0, pl.ds(pl.multiple_of(row + offset, rows // 2), piece.shape[1]), :] = piece[0]
+
+
+def collect(begin, band, pieces, owners, *before):
+    return pl.pallas_call(
+        functools.partial(collect_kernel, owners),
+        grid=(pieces[0].shape[0],),
+        out_shape=jax.ShapeDtypeStruct((PLANES, SIZE, SIZE), jnp.float32),
+        in_specs=[
+            pl.BlockSpec(memory_space=pltpu.SMEM),
+            *[pl.BlockSpec((1, piece.shape[1], SIZE), lambda i: (i, 0, 0)) for piece in pieces],
+            *[pl.BlockSpec(memory_space=pl.ANY) for _ in before],
+        ],
+        out_specs=pl.BlockSpec((1, SIZE, SIZE), lambda i: (i + begin, 0, 0)),
+        input_output_aliases={1 + len(pieces) + k: k for k in range(len(before))},
+        compiler_params=pltpu.CompilerParams(vmem_limit_bytes=16 << 20),
+        cost_estimate=pl.CostEstimate(flops=0, bytes_accessed=3 * 10**6, transcendentals=0),
+        name=f"collect{begin}",
+    )(band, *pieces, *before)
+
+
+def onward(array, steps):
+    return lax.ppermute(array, "band", [(b, (b + steps) % BANDS) for b in range(BANDS)])
+
+
+def ring_reduce(pieces):
+    own, right, across, left = pieces
+    low, high = (slice(None), slice(0, SIZE // BANDS // 2)), (slice(None), slice(SIZE // BANDS // 2, None))
+    right = right.at[low].add(onward(across[low], 1))
+    left = left.at[high].add(onward(across[high], 3))
+    return own + onward(right, 1) + onward(left, 3)
+
+
+def ring_gather(total):
+    before, after = onward(total, 1), onward(total, 3)
+    half = SIZE // BANDS // 2
+    pieces = total, before, after, onward(before[:, :half], 1), onward(after[:, half:], 3)
+    return pieces, ((0, 0), (3, 0), (1, 0), (2, 0), (2, half))
+
+
+def direct_reduce(pieces):
+    return pieces[0] + onward(pieces[1], 1) + onward(pieces[2], 2) + onward(pieces[3], 3)
+
+
+def direct_gather(total):
+    return (total, *[onward(total, k) for k in range(1, BANDS)]), ((0, 0), (3, 0), (2, 0), (1, 0))
 
 
 def exchange(array):
@@ -420,36 +479,45 @@
 def body(left, right, orbitals, potential, projectors, entry_atom, entry_block, entry_count, owner_slot, strength):
     atom_ids = jnp.arange(ATOMS, dtype=jnp.int32)
     rows = PLANES * SIZE
-    sent, partials, masked = project(
+    band = lax.axis_index("band").astype(jnp.int32).reshape(1)
+    sent, masked = project(
         orbitals.reshape(2 * ORBS, rows, SIZE), potential.reshape(rows, SIZE), projectors,
-        entry_atom, entry_block, entry_count,
+        entry_atom, entry_block, entry_count, owner_slot,
     )
     received = exchange(sent)
-    shifted = shift(orbitals, potential)
     x, y, z = entry_block // 512, (entry_block // 2) % SIZE, entry_block % 2
     place = (y // 8) * 256 + z * 64 + (y % 8) * 8 + x
     in_slot = owner_slot[:, None] == atom_ids[None, :]
     strength_atom = jnp.sum(jnp.where(in_slot, strength[None, :], 0.0), axis=1).reshape(4, LANES)
     atoms = entry_atom.reshape(1, ENTRIES)
-    pencils = [
-        exchange(correct(n, place, received, strength_atom, atoms, masked, shifted[n]).reshape(GROUPS, 256, LANES))
-        for n in range(ORBS)
-    ]
-    in_slots = jnp.einsum("ka,as->ks", partials, in_slot.astype(jnp.float32), precision=HIGHEST)
-    owned = ATOMS // GROUPS
-    mine = lax.psum_scatter(in_slots, "grid", scatter_dimension=1, tiled=True).reshape(4, 2 * ORBS, owned)
-    strength_mine = lax.dynamic_slice_in_dim(strength, lax.axis_index("grid") * owned, owned)
-    force_local = -2.0 * strength_mine * jnp.sum(mine[0][None] * mine[1:], axis=1)
-    forces = lax.psum(force_local, "band")
+    pencils, sent = [], ()
+    for n in range(ORBS):
+        shifted = shift(n, orbitals, potential, *sent)
+        fixed = correct(n, place, received, strength_atom, atoms, masked, shifted)
+        pencils.append(exchange(fixed.reshape(GROUPS, 256, LANES)))
+        sent = (fixed,)
+    mine = jnp.sum(received[:, 16:], axis=0)
+    mine = jnp.concatenate([mine[:, :OWNED], mine[:, OWNED : 2 * OWNED]], axis=0).reshape(4, 2 * ORBS, OWNED)
+    strength_mine = lax.dynamic_slice_in_dim(strength, lax.axis_index("grid") * OWNED, OWNED)
+    forces = -2.0 * strength_mine * jnp.sum(mine[0][None] * mine[1:], axis=1)
+    forces = sum([onward(forces, k) for k in range(1, BANDS)], forces)
 
     back = lines(0, pencils[0], left, right)
-    back = lines(1, pencils[1], left, right, *back)
-    head = exchange(back[0])
-    tail = exchange(back[1])
-    out, density_head = finish(FIRST, 0, head, potential, left)
-    out, density_tail = finish(PLANES - FIRST, FIRST, tail, potential, left, out)
-    density = jnp.concatenate([lax.psum(density_head, "band"), lax.psum(density_tail, "band")], axis=0)
-    return out, density, forces
+    back = lines(1, pencils[1], left, right, back, (forces,))
+    out, density, ready, begin = (), (), (), 0
+    for k, planes in enumerate(CHUNKS):
+        field = exchange(back[k])
+        made, *pieces = finish(planes, begin, band, field, potential, left, out, ready)
+        out = (made,)
+        if k == 0:
+            density = (collect(begin, band, *ring_gather(ring_reduce(pieces))),)
+            ready = density
+        else:
+            total = direct_reduce(pieces)
+            ready = (total,)
+            density = (collect(begin, band, *direct_gather(total), *density),)
+        begin += planes
+    return out[0], density[0], forces
 
 
 def solution(mesh):

time: 380 us -> 330 us (0.87)
  waiting for transfers between devices: 152 us -> 116 us
  local copies, waits for them, and re-layouts: 38 us -> 3.53 us
  Pallas kernels: 53.7 us -> 85.3 us
  blocking collectives: 88.3 us -> 67.1 us
  starting transfers between devices: 25.9 us -> 47 us
  between operations: 15.7 us -> 0.8 us
  other arithmetic: 3.42 us -> 8.38 us
    unnamed x3 -> x0, waiting for transfers between devices: 49 us -> none
    ppermute x0 -> x17, waiting for transfers between devices: none -> 46.2 us  [onward(): lax.ppermute(array, 'band', [(b, (b + steps) % BANDS) for b in range(BAND...]
    unnamed x56 -> x10, local copies, waits for them, and re-layouts: 37.2 us -> 2.4 us
    all_to_all x4, waiting for transfers between devices: 103 us -> 69.8 us  [exchange(): lax.all_to_all(array, 'grid', split_axis=0, concat_axis=0, tiled=True)]
    ppermute x0 -> x17, starting transfers between devices: none -> 22.2 us  [onward(): lax.ppermute(array, 'band', [(b, (b + steps) % BANDS) for b in range(BAND...]
    pallas_call x4 -> x7, Pallas kernels: 35 us -> 55.5 us  [the longest x2 22.3 us: lines(): pl.pallas_call(functools.partial(lines_kernel, n), grid=(8,), out_shape=t...]
    psum x1 -> x0, blocking collectives: 11 us -> none  [body(): forces = lax.psum(force_local, 'band')]
    all_to_all x1, blocking collectives: 77.3 us -> 67.1 us  [exchange(): lax.all_to_all(array, 'grid', split_axis=0, concat_axis=0, tiled=True)]
  transfers between devices with their start and end apart: 6 -> 21, of which waited for: 4 -> 16; matrix products, arithmetic and copies ran while one was open for 1% -> 3% of each run, Pallas kernels for 8% -> 14%
where the time goes in v2:
time: 330 us; the launch traced here: 328 us
  waiting for transfers between devices  116 us (35%)
  Pallas kernels  85.3 us (26%)
  blocking collectives  67.1 us (20%)
  starting transfers between devices  47 us (14%)
  other arithmetic  8.38 us (3%)
  local copies, waits for them, and re-layouts  3.53 us (1%)
    all_to_all x4, waiting for transfers between devices, exchange(): lax.all_to_all(array, 'grid', split_axis=0, concat_axis=0, tiled=True)  69.8 us
    all_to_all x1, blocking collectives, exchange(): lax.all_to_all(array, 'grid', split_axis=0, concat_axis=0, tiled=True)  67.1 us
    ppermute x17, waiting for transfers between devices, onward(): lax.ppermute(array, 'band', [(b, (b + steps) % BANDS) for b in range(BAND...  46.2 us
    all_to_all x4, starting transfers between devices, exchange(): lax.all_to_all(array, 'grid', split_axis=0, concat_axis=0, tiled=True)  24.8 us
    pallas_call x2, Pallas kernels, lines(): pl.pallas_call(functools.partial(lines_kernel, n), grid=(8,), out_shape=t...  22.3 us
    ppermute x17, starting transfers between devices, onward(): lax.ppermute(array, 'band', [(b, (b + steps) % BANDS) for b in range(BAND...  22.2 us
    pallas_call x2, Pallas kernels, shift(): pl.pallas_call(shift_kernel, grid=(GROUPS // SHIFT_STEP,), out_shape=jax....  16.8 us
    pallas_call x2, Pallas kernels, finish(): pl.pallas_call(finish_kernel, grid=(planes,), out_shape=(jax.ShapeDtypeSt...  15.5 us
  transfers between devices with their start and end apart: 21, of which 16 were waited for; matrix products, arithmetic and copies ran while one was open for 3% of the time, Pallas kernels for 14%

profile of v2, /device:TPU:0, one launch (start us, length us, event | category | flops | bytes accessed | tf_op | source)
XLA Modules:
  0.0 328.1 jit_solution(2208150910379691478)
XLA Ops:
  0.6 12.8 %project.1 = (f32[32,24,128]{2,1,0:T(8,128)}, f32[512,128]{1,0:T(8,128)}) custom-call(s32[512]{0:T(512)} %block.1, s32[512]{0:T(512)} %count.1, s32[1,512]{1,0:T(1,128)} %bitcast.18, s32[1,512]{1,0:T(1,128)} %bitcast.23, f32[4,2048,256]{2,1,0:T(8,128)} %bitcast.12, f32[2048,256]{1,0:T(8,128)} %bitcast.17, f32[4,512,128]{2,1,0:T(8,128)} %projectors.1), custom_call_target="tpu_custom_call" | custom-call | flops 1000000000 | bytes 36000000 | tf_op jit(solution)/shard_map/project/pallas_call | solution.py:208
  13.4 8.3 %all-to-all-start = ((f32[32,24,128]{2,1,0:T(8,128)}), f32[32,24,128]{2,1,0:T(8,128)S(1)}, u32[]{:S(2)}, u32[]{:S(2)}) async-start(f32[32,24,128]{2,1,0:T(8,128)} %get-tuple-element.43), calls=%async_computation | async-start | bytes 786432 | tf_op jit(solution)/shard_map/all_to_all | solution.py:476
  21.7 8.3 %shift0.1 = f32[32,256,128]{2,1,0:T(8,128)} custom-call(f32[2,2,8,256,256]{4,3,2,1,0:T(8,128)} %orbs.3, f32[8,256,256]{2,1,0:T(8,128)} %potential.7), custom_call_target="tpu_custom_call" | custom-call | flops 100000000 | bytes 11000000 | tf_op jit(solution)/shard_map/shift0/pallas_call | solution.py:251
  32.7 7.2 %correct0.1.rest_0_ = f32[8192,128]{1,0:T(8,128)} custom-call(s32[512]{0:T(512)} %fusion.4.place, f32[32,24,128]{2,1,0:T(8,128)} %copy-done.1, f32[4,128]{1,0:T(4,128)} %bitcast.21, s32[1,512]{1,0:T(1,128)} %bitcast.19, f32[512,128]{1,0:T(8,128)} %get-tuple-element.44.masked, f32[8192,128]{1,0:T(8,128)} %bitcast.13), custom_call_target="tpu_custom_call", output_to_operand_aliasing={{}: (5, {})} | custom-call | flops 500000000 | bytes 20000000 | tf_op jit(solution)/shard_map/correct0/pallas_call | solution.py:303
  39.9 7.1 %all-to-all-start.2 = ((f32[32,256,128]{2,1,0:T(8,128)}), f32[32,256,128]{2,1,0:T(8,128)}, u32[]{:S(2)}, u32[]{:S(2)}) async-start(f32[32,256,128]{2,1,0:T(8,128)} %bitcast.14), calls=%async_computation.2 | async-start | bytes 8388608 | tf_op jit(solution)/shard_map/all_to_all | solution.py:476
  46.9 8.4 %shift1.1 = f32[32,256,128]{2,1,0:T(8,128)} custom-call(f32[2,2,8,256,256]{4,3,2,1,0:T(8,128)} %orbs.3, f32[8,256,256]{2,1,0:T(8,128)} %potential.7, f32[8192,128]{1,0:T(8,128)} %correct0.1.rest_0_), custom_call_target="tpu_custom_call" | custom-call | flops 100000000 | bytes 11000000 | tf_op jit(solution)/shard_map/shift1/pallas_call | solution.py:251
  55.4 7.1 %correct1.1 = f32[8192,128]{1,0:T(8,128)} custom-call(s32[512]{0:T(512)} %fusion.4.place, f32[32,24,128]{2,1,0:T(8,128)} %copy-done.1, f32[4,128]{1,0:T(4,128)} %bitcast.22, s32[1,512]{1,0:T(1,128)} %bitcast.20, f32[512,128]{1,0:T(8,128)} %get-tuple-element.44.masked, f32[8192,128]{1,0:T(8,128)} %bitcast.15), custom_call_target="tpu_custom_call", output_to_operand_aliasing={{}: (5, {})} | custom-call | flops 500000000 | bytes 20000000 | tf_op jit(solution)/shard_map/correct1/pallas_call | solution.py:303
  62.5 37.9 %all-to-all-done.2 = f32[32,256,128]{2,1,0:T(8,128)} async-done(((f32[32,256,128]{2,1,0:T(8,128)}), f32[32,256,128]{2,1,0:T(8,128)}, u32[]{:S(2)}, u32[]{:S(2)}) %all-to-all-start.2) | async-done | bytes 4194336 | tf_op jit(solution)/shard_map/all_to_all | solution.py:476
  100.4 4.9 %all-to-all-start.1 = ((f32[32,256,128]{2,1,0:T(8,128)}), f32[32,256,128]{2,1,0:T(8,128)}, u32[]{:S(2)}, u32[]{:S(2)}) async-start(f32[32,256,128]{2,1,0:T(8,128)} %bitcast.16), calls=%async_computation.1 | async-start | bytes 8388608 | tf_op jit(solution)/shard_map/all_to_all | solution.py:476
  105.4 0.9 slice_reduce_fusion
  106.4 3.3 collective-permute-start.1
  109.7 1.1 collective-permute-start.2
  110.8 1.0 collective-permute-start
  111.8 1.6 collective-permute-done.2
  113.3 2.3 collective-permute-done
  116.2 11.2 %lines0.1 = (f32[32,2,2,2,40,128]{5,4,3,2,1,0:T(8,128)}, f32[32,2,2,2,24,128]{5,4,3,2,1,0:T(8,128)}) custom-call(f32[32,2,2,8,8,128]{5,4,3,2,1,0:T(8,128)} %bitcast.11.field, bf16[2,256,768]{2,1,0:T(8,128)(2,1)} %constant.147.clone.left, bf16[2,768,256]{2,1,0:T(8,128)(2,1)} %constant.148.clone.right), custom_call_target="tpu_custom_call" | custom-call | flops 5000000000 | bytes 10000000 | tf_op jit(solution)/shard_map/lines0/pallas_call | solution.py:349
  127.3 31.4 %all-to-all-done.1 = f32[32,256,128]{2,1,0:T(8,128)} async-done(((f32[32,256,128]{2,1,0:T(8,128)}), f32[32,256,128]{2,1,0:T(8,128)}, u32[]{:S(2)}, u32[]{:S(2)}) %all-to-all-start.1) | async-done | bytes 4194336 | tf_op jit(solution)/shard_map/all_to_all | solution.py:476
  158.8 11.2 %lines1.1 = (f32[32,2,2,2,40,128]{5,4,3,2,1,0:T(8,128)}, f32[32,2,2,2,24,128]{5,4,3,2,1,0:T(8,128)}) custom-call(f32[32,2,2,8,8,128]{5,4,3,2,1,0:T(8,128)} %bitcast.9.field, bf16[2,256,768]{2,1,0:T(8,128)(2,1)} %constant.147.clone.left, bf16[2,768,256]{2,1,0:T(8,128)(2,1)} %constant.148.clone.right, ...), custom_call_target="tpu_custom_call", output_to_operand_aliasing={{0}: (3, {}), {1}: (4, {})} | custom-call | flops 5000000000 | bytes 10000000 | tf_op jit(solution)/shard_map/lines1/pallas_call | solution.py:349
  170.0 67.1 %all_to_all.25.field = f32[32,2,2,2,40,128]{5,4,3,2,1,0:T(8,128)} all-to-all(f32[32,2,2,2,40,128]{5,4,3,2,1,0:T(8,128)} %get-tuple-element.48), channel_id=1, replica_groups=mesh['band'=4,'grid'=32] {'grid'}, dimensions={0} | all-to-all | bytes 10485760 | tf_op jit(solution)/shard_map/all_to_all | solution.py:476
  237.1 4.6 %all-to-all-start.3 = ((f32[32,2,2,2,24,128]{5,4,3,2,1,0:T(8,128)}), f32[32,2,2,2,24,128]{5,4,3,2,1,0:T(8,128)S(1)}, u32[]{:S(2)}, u32[]{:S(2)}) async-start(f32[32,2,2,2,24,128]{5,4,3,2,1,0:T(8,128)} %get-tuple-element.47), calls=%async_computation.3 | async-start | bytes 6291456 | tf_op jit(solution)/shard_map/all_to_all | solution.py:476
  241.7 9.1 %finish0.1 = (f32[2,2,8,256,256]{4,3,2,1,0:T(8,128)}, f32[5,64,256]{2,1,0:T(8,128)}, f32[5,64,256]{2,1,0:T(8,128)}, f32[5,64,256]{2,1,0:T(8,128)}, f32[5,64,256]{2,1,0:T(8,128)}) custom-call(s32[1]{0:T(128)} %bitcast.band, f32[32,2,2,2,40,128]{5,4,3,2,1,0:T(8,128)} %all_to_all.25.field, f32[8,256,256]{2,1,0:T(8,128)} %potential.7, ...), custom_call_target="tpu_custom_call" | custom-call | flops 5000000000 | bytes 15000000 | tf_op jit(solution)/shard_map/finish0/pallas_call | solution.py:396
  250.8 1.0 fusion.11
  251.8 3.1 collective-permute-start.5
  254.9 3.9 %collective-permute-done.5 = f32[5,32,256]{2,1,0:T(8,128)S(1)} collective-permute-done((f32[5,32,256]{2,1,0:T(8,128)S(1)}, f32[5,32,256]{2,1,0:T(8,128)S(1)}, u32[]{:S(2)}, u32[]{:S(2)}) %collective-permute-start.5) | collective-permute-done | bytes 163872 | tf_op jit(solution)/shard_map/ppermute | solution.py:449
  258.8 1.6 add_dynamic-update-slice_fusion
  260.5 3.7 %collective-permute-start.6 = (f32[5,64,256]{2,1,0:T(8,128)}, f32[5,64,256]{2,1,0:T(8,128)S(1)}, u32[]{:S(2)}, u32[]{:S(2)}) collective-permute-start(f32[5,64,256]{2,1,0:T(8,128)} %add_dynamic-update-slice_fusion), channel_id=1, source_target_pairs={{0,96},{32,0},{64,32},{96,64},{1,97},{33,1},{65,33},{97,65},{2,98}... | collective-permute-start | bytes 983048 | tf_op jit(solution)/shard_map/ppermute | solution.py:449
  264.2 1.6 add_dynamic-update-slice_fusion.1
  265.8 5.3 %collective-permute-done.6 = f32[5,64,256]{2,1,0:T(8,128)S(1)} collective-permute-done((f32[5,64,256]{2,1,0:T(8,128)}, f32[5,64,256]{2,1,0:T(8,128)S(1)}, u32[]{:S(2)}, u32[]{:S(2)}) %collective-permute-start.6) | collective-permute-done | bytes 327712 | tf_op jit(solution)/shard_map/ppermute | solution.py:449
  271.1 4.9 %collective-permute-done.4 = f32[5,64,256]{2,1,0:T(8,128)S(1)} collective-permute-done((f32[5,64,256]{2,1,0:T(8,128)}, f32[5,64,256]{2,1,0:T(8,128)S(1)}, u32[]{:S(2)}, u32[]{:S(2)}) %collective-permute-start.4) | collective-permute-done | bytes 327712 | tf_op jit(solution)/shard_map/ppermute | solution.py:449
  276.0 1.0 add_add_fusion.refs_0_
  277.2 2.0 collective-permute-start.7
  279.2 5.8 %collective-permute-done.8.refs_2_ = f32[5,64,256]{2,1,0:T(8,128)S(1)} collective-permute-done((f32[5,64,256]{2,1,0:T(8,128)S(1)}, f32[5,64,256]{2,1,0:T(8,128)S(1)}, u32[]{:S(2)}, u32[]{:S(2)}) %collective-permute-start.8) | collective-permute-done | bytes 327712 | tf_op jit(solution)/shard_map/ppermute | solution.py:449
  285.0 1.6 collective-permute-start.10
  287.4 3.0 collective-permute-done.10.refs_4_
  290.4 3.0 collective-permute-done.9.refs_3_
  293.4 2.2 collect0.1.rest_1_.refs_4_
  295.6 1.6 copy-done
  297.2 6.3 %finish5.1 = (f32[2,2,8,256,256]{4,3,2,1,0:T(8,128)}, f32[3,64,256]{2,1,0:T(8,128)}, f32[3,64,256]{2,1,0:T(8,128)}, f32[3,64,256]{2,1,0:T(8,128)}, f32[3,64,256]{2,1,0:T(8,128)}) custom-call(s32[1]{0:T(128)} %bitcast.band, f32[32,2,2,2,24,128]{5,4,3,2,1,0:T(8,128)} %copy-done, f32[8,256,256]{2,1,0:T(8,128)} %potential.7, ...), custom_call_target="tpu_custom_call", output_to_operand_aliasing={{0}: (4, {})} | custom-call | flops 3000000000 | bytes 9000000 | tf_op jit(solution)/shard_map/finish5/pallas_call | solution.py:396
  303.6 1.2 collective-permute-start.12
  304.8 2.0 collective-permute-start.13
  306.8 6.0 %collective-permute-done.11 = f32[3,64,256]{2,1,0:T(8,128)S(1)} collective-permute-done((f32[3,64,256]{2,1,0:T(8,128)}, f32[3,64,256]{2,1,0:T(8,128)S(1)}, u32[]{:S(2)}, u32[]{:S(2)}) %collective-permute-start.11) | collective-permute-done | bytes 196640 | tf_op jit(solution)/shard_map/ppermute | solution.py:449
  312.8 2.1 collective-permute-done.13
  314.9 1.0 add_add_fusion.1.refs_0_
  315.9 1.5 collective-permute-start.16
  318.3 3.3 %collective-permute-done.16.refs_3_ = f32[3,64,256]{2,1,0:T(8,128)S(1)} collective-permute-done((f32[3,64,256]{2,1,0:T(8,128)S(1)}, f32[3,64,256]{2,1,0:T(8,128)S(1)}, u32[]{:S(2)}, u32[]{:S(2)}) %collective-permute-start.16) | collective-permute-done | bytes 196640 | tf_op jit(solution)/shard_map/ppermute | solution.py:449
  321.6 3.0 collective-permute-done.15.refs_2_
  324.7 2.0 collective-permute-done.14.refs_1_
  326.7 1.5 collect5.1
  (34 shorter events, 5.4 us)
Async XLA Ops:
  13.4 18.6 %all-to-all-start = ((f32[32,24,128]{2,1,0:T(8,128)}), f32[32,24,128]{2,1,0:T(8,128)S(1)}, u32[]{:S(2)}, u32[]{:S(2)}) async-start(f32[32,24,128]{2,1,0:T(8,128)} %get-tuple-element.43), calls=%async_computation | async-start | bytes 786432 | tf_op jit(solution)/shard_map/all_to_all | solution.py:476
  21.7 8.4 %copy-start.2 = (s32[512]{0:T(512)S(1)}, s32[512]{0:T(512)}, u32[]{:S(2)}) copy-start(s32[512]{0:T(512)} %param.20) | copy-start | bytes 6148
  21.7 8.4 %copy-start.4 = (f32[512]{0:T(512)S(1)}, f32[512]{0:T(512)}, u32[]{:S(2)}) copy-start(f32[512]{0:T(512)} %param.21) | copy-start | bytes 6148
  21.7 9.2 %copy-start.3 = (s32[512]{0:T(512)S(1)}, s32[512]{0:T(512)}, u32[]{:S(2)}) copy-start(s32[512]{0:T(512)} %block.1) | copy-start | bytes 6148
  32.0 0.7 copy-start.1
  39.9 60.5 %all-to-all-start.2 = ((f32[32,256,128]{2,1,0:T(8,128)}), f32[32,256,128]{2,1,0:T(8,128)}, u32[]{:S(2)}, u32[]{:S(2)}) async-start(f32[32,256,128]{2,1,0:T(8,128)} %bitcast.14), calls=%async_computation.2 | async-start | bytes 8388608 | tf_op jit(solution)/shard_map/all_to_all | solution.py:476
  100.4 58.3 %all-to-all-start.1 = ((f32[32,256,128]{2,1,0:T(8,128)}), f32[32,256,128]{2,1,0:T(8,128)}, u32[]{:S(2)}, u32[]{:S(2)}) async-start(f32[32,256,128]{2,1,0:T(8,128)} %bitcast.16), calls=%async_computation.1 | async-start | bytes 8388608 | tf_op jit(solution)/shard_map/all_to_all | solution.py:476
  106.4 5.3 %collective-permute-start.1 = (f32[3,16]{1,0:T(4,128)S(1)}, f32[3,16]{1,0:T(4,128)S(1)}, u32[]{:S(2)}, u32[]{:S(2)}) collective-permute-start(f32[3,16]{1,0:T(4,128)S(1)} %broadcast_multiply_fusion), channel_id=1, source_target_pairs={{0,64},{32,96},{64,0},{96,32},{1,65},{33,97},{65,1},{97,33},{2,66}... | collective-permute-start | bytes 584 | tf_op jit(solution)/shard_map/ppermute | solution.py:449
  109.7 3.6 %collective-permute-start.2 = (f32[3,16]{1,0:T(4,128)S(1)}, f32[3,16]{1,0:T(4,128)S(1)}, u32[]{:S(2)}, u32[]{:S(2)}) collective-permute-start(f32[3,16]{1,0:T(4,128)S(1)} %broadcast_multiply_fusion), channel_id=1, source_target_pairs={{0,96},{32,0},{64,32},{96,64},{1,97},{33,1},{65,33},{97,65},{2,98}... | collective-permute-start | bytes 584 | tf_op jit(solution)/shard_map/ppermute | solution.py:449
  110.8 4.8 %collective-permute-start = (f32[3,16]{1,0:T(4,128)S(1)}, f32[3,16]{1,0:T(4,128)S(1)}, u32[]{:S(2)}, u32[]{:S(2)}) collective-permute-start(f32[3,16]{1,0:T(4,128)S(1)} %broadcast_multiply_fusion), channel_id=1, source_target_pairs={{0,32},{32,64},{64,96},{96,0},{1,33},{33,65},{65,97},{97,1},{2,34}... | collective-permute-start | bytes 584 | tf_op jit(solution)/shard_map/ppermute | solution.py:449
  237.1 58.5 %all-to-all-start.3 = ((f32[32,2,2,2,24,128]{5,4,3,2,1,0:T(8,128)}), f32[32,2,2,2,24,128]{5,4,3,2,1,0:T(8,128)S(1)}, u32[]{:S(2)}, u32[]{:S(2)}) async-start(f32[32,2,2,2,24,128]{5,4,3,2,1,0:T(8,128)} %get-tuple-element.47), calls=%async_computation.3 | async-start | bytes 6291456 | tf_op jit(solution)/shard_map/all_to_all | solution.py:476
  251.8 7.0 %collective-permute-start.5 = (f32[5,32,256]{2,1,0:T(8,128)S(1)}, f32[5,32,256]{2,1,0:T(8,128)S(1)}, u32[]{:S(2)}, u32[]{:S(2)}) collective-permute-start(f32[5,32,256]{2,1,0:T(8,128)S(1)} %get-tuple-element.60), channel_id=1, source_target_pairs={{0,96},{32,0},{64,32},{96,64},{1,97},{33,1},{65,33},{97,65},{2,98}... | collective-permute-start | bytes 491528 | tf_op jit(solution)/shard_map/ppermute | solution.py:449
  254.9 9.2 %collective-permute-start.3 = (f32[5,32,256]{2,1,0:T(8,128)S(1)}, f32[5,32,256]{2,1,0:T(8,128)S(1)}, u32[]{:S(2)}, u32[]{:S(2)}) collective-permute-start(f32[5,32,256]{2,1,0:T(8,128)S(1)} %get-tuple-element.59), channel_id=1, source_target_pairs={{0,32},{32,64},{64,96},{96,0},{1,33},{33,65},{65,97},{97,1},{2,34}... | collective-permute-start | bytes 491528 | tf_op jit(solution)/shard_map/ppermute | solution.py:449
  260.5 10.6 %collective-permute-start.6 = (f32[5,64,256]{2,1,0:T(8,128)}, f32[5,64,256]{2,1,0:T(8,128)S(1)}, u32[]{:S(2)}, u32[]{:S(2)}) collective-permute-start(f32[5,64,256]{2,1,0:T(8,128)} %add_dynamic-update-slice_fusion), channel_id=1, source_target_pairs={{0,96},{32,0},{64,32},{96,64},{1,97},{33,1},{65,33},{97,65},{2,98}... | collective-permute-start | bytes 983048 | tf_op jit(solution)/shard_map/ppermute | solution.py:449
  265.8 10.2 %collective-permute-start.4 = (f32[5,64,256]{2,1,0:T(8,128)}, f32[5,64,256]{2,1,0:T(8,128)S(1)}, u32[]{:S(2)}, u32[]{:S(2)}) collective-permute-start(f32[5,64,256]{2,1,0:T(8,128)} %add_dynamic-update-slice_fusion.1), channel_id=1, source_target_pairs={{0,32},{32,64},{64,96},{96,0},{1,33},{33,65},{65,97},{97,1},{2,34}... | collective-permute-start | bytes 983048 | tf_op jit(solution)/shard_map/ppermute | solution.py:449
  277.1 7.9 %collective-permute-start.8 = (f32[5,64,256]{2,1,0:T(8,128)S(1)}, f32[5,64,256]{2,1,0:T(8,128)S(1)}, u32[]{:S(2)}, u32[]{:S(2)}) collective-permute-start(f32[5,64,256]{2,1,0:T(8,128)S(1)} %add_add_fusion.refs_0_), channel_id=1, source_target_pairs={{0,96},{32,0},{64,32},{96,64},{1,97},{33,1},{65,33},{97,65},{2,98}... | collective-permute-start | bytes 983048 | tf_op jit(solution)/shard_map/ppermute | solution.py:449
  277.2 9.4 %collective-permute-start.7 = (f32[5,64,256]{2,1,0:T(8,128)S(1)}, f32[5,64,256]{2,1,0:T(8,128)S(1)}, u32[]{:S(2)}, u32[]{:S(2)}) collective-permute-start(f32[5,64,256]{2,1,0:T(8,128)S(1)} %add_add_fusion.refs_0_), channel_id=1, source_target_pairs={{0,32},{32,64},{64,96},{96,0},{1,33},{33,65},{65,97},{97,1},{2,34}... | collective-permute-start | bytes 983048 | tf_op jit(solution)/shard_map/ppermute | solution.py:449
  285.0 5.4 %collective-permute-start.10 = (f32[5,32,256]{2,1,0:T(8,128)S(1)}, f32[5,32,256]{2,1,0:T(8,128)S(1)}, u32[]{:S(2)}, u32[]{:S(2)}) collective-permute-start(f32[5,32,256]{2,1,0:T(8,128)S(1)} %slice.95), channel_id=1, source_target_pairs={{0,96},{32,0},{64,32},{96,64},{1,97},{33,1},{65,33},{97,65},{2,98}... | collective-permute-start | bytes 491528 | tf_op jit(solution)/shard_map/ppermute | solution.py:449
  286.6 6.8 %collective-permute-start.9 = (f32[5,32,256]{2,1,0:T(8,128)S(1)}, f32[5,32,256]{2,1,0:T(8,128)S(1)}, u32[]{:S(2)}, u32[]{:S(2)}) collective-permute-start(f32[5,32,256]{2,1,0:T(8,128)S(1)} %slice.94), channel_id=1, source_target_pairs={{0,32},{32,64},{64,96},{96,0},{1,33},{33,65},{65,97},{97,1},{2,34}... | collective-permute-start | bytes 491528 | tf_op jit(solution)/shard_map/ppermute | solution.py:449
  295.6 1.6 copy-start
  303.5 9.2 %collective-permute-start.11 = (f32[3,64,256]{2,1,0:T(8,128)}, f32[3,64,256]{2,1,0:T(8,128)S(1)}, u32[]{:S(2)}, u32[]{:S(2)}) collective-permute-start(f32[3,64,256]{2,1,0:T(8,128)} %get-tuple-element.56), channel_id=1, source_target_pairs={{0,32},{32,64},{64,96},{96,0},{1,33},{33,65},{65,97},{97,1},{2,34}... | collective-permute-start | bytes 589832 | tf_op jit(solution)/shard_map/ppermute | solution.py:449
  303.6 9.2 %collective-permute-start.12 = (f32[3,64,256]{2,1,0:T(8,128)}, f32[3,64,256]{2,1,0:T(8,128)S(1)}, u32[]{:S(2)}, u32[]{:S(2)}) collective-permute-start(f32[3,64,256]{2,1,0:T(8,128)} %get-tuple-element.57), channel_id=1, source_target_pairs={{0,64},{32,96},{64,0},{96,32},{1,65},{33,97},{65,1},{97,33},{2,66}... | collective-permute-start | bytes 589832 | tf_op jit(solution)/shard_map/ppermute | solution.py:449
  304.8 10.1 %collective-permute-start.13 = (f32[3,64,256]{2,1,0:T(8,128)}, f32[3,64,256]{2,1,0:T(8,128)S(1)}, u32[]{:S(2)}, u32[]{:S(2)}) collective-permute-start(f32[3,64,256]{2,1,0:T(8,128)} %get-tuple-element.58), channel_id=1, source_target_pairs={{0,96},{32,0},{64,32},{96,64},{1,97},{33,1},{65,33},{97,65},{2,98}... | collective-permute-start | bytes 589832 | tf_op jit(solution)/shard_map/ppermute | solution.py:449
  315.9 5.7 %collective-permute-start.16 = (f32[3,64,256]{2,1,0:T(8,128)S(1)}, f32[3,64,256]{2,1,0:T(8,128)S(1)}, u32[]{:S(2)}, u32[]{:S(2)}) collective-permute-start(f32[3,64,256]{2,1,0:T(8,128)S(1)} %add_add_fusion.1.refs_0_), channel_id=1, source_target_pairs={{0,96},{32,0},{64,32},{96,64},{1,97},{33,1},{65,33},{97,65},{2,98}... | collective-permute-start | bytes 589832 | tf_op jit(solution)/shard_map/ppermute | solution.py:449
  317.4 7.3 %collective-permute-start.15 = (f32[3,64,256]{2,1,0:T(8,128)S(1)}, f32[3,64,256]{2,1,0:T(8,128)S(1)}, u32[]{:S(2)}, u32[]{:S(2)}) collective-permute-start(f32[3,64,256]{2,1,0:T(8,128)S(1)} %add_add_fusion.1.refs_0_), channel_id=1, source_target_pairs={{0,64},{32,96},{64,0},{96,32},{1,65},{33,97},{65,1},{97,33},{2,66}... | collective-permute-start | bytes 589832 | tf_op jit(solution)/shard_map/ppermute | solution.py:449
  317.8 8.9 %collective-permute-start.14 = (f32[3,64,256]{2,1,0:T(8,128)S(1)}, f32[3,64,256]{2,1,0:T(8,128)S(1)}, u32[]{:S(2)}, u32[]{:S(2)}) collective-permute-start(f32[3,64,256]{2,1,0:T(8,128)S(1)} %add_add_fusion.1.refs_0_), channel_id=1, source_target_pairs={{0,32},{32,64},{64,96},{96,0},{1,33},{33,65},{65,97},{97,1},{2,34}... | collective-permute-start | bytes 589832 | tf_op jit(solution)/shard_map/ppermute | solution.py:449

commit v3 on v2

--- a/solution.py
+++ b/solution.py
@@ -111,8 +111,8 @@
 
 
 def project_kernel(
-    block, count, atom_ref, slot_ref, orbs_hbm, potential_hbm, projectors, sent, masked_ref,
-    orbs, potential, rows, counts, table, packed, sems,
+    block, count, atom_ref, slot_ref, orbs_hbm, potential_hbm, projectors_hbm, sent, masked_ref,
+    orbs, potential, projectors, rows, counts, table, packed, sems,
 ):
     half_rows = PLANES * SIZE
 
@@ -126,9 +126,11 @@
 
     copies = [load(potential_hbm, potential, sems.at[4])]
     copies += [load(orbs_hbm.at[k], orbs.at[k], sems.at[k]) for k in range(4)]
+    projectors_copy = pltpu.make_async_copy(projectors_hbm, projectors, sems.at[5, 0])
     for pair in copies:
         for copy in pair:
             copy.start()
+    projectors_copy.start()
 
     def arrived(pair):
         for copy in pair:
@@ -146,6 +148,9 @@
         return carry
 
     lax.fori_loop(0, ENTRIES, first, 0, unroll=8)
+    cosine, sine = cos_sin((0.5 * TIME_STEP) * rows[4])
+    rows[4] = cosine
+    rows[5] = sine
     for k in range(4):
         arrived(copies[k + 1])
 
@@ -155,12 +160,13 @@
 
         lax.fori_loop(0, ENTRIES, step, 0, unroll=8)
 
+    projectors_copy.wait()
     piece = 64
 
     def reduce(index, carry):
         at = pl.ds(pl.multiple_of(index * piece, piece), piece)
         lane = lax.broadcasted_iota(jnp.int32, (piece, LANES), 1)
-        cosine, sine = cos_sin((0.5 * TIME_STEP) * rows[4, at, :])
+        cosine, sine = rows[4, at, :], rows[5, at, :]
         inside = lane < counts[at, :]
         fields = []
         for n in range(ORBS):
@@ -211,16 +217,17 @@
             jax.ShapeDtypeStruct((GROUPS, SENT, LANES), jnp.float32),
             jax.ShapeDtypeStruct((ENTRIES, LANES), jnp.float32),
         ),
-        in_specs=[smem, smem, vmem, vmem, hbm, hbm, vmem],
+        in_specs=[smem, smem, vmem, vmem, hbm, hbm, hbm],
         out_specs=(vmem, vmem),
         scratch_shapes=[
             pltpu.VMEM((4, 2 * rows, LANES), jnp.float32),
             pltpu.VMEM((2 * rows, LANES), jnp.float32),
-            pltpu.VMEM((5, ENTRIES, LANES), jnp.float32),
+            pltpu.VMEM((4, ENTRIES, LANES), jnp.float32),
+            pltpu.VMEM((6, ENTRIES, LANES), jnp.float32),
             pltpu.VMEM((ENTRIES, LANES), jnp.int32),
             pltpu.VMEM((ENTRIES, LANES), jnp.float32),
             pltpu.VMEM((16, LANES), jnp.float32),
-            pltpu.SemaphoreType.DMA((5, 2)),
+            pltpu.SemaphoreType.DMA((6, 2)),
         ],
         compiler_params=pltpu.CompilerParams(vmem_limit_bytes=VMEM),
         cost_estimate=pl.CostEstimate(flops=10**9, bytes_accessed=36 * 10**6, transcendentals=0),
@@ -230,7 +237,7 @@
     )
 
 
-SHIFT_STEP = 4
+SHIFT_STEP = 8
 
 
 def shift_kernel(orbs, potential, *rest):
@@ -243,7 +250,7 @@
             for d in range(SHIFT_STEP):
                 for z in range(2):
                     tile = both[c][d * 8 : d * 8 + 8, z * LANES : (z + 1) * LANES]
-                    out[d, pl.ds(c * 128 + z * 64 + x, 8, stride=8), :] = tile
+                    out[pl.ds(d * 256 + c * 16 + z * 8 + x, 8, stride=32), :] = tile
 
 
 def shift(n, orbitals, potential, *first):
@@ -251,13 +258,13 @@
     return pl.pallas_call(
         shift_kernel,
         grid=(GROUPS // SHIFT_STEP,),
-        out_shape=jax.ShapeDtypeStruct((GROUPS, 256, LANES), jnp.float32),
+        out_shape=pltpu.HBM((GROUPS * 256, LANES), jnp.float32),
         in_specs=[
             pl.BlockSpec((2, 1, PLANES, width, SIZE), lambda i: (0, n, 0, i, 0)),
             pl.BlockSpec((PLANES, width, SIZE), lambda i: (0, i, 0)),
             *[pl.BlockSpec(memory_space=pl.ANY) for _ in first],
         ],
-        out_specs=pl.BlockSpec((SHIFT_STEP, 256, LANES), lambda i: (i, 0, 0)),
+        out_specs=pl.BlockSpec((SHIFT_STEP * 256, LANES), lambda i: (i, 0)),
         compiler_params=pltpu.CompilerParams(vmem_limit_bytes=VMEM),
         cost_estimate=pl.CostEstimate(flops=10**8, bytes_accessed=11 * 10**6, transcendentals=0),
         name=f"shift{n}",
@@ -285,9 +292,10 @@
 
     def step(entry, carry):
         row = place[entry]
+        at = [pl.ds(row + c * 16, 1) for c in range(2)]
+        both = [field[at[c], :] + updates[c, pl.ds(entry, 1), :] for c in range(2)]
         for c in range(2):
-            at = pl.ds(row + c * 128, 1)
-            field[at, :] = field[at, :] + updates[c, pl.ds(entry, 1), :]
+            field[at[c], :] = both[c]
         return carry
 
     lax.fori_loop(0, ENTRIES, step, 0, unroll=8)
@@ -302,7 +310,7 @@
     hbm = pl.BlockSpec(memory_space=pltpu.HBM)
     return pl.pallas_call(
         functools.partial(correct_kernel, n),
-        out_shape=jax.ShapeDtypeStruct((GROUPS * 256, LANES), jnp.float32),
+        out_shape=pltpu.HBM((GROUPS * 256, LANES), jnp.float32),
         in_specs=[smem, vmem, vmem, vmem, vmem, hbm],
         out_specs=hbm,
         scratch_shapes=[
@@ -312,34 +320,47 @@
             pltpu.SemaphoreType.DMA((2,)),
         ],
         input_output_aliases={5: 0},
-        compiler_params=pltpu.CompilerParams(vmem_limit_bytes=VMEM),
+        compiler_params=pltpu.CompilerParams(vmem_limit_bytes=24 << 20),
         cost_estimate=pl.CostEstimate(flops=5 * 10**8, bytes_accessed=20 * 10**6, transcendentals=0),
         name=f"correct{n}",
-    )(place, received, strength, atoms, masked, before.reshape(GROUPS * 256, LANES))
+    )(place, received, strength, atoms, masked, before)
+
+
+LINES_STEP = 4
 
 
 def lines_kernel(n, field, left, right, *rest):
-    *chunks, turned, sems = rest[-2 - len(CHUNKS) :]
-    y = pl.program_id(0)
-    real = [field[:, 0, z, 0].reshape(SIZE, LANES) for z in range(2)]
-    imag = [field[:, 1, z, 0].reshape(SIZE, LANES) for z in range(2)]
-    real, imag = propagate_lanes(right, real, imag)
-    both = propagate_rows(left, real, imag)
-    for c in range(2):
+    *chunks, half_done, turned, sems = rest[-3 - len(CHUNKS) :]
+    step = pl.program_id(0)
+    for k in range(LINES_STEP):
+        real, imag = ([field[:, k, c, z].reshape(SIZE, LANES) for z in range(2)] for c in range(2))
+        both = propagate_lanes(right, real, imag)
+        y = step * LINES_STEP + k
+        for c in range(2):
+            for z in range(2):
+                half_done[c, z, y] = both[c][:, z * LANES : (z + 1) * LANES]
+
+    @pl.when(step == pl.num_programs(0) - 1)
+    def _():
+        rows = turned.reshape(GROUPS, 2, PLANES * 16, LANES)
+        copies = []
         for z in range(2):
-            for d in range(GROUPS):
-                tile = both[c][d * 8 : d * 8 + 8, z * LANES : (z + 1) * LANES]
-                turned[d, c, z, pl.ds(y, 8, stride=8), :] = tile
-
-    @pl.when(y == pl.num_programs(0) - 1)
-    def _():
-        copies, begin = [], 0
-        for k, (chunk, planes) in enumerate(zip(chunks, CHUNKS)):
-            part = turned.at[:, :, :, pl.ds(begin * 8, planes * 8)]
-            copies.append(pltpu.make_async_copy(part, chunk.at[:, :, n], sems.at[k]))
-            begin += planes
-        for copy in copies:
-            copy.start()
+            for y in range(0, 8, 2):
+                real, imag = (
+                    jnp.concatenate([half_done[c, z, y], half_done[c, z, y + 1]], axis=1) for c in range(2)
+                )
+                both = propagate_rows(left, real, imag)
+                for c in range(2):
+                    for k in range(2):
+                        for d in range(GROUPS):
+                            tile = both[c][d * 8 : d * 8 + 8, k * LANES : (k + 1) * LANES]
+                            rows[d, z, pl.ds(c * 8 + y + k, 8, stride=16), :] = tile
+            begin = 0
+            for k, (chunk, planes) in enumerate(zip(chunks, CHUNKS)):
+                part = turned.at[:, z, pl.ds(begin, planes)]
+                copies.append(pltpu.make_async_copy(part, chunk.at[:, :, n, z], sems.at[z, k]))
+                copies[-1].start()
+                begin += planes
         for copy in copies:
             copy.wait()
 
@@ -348,35 +369,36 @@
     hbm = pl.BlockSpec(memory_space=pltpu.HBM)
     return pl.pallas_call(
         functools.partial(lines_kernel, n),
-        grid=(8,),
+        grid=(8 // LINES_STEP,),
         out_shape=tuple(
-            jax.ShapeDtypeStruct((GROUPS, 2, ORBS, 2, planes * 8, LANES), jnp.float32) for planes in CHUNKS
+            jax.ShapeDtypeStruct((GROUPS, planes, ORBS, 2, 16, LANES), jnp.float32) for planes in CHUNKS
         ),
         in_specs=[
-            pl.BlockSpec((GROUPS, 2, 2, 1, 8, LANES), lambda i: (0, 0, 0, i, 0, 0)),
+            pl.BlockSpec((GROUPS, LINES_STEP, 2, 2, 8, LANES), lambda i: (0, i, 0, 0, 0, 0)),
             pl.BlockSpec(left.shape, lambda i: (0, 0, 0)),
             pl.BlockSpec(right.shape, lambda i: (0, 0, 0)),
             *[hbm for _ in (*before, *first)],
         ],
         out_specs=tuple(hbm for _ in CHUNKS),
         scratch_shapes=[
-            pltpu.VMEM((GROUPS, 2, 2, 64, LANES), jnp.float32),
-            pltpu.SemaphoreType.DMA((len(CHUNKS),)),
+            pltpu.VMEM((2, 2, 8, SIZE, LANES), jnp.float32),
+            pltpu.VMEM((GROUPS, 2, PLANES, 16, LANES), jnp.float32),
+            pltpu.SemaphoreType.DMA((2, len(CHUNKS))),
         ],
         input_output_aliases={3 + k: k for k in range(len(before))},
         compiler_params=pltpu.CompilerParams(vmem_limit_bytes=VMEM),
         cost_estimate=pl.CostEstimate(flops=5 * 10**9, bytes_accessed=10 * 10**6, transcendentals=0),
         name=f"lines{n}",
-    )(field.reshape(GROUPS, 2, 2, 8, 8, LANES), left, right, *before, *first)
-
-
-def finish_kernel(band, field, potential, left, *rest):
-    out, *pieces, whole = rest[-6:]
+    )(field.reshape(GROUPS, 8, 2, 2, 8, LANES), left, right, *before, *first)
+
+
+def finish_kernel(halves, band, field, potential, left, *rest):
+    out, *pieces, whole = rest[-2 - BANDS * halves :]
     cosine, sine = cos_sin((0.5 * TIME_STEP) * potential[0])
     total = None
     for n in range(ORBS):
         real, imag = (
-            jnp.concatenate([field[:, c, n, z].reshape(SIZE, LANES) for z in range(2)], axis=1) for c in range(2)
+            jnp.concatenate([field[:, 0, n, z, c].reshape(SIZE, LANES) for z in range(2)], axis=1) for c in range(2)
         )
         real, imag = propagate_rows(left, real, imag)
         real, imag = cosine * real + sine * imag, cosine * imag - sine * real
@@ -385,38 +407,38 @@
         square = real * real + imag * imag
         total = square if total is None else total + square
     whole[...] = total
-    rows = SIZE // BANDS
+    rows = SIZE // BANDS // halves
     for k, piece in enumerate(pieces):
-        begin = pl.multiple_of((band[0] + k) % BANDS * rows, rows)
-        piece[0] = whole[pl.ds(begin, rows), :]
-
-
-def finish(planes, begin, band, field, potential, left, before=(), first=()):
-    rows = SIZE // BANDS
-    return pl.pallas_call(
-        finish_kernel,
+        begin = (band[0] + k // halves) % BANDS * halves + k % halves
+        piece[0] = whole[pl.ds(pl.multiple_of(begin * rows, rows), rows), :]
+
+
+def finish(planes, begin, halves, band, field, potential, left, before=(), first=()):
+    rows = SIZE // BANDS // halves
+    return pl.pallas_call(
+        functools.partial(finish_kernel, halves),
         grid=(planes,),
         out_shape=(
             jax.ShapeDtypeStruct((2, ORBS, PLANES, SIZE, SIZE), jnp.float32),
-            *[jax.ShapeDtypeStruct((planes, rows, SIZE), jnp.float32) for _ in range(BANDS)],
+            *[jax.ShapeDtypeStruct((planes, rows, SIZE), jnp.float32) for _ in range(BANDS * halves)],
         ),
         in_specs=[
             pl.BlockSpec(memory_space=pltpu.SMEM),
-            pl.BlockSpec((GROUPS, 2, ORBS, 2, 8, LANES), lambda i: (0, 0, 0, 0, i, 0)),
+            pl.BlockSpec((GROUPS, 1, ORBS, 2, 2, 8, LANES), lambda i: (0, i, 0, 0, 0, 0, 0)),
             pl.BlockSpec((1, SIZE, SIZE), lambda i: (i + begin, 0, 0)),
             pl.BlockSpec(left.shape, lambda i: (0, 0, 0)),
             *[pl.BlockSpec(memory_space=pl.ANY) for _ in (*before, *first)],
         ],
         out_specs=(
             pl.BlockSpec((2, ORBS, 1, SIZE, SIZE), lambda i: (0, 0, i + begin, 0, 0)),
-            *[pl.BlockSpec((1, rows, SIZE), lambda i: (i, 0, 0)) for _ in range(BANDS)],
+            *[pl.BlockSpec((1, rows, SIZE), lambda i: (i, 0, 0)) for _ in range(BANDS * halves)],
         ),
         scratch_shapes=[pltpu.VMEM((SIZE, SIZE), jnp.float32)],
         input_output_aliases={4 + k: k for k in range(len(before))},
         compiler_params=pltpu.CompilerParams(vmem_limit_bytes=VMEM),
         cost_estimate=pl.CostEstimate(flops=10**9 * planes, bytes_accessed=3 * 10**6 * planes, transcendentals=0),
         name=f"finish{begin}",
-    )(band, field, potential, left, *before, *first)
+    )(band, field.reshape(GROUPS, planes, ORBS, 2, 2, 8, LANES), potential, left, *before, *first)
 
 
 def collect_kernel(owners, band, *refs):
@@ -435,11 +457,11 @@
         in_specs=[
             pl.BlockSpec(memory_space=pltpu.SMEM),
             *[pl.BlockSpec((1, piece.shape[1], SIZE), lambda i: (i, 0, 0)) for piece in pieces],
-            *[pl.BlockSpec(memory_space=pl.ANY) for _ in before],
+            *[pl.BlockSpec(memory_space=pltpu.HBM) for _ in before],
         ],
         out_specs=pl.BlockSpec((1, SIZE, SIZE), lambda i: (i + begin, 0, 0)),
         input_output_aliases={1 + len(pieces) + k: k for k in range(len(before))},
-        compiler_params=pltpu.CompilerParams(vmem_limit_bytes=16 << 20),
+        compiler_params=pltpu.CompilerParams(vmem_limit_bytes=VMEM),
         cost_estimate=pl.CostEstimate(flops=0, bytes_accessed=3 * 10**6, transcendentals=0),
         name=f"collect{begin}",
     )(band, *pieces, *before)
@@ -450,22 +472,40 @@
 
 
 def ring_reduce(pieces):
-    own, right, across, left = pieces
-    low, high = (slice(None), slice(0, SIZE // BANDS // 2)), (slice(None), slice(SIZE // BANDS // 2, None))
-    right = right.at[low].add(onward(across[low], 1))
-    left = left.at[high].add(onward(across[high], 3))
-    return own + onward(right, 1) + onward(left, 3)
-
-
-def ring_gather(total):
-    before, after = onward(total, 1), onward(total, 3)
+    own_low, own_high, next_low, next_high, across_low, across_high, last_low, last_high = pieces
+    from_last = onward(across_low, 1)
+    from_next = onward(across_high, 3)
+    high = own_high + onward(next_high, 1)
+    low = own_low + onward(last_low, 3)
+    return low + onward(next_low + from_last, 1), high + onward(last_high + from_next, 3)
+
+
+def ring_gather(low, high):
+    last_low, next_high = onward(low, 1), onward(high, 3)
+    last_high, next_low = onward(high, 1), onward(low, 3)
+    pieces = low, high, last_low, last_high, next_low, next_high, onward(last_low, 1), onward(next_high, 3)
     half = SIZE // BANDS // 2
-    pieces = total, before, after, onward(before[:, :half], 1), onward(after[:, half:], 3)
-    return pieces, ((0, 0), (3, 0), (1, 0), (2, 0), (2, half))
-
-
-def direct_reduce(pieces):
-    return pieces[0] + onward(pieces[1], 1) + onward(pieces[2], 2) + onward(pieces[3], 3)
+    return pieces, tuple((owner, offset) for owner in (0, 3, 1, 2) for offset in (0, half))
+
+
+def add_kernel(own, from_last, across, from_next, *rest):
+    rest[-1][...] = own[...] + from_last[...] + across[...] + from_next[...]
+
+
+def direct_reduce(pieces, first):
+    parts = [pieces[0], *[onward(pieces[k], k) for k in range(1, BANDS)]]
+    return pl.pallas_call(
+        add_kernel,
+        out_shape=jax.ShapeDtypeStruct(pieces[0].shape, jnp.float32),
+        in_specs=[
+            *[pl.BlockSpec(memory_space=pltpu.VMEM) for _ in parts],
+            *[pl.BlockSpec(memory_space=pltpu.HBM) for _ in first],
+        ],
+        out_specs=pl.BlockSpec(memory_space=pltpu.VMEM),
+        compiler_params=pltpu.CompilerParams(vmem_limit_bytes=VMEM),
+        cost_estimate=pl.CostEstimate(flops=10**6, bytes_accessed=10**6, transcendentals=0),
+        name="add",
+    )(*parts, *first)
 
 
 def direct_gather(total):
@@ -486,7 +526,7 @@
     )
     received = exchange(sent)
     x, y, z = entry_block // 512, (entry_block // 2) % SIZE, entry_block % 2
-    place = (y // 8) * 256 + z * 64 + (y % 8) * 8 + x
+    place = y * 32 + z * 8 + x
     in_slot = owner_slot[:, None] == atom_ids[None, :]
     strength_atom = jnp.sum(jnp.where(in_slot, strength[None, :], 0.0), axis=1).reshape(4, LANES)
     atoms = entry_atom.reshape(1, ENTRIES)
@@ -507,15 +547,14 @@
     out, density, ready, begin = (), (), (), 0
     for k, planes in enumerate(CHUNKS):
         field = exchange(back[k])
-        made, *pieces = finish(planes, begin, band, field, potential, left, out, ready)
+        made, *pieces = finish(planes, begin, 2 if k == 0 else 1, band, field, potential, left, out, ready)
         out = (made,)
         if k == 0:
-            density = (collect(begin, band, *ring_gather(ring_reduce(pieces))),)
-            ready = density
+            sums, owners = ring_gather(*ring_reduce(pieces))
+            ready = sums[2:]
         else:
-            total = direct_reduce(pieces)
-            ready = (total,)
-            density = (collect(begin, band, *direct_gather(total), *density),)
+            sums, owners = direct_gather(direct_reduce(pieces, density))
+        density = (collect(begin, band, sums, owners, *density),)
         begin += planes
     return out[0], density[0], forces
 

time: 330 us -> 316 us (0.958)
  waiting for transfers between devices: 116 us -> 102 us
  starting transfers between devices: 47 us -> 54.5 us
  Pallas kernels: 85.3 us -> 81.8 us
    ppermute x17 -> x21, waiting for transfers between devices: 46.2 us -> 23.8 us  [onward(): lax.ppermute(array, 'band', [(b, (b + steps) % BANDS) for b in range(BAND...]
    ppermute x17 -> x21, starting transfers between devices: 22.2 us -> 31.1 us  [onward(): lax.ppermute(array, 'band', [(b, (b + steps) % BANDS) for b in range(BAND...]
    all_to_all x4, waiting for transfers between devices: 69.8 us -> 78 us  [exchange(): lax.all_to_all(array, 'grid', split_axis=0, concat_axis=0, tiled=True)]
    pallas_call x8 -> x9, Pallas kernels: 68.9 us -> 63 us  [the longest x2 17 us: lines(): pl.pallas_call(functools.partial(lines_kernel, n), grid=(8 // LINES_STEP,...]
  transfers between devices with their start and end apart: 21 -> 25, of which waited for: 16 -> 17; matrix products, arithmetic and copies ran while one was open for 3% -> 2% of each run, Pallas kernels for 14% -> 14%
where the time goes in v3:
time: 316 us; the launch traced here: 314 us
  waiting for transfers between devices  102 us (32%)
  Pallas kernels  81.8 us (26%)
  blocking collectives  67.1 us (21%)
  starting transfers between devices  54.5 us (17%)
  other arithmetic  6.12 us (2%)
    all_to_all x4, waiting for transfers between devices, exchange(): lax.all_to_all(array, 'grid', split_axis=0, concat_axis=0, tiled=True)  78 us
    all_to_all x1, blocking collectives, exchange(): lax.all_to_all(array, 'grid', split_axis=0, concat_axis=0, tiled=True)  67.1 us
    ppermute x21, starting transfers between devices, onward(): lax.ppermute(array, 'band', [(b, (b + steps) % BANDS) for b in range(BAND...  31.1 us
    ppermute x21, waiting for transfers between devices, onward(): lax.ppermute(array, 'band', [(b, (b + steps) % BANDS) for b in range(BAND...  23.8 us
    all_to_all x4, starting transfers between devices, exchange(): lax.all_to_all(array, 'grid', split_axis=0, concat_axis=0, tiled=True)  23.4 us
    pallas_call x2, Pallas kernels, lines(): pl.pallas_call(functools.partial(lines_kernel, n), grid=(8 // LINES_STEP,...  17 us
    pallas_call x2, Pallas kernels, shift(): pl.pallas_call(shift_kernel, grid=(GROUPS // SHIFT_STEP,), out_shape=pltp...  16.3 us
    pallas_call x2, Pallas kernels, finish(): pl.pallas_call(functools.partial(finish_kernel, halves), grid=(planes,),...  15.4 us
  transfers between devices with their start and end apart: 25, of which 17 were waited for; matrix products, arithmetic and copies ran while one was open for 2% of the time, Pallas kernels for 14%

profile of v3, /device:TPU:0, one launch (start us, length us, event | category | flops | bytes accessed | tf_op | source)
XLA Modules:
  0.0 314.3 jit_solution(15110769047842574138)
XLA Ops:
  0.6 12.2 %project.1 = (f32[32,24,128]{2,1,0:T(8,128)}, f32[512,128]{1,0:T(8,128)}) custom-call(s32[512]{0:T(512)} %block.1, s32[512]{0:T(512)} %count.1, s32[1,512]{1,0:T(1,128)} %bitcast.12, s32[1,512]{1,0:T(1,128)} %bitcast.23, f32[4,2048,256]{2,1,0:T(8,128)} %bitcast.17, f32[2048,256]{1,0:T(8,128)} %bitcast.20, f32[4,512,128]{2,1,0:T(8,128)} %projectors_hbm.1), custom_call_target="tpu_custom_call" | custom-call | flops 1000000000 | bytes 36000000 | tf_op jit(solution)/shard_map/project/pallas_call | solution.py:214
  12.8 8.3 %all-to-all-start = ((f32[32,24,128]{2,1,0:T(8,128)}), f32[32,24,128]{2,1,0:T(8,128)S(1)}, u32[]{:S(2)}, u32[]{:S(2)}) async-start(f32[32,24,128]{2,1,0:T(8,128)} %get-tuple-element.23), calls=%async_computation | async-start | bytes 786432 | tf_op jit(solution)/shard_map/all_to_all | solution.py:516
  21.2 8.1 %shift0.1.before = f32[8192,128]{1,0:T(8,128)} custom-call(f32[2,2,8,256,256]{4,3,2,1,0:T(8,128)} %orbs.3, f32[8,256,256]{2,1,0:T(8,128)} %potential.7), custom_call_target="tpu_custom_call" | custom-call | flops 100000000 | bytes 11000000 | tf_op jit(solution)/shard_map/shift0/pallas_call | solution.py:258
  29.6 1.8 all-to-all-done.received
  31.4 6.2 %correct0.1.rest_0_ = f32[8192,128]{1,0:T(8,128)} custom-call(s32[512]{0:T(512)S(1)} %fusion.3.place, f32[32,24,128]{2,1,0:T(8,128)S(1)} %all-to-all-done.received, f32[4,128]{1,0:T(4,128)S(1)} %bitcast.15, s32[1,512]{1,0:T(1,128)S(1)} %bitcast.13, f32[512,128]{1,0:T(8,128)S(1)} %copy-done, f32[8192,128]{1,0:T(8,128)} %shift0.1.before), custom_call_target="tpu_custom_call", output_to_operand_aliasing={{}: (5, {})} | custom-call | flops 500000000 | bytes 20000000 | tf_op jit(solution)/shard_map/correct0/pallas_call | solution.py:311
  37.6 5.7 %all-to-all-start.2 = ((f32[32,256,128]{2,1,0:T(8,128)}), f32[32,256,128]{2,1,0:T(8,128)}, u32[]{:S(2)}, u32[]{:S(2)}) async-start(f32[32,256,128]{2,1,0:T(8,128)} %bitcast.18), calls=%async_computation.2 | async-start | bytes 8388608 | tf_op jit(solution)/shard_map/all_to_all | solution.py:516
  43.3 8.1 %shift1.1.before = f32[8192,128]{1,0:T(8,128)} custom-call(f32[2,2,8,256,256]{4,3,2,1,0:T(8,128)} %orbs.3, f32[8,256,256]{2,1,0:T(8,128)} %potential.7, f32[8192,128]{1,0:T(8,128)} %correct0.1.rest_0_), custom_call_target="tpu_custom_call" | custom-call | flops 100000000 | bytes 11000000 | tf_op jit(solution)/shard_map/shift1/pallas_call | solution.py:258
  51.5 6.2 %correct1.1 = f32[8192,128]{1,0:T(8,128)} custom-call(s32[512]{0:T(512)S(1)} %fusion.3.place, f32[32,24,128]{2,1,0:T(8,128)S(1)} %all-to-all-done.received, f32[4,128]{1,0:T(4,128)S(1)} %bitcast.16, s32[1,512]{1,0:T(1,128)S(1)} %bitcast.14, f32[512,128]{1,0:T(8,128)S(1)} %copy-done, f32[8192,128]{1,0:T(8,128)} %shift1.1.before), custom_call_target="tpu_custom_call", output_to_operand_aliasing={{}: (5, {})} | custom-call | flops 500000000 | bytes 20000000 | tf_op jit(solution)/shard_map/correct1/pallas_call | solution.py:311
  57.7 39.1 %all-to-all-done.2 = f32[32,256,128]{2,1,0:T(8,128)} async-done(((f32[32,256,128]{2,1,0:T(8,128)}), f32[32,256,128]{2,1,0:T(8,128)}, u32[]{:S(2)}, u32[]{:S(2)}) %all-to-all-start.2) | async-done | bytes 4194336 | tf_op jit(solution)/shard_map/all_to_all | solution.py:516
  96.8 4.9 %all-to-all-start.1 = ((f32[32,256,128]{2,1,0:T(8,128)}), f32[32,256,128]{2,1,0:T(8,128)}, u32[]{:S(2)}, u32[]{:S(2)}) async-start(f32[32,256,128]{2,1,0:T(8,128)} %bitcast.19), calls=%async_computation.1 | async-start | bytes 8388608 | tf_op jit(solution)/shard_map/all_to_all | solution.py:516
  101.9 3.3 %collective-permute-start.1 = (f32[3,16]{1,0:T(4,128)S(1)}, f32[3,16]{1,0:T(4,128)S(1)}, u32[]{:S(2)}, u32[]{:S(2)}) collective-permute-start(f32[3,16]{1,0:T(4,128)S(1)} %broadcast_multiply_fusion), channel_id=1, source_target_pairs={{0,64},{32,96},{64,0},{96,32},{1,65},{33,97},{65,1},{97,33},{2,66}... | collective-permute-start | bytes 584 | tf_op jit(solution)/shard_map/ppermute | solution.py:471
  105.2 1.1 collective-permute-start.2
  107.2 1.6 collective-permute-done.2
  108.8 2.3 collective-permute-done
  111.7 8.5 %lines0.1 = (f32[32,5,2,2,16,128]{5,4,3,2,1,0:T(8,128)}, f32[32,3,2,2,16,128]{5,4,3,2,1,0:T(8,128)}) custom-call(f32[32,8,2,2,8,128]{5,4,3,2,1,0:T(8,128)} %bitcast.9.field, bf16[2,256,768]{2,1,0:T(8,128)(2,1)} %constant.73.clone.left, bf16[2,768,256]{2,1,0:T(8,128)(2,1)} %constant.74.clone.right), custom_call_target="tpu_custom_call" | custom-call | flops 5000000000 | bytes 10000000 | tf_op jit(solution)/shard_map/lines0/pallas_call | solution.py:370
  120.1 35.0 %all-to-all-done.1 = f32[32,256,128]{2,1,0:T(8,128)} async-done(((f32[32,256,128]{2,1,0:T(8,128)}), f32[32,256,128]{2,1,0:T(8,128)}, u32[]{:S(2)}, u32[]{:S(2)}) %all-to-all-start.1) | async-done | bytes 4194336 | tf_op jit(solution)/shard_map/all_to_all | solution.py:516
  155.2 8.5 %lines1.1 = (f32[32,5,2,2,16,128]{5,4,3,2,1,0:T(8,128)}, f32[32,3,2,2,16,128]{5,4,3,2,1,0:T(8,128)}) custom-call(f32[32,8,2,2,8,128]{5,4,3,2,1,0:T(8,128)} %bitcast.7.field, bf16[2,256,768]{2,1,0:T(8,128)(2,1)} %constant.73.clone.left, bf16[2,768,256]{2,1,0:T(8,128)(2,1)} %constant.74.clone.right, ...), custom_call_target="tpu_custom_call", output_to_operand_aliasing={{0}: (3, {}), {1}: (4, {})} | custom-call | flops 5000000000 | bytes 10000000 | tf_op jit(solution)/shard_map/lines1/pallas_call | solution.py:370
  163.7 67.1 %all_to_all.25 = f32[32,5,2,2,16,128]{5,4,3,2,1,0:T(8,128)} all-to-all(f32[32,5,2,2,16,128]{5,4,3,2,1,0:T(8,128)} %get-tuple-element.28), channel_id=1, replica_groups=mesh['band'=4,'grid'=32] {'grid'}, dimensions={0} | all-to-all | bytes 10485760 | tf_op jit(solution)/shard_map/all_to_all | solution.py:516
  230.8 4.6 %all-to-all-start.3 = ((f32[32,3,2,2,16,128]{5,4,3,2,1,0:T(8,128)}), f32[32,3,2,2,16,128]{5,4,3,2,1,0:T(8,128)S(1)}, u32[]{:S(2)}, u32[]{:S(2)}) async-start(f32[32,3,2,2,16,128]{5,4,3,2,1,0:T(8,128)} %get-tuple-element.27), calls=%async_computation.3 | async-start | bytes 6291456 | tf_op jit(solution)/shard_map/all_to_all | solution.py:516
  235.4 9.1 %finish0.1 = (f32[2,2,8,256,256]{4,3,2,1,0:T(8,128)}, f32[5,32,256]{2,1,0:T(8,128)}, f32[5,32,256]{2,1,0:T(8,128)}, f32[5,32,256]{2,1,0:T(8,128)}, f32[5,32,256]...) custom-call(s32[1]{0:T(128)} %bitcast.band, ...), custom_call_target="tpu_custom_call" | custom-call | flops 5000000000 | bytes 15000000 | tf_op jit(solution)/shard_map/finish0/pallas_call | solution.py:418
  244.5 1.6 collective-permute-start.4
  246.2 1.7 collective-permute-start.8
  247.9 1.8 collective-permute-start.3
  249.7 2.8 collective-permute-done.4
  253.8 1.6 collective-permute-start.7
  256.3 1.7 collective-permute-start.9
  258.1 3.8 %collective-permute-done.5 = f32[5,32,256]{2,1,0:T(8,128)S(1)} collective-permute-done((f32[5,32,256]{2,1,0:T(8,128)S(1)}, f32[5,32,256]{2,1,0:T(8,128)S(1)}, u32[]{:S(2)}, u32[]{:S(2)}) %collective-permute-start.5) | collective-permute-done | bytes 163872 | tf_op jit(solution)/shard_map/ppermute | solution.py:471
  261.8 1.6 add_add_fusion.1.refs_0_
  263.9 1.6 add_add_fusion.refs_1_
  265.5 2.8 collective-permute-start.12
  268.3 2.0 collective-permute-start.10
  270.3 1.2 collective-permute-done.6.rest_1_.refs_2_
  271.5 1.3 collective-permute-done.12.rest_4_.refs_5_
  272.8 2.4 collective-permute-start.14
  275.2 2.0 all-to-all-done.3
  278.8 6.3 %finish5.1 = (f32[2,2,8,256,256]{4,3,2,1,0:T(8,128)}, f32[3,64,256]{2,1,0:T(8,128)}, f32[3,64,256]{2,1,0:T(8,128)}, f32[3,64,256]{2,1,0:T(8,128)}, f32[3,64,256]{2,1,0:T(8,128)}) custom-call(s32[1]{0:T(128)} %bitcast.band, f32[32,3,2,2,2,8,128]{6,5,4,3,2,1,0:T(8,128)} %bitcast.21, f32[8,256,256]{2,1,0:T(8,128)} %potential.7, ...), custom_call_target="tpu_custom_call", output_to_operand_aliasing={{0}: (4, {})} | custom-call | flops 3000000000 | bytes 9000000 | tf_op jit(solution)/shard_map/finish5/pallas_call | solution.py:418
  285.1 1.6 collective-permute-start.15
  286.7 2.9 collective-permute-start.16
  289.7 1.3 collective-permute-start.17
  291.0 3.8 %collect0.1.rest_0_.refs_4_ = f32[8,256,256]{2,1,0:T(8,128)} custom-call(s32[1]{0:T(128)} %bitcast.band, f32[5,32,256]{2,1,0:T(8,128)} %add_add_fusion.1.refs_0_, f32[5,32,256]{2,1,0:T(8,128)} %add_add_fusion.refs_1_, f32[5,32,256]{2,1,0:T(8,128)} %copy-done.3, f32[5,32,256]{2,1,0:T(8,128)} %collective-permute-done.10.rest_2_.refs_3_, ...), custom_call_target="tpu_custom_call" | custom-call | bytes 3000000 | tf_op jit(solution)/shard_map/collect0/pallas_call | solution.py:453
  294.8 1.8 collective-permute-done.16.across
  297.3 1.9 add.86.refs_0_
  299.3 2.0 collective-permute-start.20
  301.3 1.1 collective-permute-start.19
  303.2 3.8 %collective-permute-done.20.refs_3_ = f32[3,64,256]{2,1,0:T(8,128)S(1)} collective-permute-done((f32[3,64,256]{2,1,0:T(8,128)}, f32[3,64,256]{2,1,0:T(8,128)S(1)}, u32[]{:S(2)}, u32[]{:S(2)}) %collective-permute-start.20) | collective-permute-done | bytes 196640 | tf_op jit(solution)/shard_map/ppermute | solution.py:471
  307.0 1.8 collective-permute-done.19.refs_2_
  308.8 2.0 collective-permute-done.18.refs_1_
  311.5 2.9 collect5.1
  (58 shorter events, 8.6 us)
Async XLA Ops:
  12.8 18.6 %all-to-all-start = ((f32[32,24,128]{2,1,0:T(8,128)}), f32[32,24,128]{2,1,0:T(8,128)S(1)}, u32[]{:S(2)}, u32[]{:S(2)}) async-start(f32[32,24,128]{2,1,0:T(8,128)} %get-tuple-element.23), calls=%async_computation | async-start | bytes 786432 | tf_op jit(solution)/shard_map/all_to_all | solution.py:516
  21.1 8.2 %copy-start.11 = (s32[512]{0:T(512)S(1)}, s32[512]{0:T(512)}, u32[]{:S(2)}) copy-start(s32[512]{0:T(512)} %param.16) | copy-start | bytes 6148
  21.1 8.2 %copy-start.13 = (f32[512]{0:T(512)S(1)}, f32[512]{0:T(512)}, u32[]{:S(2)}) copy-start(f32[512]{0:T(512)} %param.17) | copy-start | bytes 6148
  21.1 8.4 %copy-start.12 = (s32[512]{0:T(512)S(1)}, s32[512]{0:T(512)}, u32[]{:S(2)}) copy-start(s32[512]{0:T(512)} %block.1) | copy-start | bytes 6148
  21.1 10.3 %copy-start = (f32[512,128]{1,0:T(8,128)S(1)}, f32[512,128]{1,0:T(8,128)}, u32[]{:S(2)}) copy-start(f32[512,128]{1,0:T(8,128)} %get-tuple-element.24.masked) | copy-start | bytes 786436
  21.1 10.3 %copy-start.1 = (s32[512]{0:T(512)S(1)}, s32[512]{0:T(512)}, u32[]{:S(2)}) copy-start(s32[512]{0:T(512)} %param.13) | copy-start | bytes 6148
  37.6 59.2 %all-to-all-start.2 = ((f32[32,256,128]{2,1,0:T(8,128)}), f32[32,256,128]{2,1,0:T(8,128)}, u32[]{:S(2)}, u32[]{:S(2)}) async-start(f32[32,256,128]{2,1,0:T(8,128)} %bitcast.18), calls=%async_computation.2 | async-start | bytes 8388608 | tf_op jit(solution)/shard_map/all_to_all | solution.py:516
  96.8 58.4 %all-to-all-start.1 = ((f32[32,256,128]{2,1,0:T(8,128)}), f32[32,256,128]{2,1,0:T(8,128)}, u32[]{:S(2)}, u32[]{:S(2)}) async-start(f32[32,256,128]{2,1,0:T(8,128)} %bitcast.19), calls=%async_computation.1 | async-start | bytes 8388608 | tf_op jit(solution)/shard_map/all_to_all | solution.py:516
  101.9 5.3 %collective-permute-start.1 = (f32[3,16]{1,0:T(4,128)S(1)}, f32[3,16]{1,0:T(4,128)S(1)}, u32[]{:S(2)}, u32[]{:S(2)}) collective-permute-start(f32[3,16]{1,0:T(4,128)S(1)} %broadcast_multiply_fusion), channel_id=1, source_target_pairs={{0,64},{32,96},{64,0},{96,32},{1,65},{33,97},{65,1},{97,33},{2,66}... | collective-permute-start | bytes 584 | tf_op jit(solution)/shard_map/ppermute | solution.py:471
  105.2 3.6 %collective-permute-start.2 = (f32[3,16]{1,0:T(4,128)S(1)}, f32[3,16]{1,0:T(4,128)S(1)}, u32[]{:S(2)}, u32[]{:S(2)}) collective-permute-start(f32[3,16]{1,0:T(4,128)S(1)} %broadcast_multiply_fusion), channel_id=1, source_target_pairs={{0,96},{32,0},{64,32},{96,64},{1,97},{33,1},{65,33},{97,65},{2,98}... | collective-permute-start | bytes 584 | tf_op jit(solution)/shard_map/ppermute | solution.py:471
  106.3 4.8 %collective-permute-start = (f32[3,16]{1,0:T(4,128)S(1)}, f32[3,16]{1,0:T(4,128)S(1)}, u32[]{:S(2)}, u32[]{:S(2)}) collective-permute-start(f32[3,16]{1,0:T(4,128)S(1)} %broadcast_multiply_fusion), channel_id=1, source_target_pairs={{0,32},{32,64},{64,96},{96,0},{1,33},{33,65},{65,97},{97,1},{2,34}... | collective-permute-start | bytes 584 | tf_op jit(solution)/shard_map/ppermute | solution.py:471
  230.8 46.4 %all-to-all-start.3 = ((f32[32,3,2,2,16,128]{5,4,3,2,1,0:T(8,128)}), f32[32,3,2,2,16,128]{5,4,3,2,1,0:T(8,128)S(1)}, u32[]{:S(2)}, u32[]{:S(2)}) async-start(f32[32,3,2,2,16,128]{5,4,3,2,1,0:T(8,128)} %get-tuple-element.27), calls=%async_computation.3 | async-start | bytes 6291456 | tf_op jit(solution)/shard_map/all_to_all | solution.py:516
  244.5 7.9 %collective-permute-start.4 = (f32[5,32,256]{2,1,0:T(8,128)}, f32[5,32,256]{2,1,0:T(8,128)S(1)}, u32[]{:S(2)}, u32[]{:S(2)}) collective-permute-start(f32[5,32,256]{2,1,0:T(8,128)} %get-tuple-element.33), channel_id=1, source_target_pairs={{0,32},{32,64},{64,96},{96,0},{1,33},{33,65},{65,97},{97,1},{2,34}... | collective-permute-start | bytes 491528 | tf_op jit(solution)/shard_map/ppermute | solution.py:471
  246.2 9.2 %collective-permute-start.8 = (f32[5,32,256]{2,1,0:T(8,128)}, f32[5,32,256]{2,1,0:T(8,128)S(1)}, u32[]{:S(2)}, u32[]{:S(2)}) collective-permute-start(f32[5,32,256]{2,1,0:T(8,128)} %get-tuple-element.37), channel_id=1, source_target_pairs={{0,96},{32,0},{64,32},{96,64},{1,97},{33,1},{65,33},{97,65},{2,98}... | collective-permute-start | bytes 491528 | tf_op jit(solution)/shard_map/ppermute | solution.py:471
  247.9 10.2 %collective-permute-start.3 = (f32[5,32,256]{2,1,0:T(8,128)}, f32[5,32,256]{2,1,0:T(8,128)S(1)}, u32[]{:S(2)}, u32[]{:S(2)}) collective-permute-start(f32[5,32,256]{2,1,0:T(8,128)} %get-tuple-element.31), channel_id=1, source_target_pairs={{0,96},{32,0},{64,32},{96,64},{1,97},{33,1},{65,33},{97,65},{2,98}... | collective-permute-start | bytes 491528 | tf_op jit(solution)/shard_map/ppermute | solution.py:471
  253.4 8.4 %collective-permute-start.5 = (f32[5,32,256]{2,1,0:T(8,128)S(1)}, f32[5,32,256]{2,1,0:T(8,128)S(1)}, u32[]{:S(2)}, u32[]{:S(2)}) collective-permute-start(f32[5,32,256]{2,1,0:T(8,128)S(1)} %add.58), channel_id=1, source_target_pairs={{0,32},{32,64},{64,96},{96,0},{1,33},{33,65},{65,97},{97,1},{2,34}... | collective-permute-start | bytes 491528 | tf_op jit(solution)/shard_map/ppermute | solution.py:471
  253.8 10.1 %collective-permute-start.7 = (f32[5,32,256]{2,1,0:T(8,128)}, f32[5,32,256]{2,1,0:T(8,128)S(1)}, u32[]{:S(2)}, u32[]{:S(2)}) collective-permute-start(f32[5,32,256]{2,1,0:T(8,128)} %get-tuple-element.35), channel_id=1, source_target_pairs={{0,32},{32,64},{64,96},{96,0},{1,33},{33,65},{65,97},{97,1},{2,34}... | collective-permute-start | bytes 491528 | tf_op jit(solution)/shard_map/ppermute | solution.py:471
  256.3 7.5 %collective-permute-start.9 = (f32[5,32,256]{2,1,0:T(8,128)S(1)}, f32[5,32,256]{2,1,0:T(8,128)S(1)}, u32[]{:S(2)}, u32[]{:S(2)}) collective-permute-start(f32[5,32,256]{2,1,0:T(8,128)S(1)} %add.61), channel_id=1, source_target_pairs={{0,96},{32,0},{64,32},{96,64},{1,97},{33,1},{65,33},{97,65},{2,98}... | collective-permute-start | bytes 491528 | tf_op jit(solution)/shard_map/ppermute | solution.py:471
  263.5 8.1 %collective-permute-start.6 = (f32[5,32,256]{2,1,0:T(8,128)}, f32[5,32,256]{2,1,0:T(8,128)S(1)}, u32[]{:S(2)}, u32[]{:S(2)}) collective-permute-start(f32[5,32,256]{2,1,0:T(8,128)} %add_add_fusion.1.refs_0_), channel_id=1, source_target_pairs={{0,32},{32,64},{64,96},{96,0},{1,33},{33,65},{65,97},{97,1},{2,34}... | collective-permute-start | bytes 491528 | tf_op jit(solution)/shard_map/ppermute | solution.py:471
  265.5 7.3 %collective-permute-start.12 = (f32[5,32,256]{2,1,0:T(8,128)}, f32[5,32,256]{2,1,0:T(8,128)S(1)}, u32[]{:S(2)}, u32[]{:S(2)}) collective-permute-start(f32[5,32,256]{2,1,0:T(8,128)} %add_add_fusion.refs_1_), channel_id=1, source_target_pairs={{0,96},{32,0},{64,32},{96,64},{1,97},{33,1},{65,33},{97,65},{2,98}... | collective-permute-start | bytes 491528 | tf_op jit(solution)/shard_map/ppermute | solution.py:471
  268.3 8.9 %collective-permute-start.11 = (f32[5,32,256]{2,1,0:T(8,128)}, f32[5,32,256]{2,1,0:T(8,128)}, u32[]{:S(2)}, u32[]{:S(2)}) collective-permute-start(f32[5,32,256]{2,1,0:T(8,128)} %add_add_fusion.1.refs_0_), channel_id=1, source_target_pairs={{0,96},{32,0},{64,32},{96,64},{1,97},{33,1},{65,33},{97,65},{2,98}... | collective-permute-start | bytes 491528 | tf_op jit(solution)/shard_map/ppermute | solution.py:471
  268.3 8.9 %collective-permute-start.10 = (f32[5,32,256]{2,1,0:T(8,128)}, f32[5,32,256]{2,1,0:T(8,128)}, u32[]{:S(2)}, u32[]{:S(2)}) collective-permute-start(f32[5,32,256]{2,1,0:T(8,128)} %add_add_fusion.refs_1_), channel_id=1, source_target_pairs={{0,32},{32,64},{64,96},{96,0},{1,33},{33,65},{65,97},{97,1},{2,34}... | collective-permute-start | bytes 491528 | tf_op jit(solution)/shard_map/ppermute | solution.py:471
  271.5 6.7 %copy-start.3 = (f32[5,32,256]{2,1,0:T(8,128)}, f32[5,32,256]{2,1,0:T(8,128)S(1)}, u32[]{:S(2)}) copy-start(f32[5,32,256]{2,1,0:T(8,128)S(1)} %collective-permute-done.6.rest_1_.refs_2_) | copy-start | bytes 491524
  271.5 6.6 %collective-permute-start.13 = (f32[5,32,256]{2,1,0:T(8,128)S(1)}, f32[5,32,256]{2,1,0:T(8,128)}, u32[]{:S(2)}, u32[]{:S(2)}) collective-permute-start(f32[5,32,256]{2,1,0:T(8,128)S(1)} %collective-permute-done.6.rest_1_.refs_2_), channel_id=1, source_target_pairs={{0,32},{32,64},{64,96},{96,0},{1,33},{33,65},{65,97},{97,1},{2,34}... | collective-permute-start | bytes 491528 | tf_op jit(solution)/shard_map/ppermute | solution.py:471
  272.8 5.4 %copy-start.4 = (f32[5,32,256]{2,1,0:T(8,128)}, f32[5,32,256]{2,1,0:T(8,128)S(1)}, u32[]{:S(2)}) copy-start(f32[5,32,256]{2,1,0:T(8,128)S(1)} %collective-permute-done.12.rest_4_.refs_5_) | copy-start | bytes 491524
  272.8 5.4 %collective-permute-start.14 = (f32[5,32,256]{2,1,0:T(8,128)S(1)}, f32[5,32,256]{2,1,0:T(8,128)}, u32[]{:S(2)}, u32[]{:S(2)}) collective-permute-start(f32[5,32,256]{2,1,0:T(8,128)S(1)} %collective-permute-done.12.rest_4_.refs_5_), channel_id=1, source_target_pairs={{0,96},{32,0},{64,32},{96,64},{1,97},{33,1},{65,33},{97,65},{2,98}... | collective-permute-start | bytes 491528 | tf_op jit(solution)/shard_map/ppermute | solution.py:471
  277.2 1.6 copy-start.2
  285.1 9.7 %collective-permute-start.15 = (f32[3,64,256]{2,1,0:T(8,128)}, f32[3,64,256]{2,1,0:T(8,128)S(1)}, u32[]{:S(2)}, u32[]{:S(2)}) collective-permute-start(f32[3,64,256]{2,1,0:T(8,128)} %get-tuple-element.40), channel_id=1, source_target_pairs={{0,32},{32,64},{64,96},{96,0},{1,33},{33,65},{65,97},{97,1},{2,34}... | collective-permute-start | bytes 589832 | tf_op jit(solution)/shard_map/ppermute | solution.py:471
  286.7 9.8 %collective-permute-start.16 = (f32[3,64,256]{2,1,0:T(8,128)}, f32[3,64,256]{2,1,0:T(8,128)S(1)}, u32[]{:S(2)}, u32[]{:S(2)}) collective-permute-start(f32[3,64,256]{2,1,0:T(8,128)} %get-tuple-element.41), channel_id=1, source_target_pairs={{0,64},{32,96},{64,0},{96,32},{1,65},{33,97},{65,1},{97,33},{2,66}... | collective-permute-start | bytes 589832 | tf_op jit(solution)/shard_map/ppermute | solution.py:471
  289.7 6.9 %collective-permute-start.17 = (f32[3,64,256]{2,1,0:T(8,128)}, f32[3,64,256]{2,1,0:T(8,128)S(1)}, u32[]{:S(2)}, u32[]{:S(2)}) collective-permute-start(f32[3,64,256]{2,1,0:T(8,128)} %get-tuple-element.42), channel_id=1, source_target_pairs={{0,96},{32,0},{64,32},{96,64},{1,97},{33,1},{65,33},{97,65},{2,98}... | collective-permute-start | bytes 589832 | tf_op jit(solution)/shard_map/ppermute | solution.py:471
  294.8 1.8 copy-start.8
  296.6 0.7 copy-start.9
  296.6 0.8 copy-start.10
  299.3 7.7 %collective-permute-start.20 = (f32[3,64,256]{2,1,0:T(8,128)}, f32[3,64,256]{2,1,0:T(8,128)S(1)}, u32[]{:S(2)}, u32[]{:S(2)}) collective-permute-start(f32[3,64,256]{2,1,0:T(8,128)} %add.86.refs_0_), channel_id=1, source_target_pairs={{0,96},{32,0},{64,32},{96,64},{1,97},{33,1},{65,33},{97,65},{2,98}... | collective-permute-start | bytes 589832 | tf_op jit(solution)/shard_map/ppermute | solution.py:471
  301.3 7.5 %collective-permute-start.19 = (f32[3,64,256]{2,1,0:T(8,128)}, f32[3,64,256]{2,1,0:T(8,128)S(1)}, u32[]{:S(2)}, u32[]{:S(2)}) collective-permute-start(f32[3,64,256]{2,1,0:T(8,128)} %add.86.refs_0_), channel_id=1, source_target_pairs={{0,64},{32,96},{64,0},{96,32},{1,65},{33,97},{65,1},{97,33},{2,66}... | collective-permute-start | bytes 589832 | tf_op jit(solution)/shard_map/ppermute | solution.py:471
  302.4 8.3 %collective-permute-start.18 = (f32[3,64,256]{2,1,0:T(8,128)}, f32[3,64,256]{2,1,0:T(8,128)S(1)}, u32[]{:S(2)}, u32[]{:S(2)}) collective-permute-start(f32[3,64,256]{2,1,0:T(8,128)} %add.86.refs_0_), channel_id=1, source_target_pairs={{0,32},{32,64},{64,96},{96,0},{1,33},{33,65},{65,97},{97,1},{2,34}... | collective-permute-start | bytes 589832 | tf_op jit(solution)/shard_map/ppermute | solution.py:471
  307.0 3.9 %copy-start.5 = (f32[3,64,256]{2,1,0:T(8,128)}, f32[3,64,256]{2,1,0:T(8,128)S(1)}, u32[]{:S(2)}) copy-start(f32[3,64,256]{2,1,0:T(8,128)S(1)} %collective-permute-done.20.refs_3_) | copy-start | bytes 589828
  308.8 2.0 copy-start.6
  310.8 0.7 copy-start.7

commit v4 on v3

--- a/solution.py
+++ b/solution.py
@@ -442,7 +442,8 @@
 
 
 def collect_kernel(owners, band, *refs):
-    out = refs[-1]
+    out, mark = refs[-2:]
+    mark[...] = jnp.zeros_like(mark)
     rows = SIZE // BANDS
     for piece, (owner, offset) in zip(refs, owners):
         row = pl.multiple_of((band[0] + owner) % BANDS * rows, rows)
@@ -453,15 +454,21 @@
     return pl.pallas_call(
         functools.partial(collect_kernel, owners),
         grid=(pieces[0].shape[0],),
-        out_shape=jax.ShapeDtypeStruct((PLANES, SIZE, SIZE), jnp.float32),
+        out_shape=(
+            jax.ShapeDtypeStruct((PLANES, SIZE, SIZE), jnp.float32),
+            jax.ShapeDtypeStruct((8, LANES), jnp.float32),
+        ),
         in_specs=[
             pl.BlockSpec(memory_space=pltpu.SMEM),
             *[pl.BlockSpec((1, piece.shape[1], SIZE), lambda i: (i, 0, 0)) for piece in pieces],
             *[pl.BlockSpec(memory_space=pltpu.HBM) for _ in before],
         ],
-        out_specs=pl.BlockSpec((1, SIZE, SIZE), lambda i: (i + begin, 0, 0)),
+        out_specs=(
+            pl.BlockSpec((1, SIZE, SIZE), lambda i: (i + begin, 0, 0)),
+            pl.BlockSpec((8, LANES), lambda i: (0, 0)),
+        ),
         input_output_aliases={1 + len(pieces) + k: k for k in range(len(before))},
-        compiler_params=pltpu.CompilerParams(vmem_limit_bytes=VMEM),
+        compiler_params=pltpu.CompilerParams(vmem_limit_bytes=VMEM if begin == 0 else 16 << 20),
         cost_estimate=pl.CostEstimate(flops=0, bytes_accessed=3 * 10**6, transcendentals=0),
         name=f"collect{begin}",
     )(band, *pieces, *before)
@@ -502,7 +509,7 @@
             *[pl.BlockSpec(memory_space=pltpu.HBM) for _ in first],
         ],
         out_specs=pl.BlockSpec(memory_space=pltpu.VMEM),
-        compiler_params=pltpu.CompilerParams(vmem_limit_bytes=VMEM),
+        compiler_params=pltpu.CompilerParams(vmem_limit_bytes=16 << 20),
         cost_estimate=pl.CostEstimate(flops=10**6, bytes_accessed=10**6, transcendentals=0),
         name="add",
     )(*parts, *first)
@@ -544,7 +551,7 @@
 
     back = lines(0, pencils[0], left, right)
     back = lines(1, pencils[1], left, right, back, (forces,))
-    out, density, ready, begin = (), (), (), 0
+    out, density, ready, marks, begin = (), (), (), (), 0
     for k, planes in enumerate(CHUNKS):
         field = exchange(back[k])
         made, *pieces = finish(planes, begin, 2 if k == 0 else 1, band, field, potential, left, out, ready)
@@ -553,8 +560,9 @@
             sums, owners = ring_gather(*ring_reduce(pieces))
             ready = sums[2:]
         else:
-            sums, owners = direct_gather(direct_reduce(pieces, density))
-        density = (collect(begin, band, sums, owners, *density),)
+            sums, owners = direct_gather(direct_reduce(pieces, marks))
+        made, mark = collect(begin, band, sums, owners, *density)
+        density, marks = (made,), (mark,)
         begin += planes
     return out[0], density[0], forces
 

time: 316 us -> 312 us (0.987)
  Pallas kernels: 81.8 us -> 78.5 us
where the time goes in v4:
time: 312 us; the launch traced here: 311 us
  waiting for transfers between devices  102 us (33%)
  Pallas kernels  78.5 us (25%)
  blocking collectives  67.1 us (22%)
  starting transfers between devices  54.6 us (18%)
  other arithmetic  6.13 us (2%)
    all_to_all x4, waiting for transfers between devices, exchange(): lax.all_to_all(array, 'grid', split_axis=0, concat_axis=0, tiled=True)  78 us
    all_to_all x1, blocking collectives, exchange(): lax.all_to_all(array, 'grid', split_axis=0, concat_axis=0, tiled=True)  67.1 us
    ppermute x21, starting transfers between devices, onward(): lax.ppermute(array, 'band', [(b, (b + steps) % BANDS) for b in range(BAND...  31.2 us
    ppermute x21, waiting for transfers between devices, onward(): lax.ppermute(array, 'band', [(b, (b + steps) % BANDS) for b in range(BAND...  23.6 us
    all_to_all x4, starting transfers between devices, exchange(): lax.all_to_all(array, 'grid', split_axis=0, concat_axis=0, tiled=True)  23.4 us
    pallas_call x2, Pallas kernels, lines(): pl.pallas_call(functools.partial(lines_kernel, n), grid=(8 // LINES_STEP,...  17 us
    pallas_call x2, Pallas kernels, shift(): pl.pallas_call(shift_kernel, grid=(GROUPS // SHIFT_STEP,), out_shape=pltp...  16.3 us
    pallas_call x2, Pallas kernels, finish(): pl.pallas_call(functools.partial(finish_kernel, halves), grid=(planes,),...  15.4 us
  transfers between devices with their start and end apart: 25, of which 17 were waited for; matrix products, arithmetic and copies ran while one was open for 2% of the time, Pallas kernels for 14%

profile of v4, /device:TPU:0, one launch (start us, length us, event | category | flops | bytes accessed | tf_op | source)
XLA Modules:
  0.0 311.1 jit_solution(1690595480153621311)
XLA Ops:
  0.6 12.2 %project.1 = (f32[32,24,128]{2,1,0:T(8,128)}, f32[512,128]{1,0:T(8,128)}) custom-call(s32[512]{0:T(512)} %block.1, s32[512]{0:T(512)} %count.1, s32[1,512]{1,0:T(1,128)} %bitcast.12, s32[1,512]{1,0:T(1,128)} %bitcast.23, f32[4,2048,256]{2,1,0:T(8,128)} %bitcast.17, f32[2048,256]{1,0:T(8,128)} %bitcast.20, f32[4,512,128]{2,1,0:T(8,128)} %projectors_hbm.1), custom_call_target="tpu_custom_call" | custom-call | flops 1000000000 | bytes 36000000 | tf_op jit(solution)/shard_map/project/pallas_call | solution.py:214
  12.8 8.3 %all-to-all-start = ((f32[32,24,128]{2,1,0:T(8,128)}), f32[32,24,128]{2,1,0:T(8,128)S(1)}, u32[]{:S(2)}, u32[]{:S(2)}) async-start(f32[32,24,128]{2,1,0:T(8,128)} %get-tuple-element.26), calls=%async_computation | async-start | bytes 786432 | tf_op jit(solution)/shard_map/all_to_all | solution.py:523
  21.2 8.1 %shift0.1.before = f32[8192,128]{1,0:T(8,128)} custom-call(f32[2,2,8,256,256]{4,3,2,1,0:T(8,128)} %orbs.3, f32[8,256,256]{2,1,0:T(8,128)} %potential.7), custom_call_target="tpu_custom_call" | custom-call | flops 100000000 | bytes 11000000 | tf_op jit(solution)/shard_map/shift0/pallas_call | solution.py:258
  29.6 1.8 all-to-all-done.received
  31.4 6.2 %correct0.1.rest_0_ = f32[8192,128]{1,0:T(8,128)} custom-call(s32[512]{0:T(512)S(1)} %fusion.3.place, f32[32,24,128]{2,1,0:T(8,128)S(1)} %all-to-all-done.received, f32[4,128]{1,0:T(4,128)S(1)} %bitcast.15, s32[1,512]{1,0:T(1,128)S(1)} %bitcast.13, f32[512,128]{1,0:T(8,128)S(1)} %copy-done, f32[8192,128]{1,0:T(8,128)} %shift0.1.before), custom_call_target="tpu_custom_call", output_to_operand_aliasing={{}: (5, {})} | custom-call | flops 500000000 | bytes 20000000 | tf_op jit(solution)/shard_map/correct0/pallas_call | solution.py:311
  37.6 5.7 %all-to-all-start.2 = ((f32[32,256,128]{2,1,0:T(8,128)}), f32[32,256,128]{2,1,0:T(8,128)}, u32[]{:S(2)}, u32[]{:S(2)}) async-start(f32[32,256,128]{2,1,0:T(8,128)} %bitcast.18), calls=%async_computation.2 | async-start | bytes 8388608 | tf_op jit(solution)/shard_map/all_to_all | solution.py:523
  43.3 8.1 %shift1.1.before = f32[8192,128]{1,0:T(8,128)} custom-call(f32[2,2,8,256,256]{4,3,2,1,0:T(8,128)} %orbs.3, f32[8,256,256]{2,1,0:T(8,128)} %potential.7, f32[8192,128]{1,0:T(8,128)} %correct0.1.rest_0_), custom_call_target="tpu_custom_call" | custom-call | flops 100000000 | bytes 11000000 | tf_op jit(solution)/shard_map/shift1/pallas_call | solution.py:258
  51.5 6.2 %correct1.1 = f32[8192,128]{1,0:T(8,128)} custom-call(s32[512]{0:T(512)S(1)} %fusion.3.place, f32[32,24,128]{2,1,0:T(8,128)S(1)} %all-to-all-done.received, f32[4,128]{1,0:T(4,128)S(1)} %bitcast.16, s32[1,512]{1,0:T(1,128)S(1)} %bitcast.14, f32[512,128]{1,0:T(8,128)S(1)} %copy-done, f32[8192,128]{1,0:T(8,128)} %shift1.1.before), custom_call_target="tpu_custom_call", output_to_operand_aliasing={{}: (5, {})} | custom-call | flops 500000000 | bytes 20000000 | tf_op jit(solution)/shard_map/correct1/pallas_call | solution.py:311
  57.7 39.2 %all-to-all-done.2 = f32[32,256,128]{2,1,0:T(8,128)} async-done(((f32[32,256,128]{2,1,0:T(8,128)}), f32[32,256,128]{2,1,0:T(8,128)}, u32[]{:S(2)}, u32[]{:S(2)}) %all-to-all-start.2) | async-done | bytes 4194336 | tf_op jit(solution)/shard_map/all_to_all | solution.py:523
  96.8 4.9 %all-to-all-start.1 = ((f32[32,256,128]{2,1,0:T(8,128)}), f32[32,256,128]{2,1,0:T(8,128)}, u32[]{:S(2)}, u32[]{:S(2)}) async-start(f32[32,256,128]{2,1,0:T(8,128)} %bitcast.19), calls=%async_computation.1 | async-start | bytes 8388608 | tf_op jit(solution)/shard_map/all_to_all | solution.py:523
  101.9 3.3 %collective-permute-start.1 = (f32[3,16]{1,0:T(4,128)S(1)}, f32[3,16]{1,0:T(4,128)S(1)}, u32[]{:S(2)}, u32[]{:S(2)}) collective-permute-start(f32[3,16]{1,0:T(4,128)S(1)} %broadcast_multiply_fusion), channel_id=1, source_target_pairs={{0,64},{32,96},{64,0},{96,32},{1,65},{33,97},{65,1},{97,33},{2,66}... | collective-permute-start | bytes 584 | tf_op jit(solution)/shard_map/ppermute | solution.py:478
  105.2 1.1 collective-permute-start.2
  106.3 1.0 collective-permute-start
  107.2 1.6 collective-permute-done.2
  108.8 2.3 collective-permute-done
  111.6 8.5 %lines0.1 = (f32[32,5,2,2,16,128]{5,4,3,2,1,0:T(8,128)}, f32[32,3,2,2,16,128]{5,4,3,2,1,0:T(8,128)}) custom-call(f32[32,8,2,2,8,128]{5,4,3,2,1,0:T(8,128)} %bitcast.9.field, bf16[2,256,768]{2,1,0:T(8,128)(2,1)} %constant.73.clone.left, bf16[2,768,256]{2,1,0:T(8,128)(2,1)} %constant.74.clone.right), custom_call_target="tpu_custom_call" | custom-call | flops 5000000000 | bytes 10000000 | tf_op jit(solution)/shard_map/lines0/pallas_call | solution.py:370
  120.1 35.0 %all-to-all-done.1 = f32[32,256,128]{2,1,0:T(8,128)} async-done(((f32[32,256,128]{2,1,0:T(8,128)}), f32[32,256,128]{2,1,0:T(8,128)}, u32[]{:S(2)}, u32[]{:S(2)}) %all-to-all-start.1) | async-done | bytes 4194336 | tf_op jit(solution)/shard_map/all_to_all | solution.py:523
  155.2 8.5 %lines1.1 = (f32[32,5,2,2,16,128]{5,4,3,2,1,0:T(8,128)}, f32[32,3,2,2,16,128]{5,4,3,2,1,0:T(8,128)}) custom-call(f32[32,8,2,2,8,128]{5,4,3,2,1,0:T(8,128)} %bitcast.7.field, bf16[2,256,768]{2,1,0:T(8,128)(2,1)} %constant.73.clone.left, bf16[2,768,256]{2,1,0:T(8,128)(2,1)} %constant.74.clone.right, ...), custom_call_target="tpu_custom_call", output_to_operand_aliasing={{0}: (3, {}), {1}: (4, {})} | custom-call | flops 5000000000 | bytes 10000000 | tf_op jit(solution)/shard_map/lines1/pallas_call | solution.py:370
  163.7 67.1 %all_to_all.25 = f32[32,5,2,2,16,128]{5,4,3,2,1,0:T(8,128)} all-to-all(f32[32,5,2,2,16,128]{5,4,3,2,1,0:T(8,128)} %get-tuple-element.31), channel_id=1, replica_groups=mesh['band'=4,'grid'=32] {'grid'}, dimensions={0} | all-to-all | bytes 10485760 | tf_op jit(solution)/shard_map/all_to_all | solution.py:523
  230.8 4.6 %all-to-all-start.3 = ((f32[32,3,2,2,16,128]{5,4,3,2,1,0:T(8,128)}), f32[32,3,2,2,16,128]{5,4,3,2,1,0:T(8,128)S(1)}, u32[]{:S(2)}, u32[]{:S(2)}) async-start(f32[32,3,2,2,16,128]{5,4,3,2,1,0:T(8,128)} %get-tuple-element.30), calls=%async_computation.3 | async-start | bytes 6291456 | tf_op jit(solution)/shard_map/all_to_all | solution.py:523
  235.4 9.1 %finish0.1 = (f32[2,2,8,256,256]{4,3,2,1,0:T(8,128)}, f32[5,32,256]{2,1,0:T(8,128)}, f32[5,32,256]{2,1,0:T(8,128)}, f32[5,32,256]{2,1,0:T(8,128)}, f32[5,32,256]...) custom-call(s32[1]{0:T(128)} %bitcast.band, ...), custom_call_target="tpu_custom_call" | custom-call | flops 5000000000 | bytes 15000000 | tf_op jit(solution)/shard_map/finish0/pallas_call | solution.py:418
  244.5 1.6 collective-permute-start.4
  246.2 1.7 collective-permute-start.8
  247.8 1.8 collective-permute-start.3
  249.6 2.8 collective-permute-done.4
  253.8 1.6 collective-permute-start.7
  256.3 1.7 collective-permute-start.9
  258.0 3.8 %collective-permute-done.5 = f32[5,32,256]{2,1,0:T(8,128)S(1)} collective-permute-done((f32[5,32,256]{2,1,0:T(8,128)S(1)}, f32[5,32,256]{2,1,0:T(8,128)S(1)}, u32[]{:S(2)}, u32[]{:S(2)}) %collective-permute-start.5) | collective-permute-done | bytes 163872 | tf_op jit(solution)/shard_map/ppermute | solution.py:478
  261.8 1.6 add_add_fusion.1.refs_0_
  263.9 1.6 add_add_fusion.refs_1_
  265.5 2.8 collective-permute-start.12
  268.3 2.0 collective-permute-start.10
  270.3 1.2 collective-permute-done.6.rest_1_.refs_2_
  271.5 1.3 collective-permute-done.12.rest_4_.refs_5_
  272.8 2.3 collective-permute-start.14
  275.2 2.0 all-to-all-done.3
  278.8 6.3 %finish5.1 = (f32[2,2,8,256,256]{4,3,2,1,0:T(8,128)}, f32[3,64,256]{2,1,0:T(8,128)}, f32[3,64,256]{2,1,0:T(8,128)}, f32[3,64,256]{2,1,0:T(8,128)}, f32[3,64,256]{2,1,0:T(8,128)}) custom-call(s32[1]{0:T(128)} %bitcast.band, f32[32,3,2,2,2,8,128]{6,5,4,3,2,1,0:T(8,128)} %bitcast.21, f32[8,256,256]{2,1,0:T(8,128)} %potential.7, ...), custom_call_target="tpu_custom_call", output_to_operand_aliasing={{0}: (4, {})} | custom-call | flops 3000000000 | bytes 9000000 | tf_op jit(solution)/shard_map/finish5/pallas_call | solution.py:418
  285.1 1.6 collective-permute-start.15
  286.7 2.9 collective-permute-start.16
  289.7 1.3 collective-permute-start.17
  291.0 3.8 %collect0.1 = (f32[8,256,256]{2,1,0:T(8,128)}, f32[8,128]{1,0:T(8,128)}) custom-call(s32[1]{0:T(128)} %bitcast.band, f32[5,32,256]{2,1,0:T(8,128)} %add_add_fusion.1.refs_0_, f32[5,32,256]{2,1,0:T(8,128)} %add_add_fusion.refs_1_, f32[5,32,256]{2,1,0:T(8,128)} %copy-done.5, f32[5,32,256]{2,1,0:T(8,128)} %collective-permute-done.10.rest_2_.refs_3_, ...), custom_call_target="tpu_custom_call" | custom-call | bytes 3000000 | tf_op jit(solution)/shard_map/collect0/pallas_call | solution.py:454
  294.8 1.8 collective-permute-done.16.across
  298.2 2.2 collective-permute-start.20
  300.4 1.1 collective-permute-start.19
  302.3 3.4 %collective-permute-done.20.refs_3_ = f32[3,64,256]{2,1,0:T(8,128)S(1)} collective-permute-done((f32[3,64,256]{2,1,0:T(8,128)S(1)}, f32[3,64,256]{2,1,0:T(8,128)S(1)}, u32[]{:S(2)}, u32[]{:S(2)}) %collective-permute-start.20) | collective-permute-done | bytes 196640 | tf_op jit(solution)/shard_map/ppermute | solution.py:478
  305.7 1.9 collective-permute-done.19.refs_2_
  307.7 2.0 collective-permute-done.18.refs_1_
  309.7 1.5 collect5.1
  (50 shorter events, 7.8 us)
Async XLA Ops:
  12.8 18.6 %all-to-all-start = ((f32[32,24,128]{2,1,0:T(8,128)}), f32[32,24,128]{2,1,0:T(8,128)S(1)}, u32[]{:S(2)}, u32[]{:S(2)}) async-start(f32[32,24,128]{2,1,0:T(8,128)} %get-tuple-element.26), calls=%async_computation | async-start | bytes 786432 | tf_op jit(solution)/shard_map/all_to_all | solution.py:523
  21.1 8.2 %copy-start.7 = (s32[512]{0:T(512)S(1)}, s32[512]{0:T(512)}, u32[]{:S(2)}) copy-start(s32[512]{0:T(512)} %param.16) | copy-start | bytes 6148
  21.1 8.2 %copy-start.9 = (f32[512]{0:T(512)S(1)}, f32[512]{0:T(512)}, u32[]{:S(2)}) copy-start(f32[512]{0:T(512)} %param.17) | copy-start | bytes 6148
  21.1 8.4 %copy-start.8 = (s32[512]{0:T(512)S(1)}, s32[512]{0:T(512)}, u32[]{:S(2)}) copy-start(s32[512]{0:T(512)} %block.1) | copy-start | bytes 6148
  21.1 10.3 %copy-start = (f32[512,128]{1,0:T(8,128)S(1)}, f32[512,128]{1,0:T(8,128)}, u32[]{:S(2)}) copy-start(f32[512,128]{1,0:T(8,128)} %get-tuple-element.27.masked) | copy-start | bytes 786436
  21.1 10.3 %copy-start.2 = (s32[512]{0:T(512)S(1)}, s32[512]{0:T(512)}, u32[]{:S(2)}) copy-start(s32[512]{0:T(512)} %param.13) | copy-start | bytes 6148
  37.6 59.2 %all-to-all-start.2 = ((f32[32,256,128]{2,1,0:T(8,128)}), f32[32,256,128]{2,1,0:T(8,128)}, u32[]{:S(2)}, u32[]{:S(2)}) async-start(f32[32,256,128]{2,1,0:T(8,128)} %bitcast.18), calls=%async_computation.2 | async-start | bytes 8388608 | tf_op jit(solution)/shard_map/all_to_all | solution.py:523
  96.8 58.3 %all-to-all-start.1 = ((f32[32,256,128]{2,1,0:T(8,128)}), f32[32,256,128]{2,1,0:T(8,128)}, u32[]{:S(2)}, u32[]{:S(2)}) async-start(f32[32,256,128]{2,1,0:T(8,128)} %bitcast.19), calls=%async_computation.1 | async-start | bytes 8388608 | tf_op jit(solution)/shard_map/all_to_all | solution.py:523
  101.9 5.3 %collective-permute-start.1 = (f32[3,16]{1,0:T(4,128)S(1)}, f32[3,16]{1,0:T(4,128)S(1)}, u32[]{:S(2)}, u32[]{:S(2)}) collective-permute-start(f32[3,16]{1,0:T(4,128)S(1)} %broadcast_multiply_fusion), channel_id=1, source_target_pairs={{0,64},{32,96},{64,0},{96,32},{1,65},{33,97},{65,1},{97,33},{2,66}... | collective-permute-start | bytes 584 | tf_op jit(solution)/shard_map/ppermute | solution.py:478
  105.2 3.6 %collective-permute-start.2 = (f32[3,16]{1,0:T(4,128)S(1)}, f32[3,16]{1,0:T(4,128)S(1)}, u32[]{:S(2)}, u32[]{:S(2)}) collective-permute-start(f32[3,16]{1,0:T(4,128)S(1)} %broadcast_multiply_fusion), channel_id=1, source_target_pairs={{0,96},{32,0},{64,32},{96,64},{1,97},{33,1},{65,33},{97,65},{2,98}... | collective-permute-start | bytes 584 | tf_op jit(solution)/shard_map/ppermute | solution.py:478
  106.3 4.8 %collective-permute-start = (f32[3,16]{1,0:T(4,128)S(1)}, f32[3,16]{1,0:T(4,128)S(1)}, u32[]{:S(2)}, u32[]{:S(2)}) collective-permute-start(f32[3,16]{1,0:T(4,128)S(1)} %broadcast_multiply_fusion), channel_id=1, source_target_pairs={{0,32},{32,64},{64,96},{96,0},{1,33},{33,65},{65,97},{97,1},{2,34}... | collective-permute-start | bytes 584 | tf_op jit(solution)/shard_map/ppermute | solution.py:478
  230.8 46.4 %all-to-all-start.3 = ((f32[32,3,2,2,16,128]{5,4,3,2,1,0:T(8,128)}), f32[32,3,2,2,16,128]{5,4,3,2,1,0:T(8,128)S(1)}, u32[]{:S(2)}, u32[]{:S(2)}) async-start(f32[32,3,2,2,16,128]{5,4,3,2,1,0:T(8,128)} %get-tuple-element.30), calls=%async_computation.3 | async-start | bytes 6291456 | tf_op jit(solution)/shard_map/all_to_all | solution.py:523
  244.5 7.9 %collective-permute-start.4 = (f32[5,32,256]{2,1,0:T(8,128)}, f32[5,32,256]{2,1,0:T(8,128)S(1)}, u32[]{:S(2)}, u32[]{:S(2)}) collective-permute-start(f32[5,32,256]{2,1,0:T(8,128)} %get-tuple-element.36), channel_id=1, source_target_pairs={{0,32},{32,64},{64,96},{96,0},{1,33},{33,65},{65,97},{97,1},{2,34}... | collective-permute-start | bytes 491528 | tf_op jit(solution)/shard_map/ppermute | solution.py:478
  246.2 9.2 %collective-permute-start.8 = (f32[5,32,256]{2,1,0:T(8,128)}, f32[5,32,256]{2,1,0:T(8,128)S(1)}, u32[]{:S(2)}, u32[]{:S(2)}) collective-permute-start(f32[5,32,256]{2,1,0:T(8,128)} %get-tuple-element.40), channel_id=1, source_target_pairs={{0,96},{32,0},{64,32},{96,64},{1,97},{33,1},{65,33},{97,65},{2,98}... | collective-permute-start | bytes 491528 | tf_op jit(solution)/shard_map/ppermute | solution.py:478
  247.8 10.2 %collective-permute-start.3 = (f32[5,32,256]{2,1,0:T(8,128)}, f32[5,32,256]{2,1,0:T(8,128)S(1)}, u32[]{:S(2)}, u32[]{:S(2)}) collective-permute-start(f32[5,32,256]{2,1,0:T(8,128)} %get-tuple-element.34), channel_id=1, source_target_pairs={{0,96},{32,0},{64,32},{96,64},{1,97},{33,1},{65,33},{97,65},{2,98}... | collective-permute-start | bytes 491528 | tf_op jit(solution)/shard_map/ppermute | solution.py:478
  253.4 8.4 %collective-permute-start.5 = (f32[5,32,256]{2,1,0:T(8,128)S(1)}, f32[5,32,256]{2,1,0:T(8,128)S(1)}, u32[]{:S(2)}, u32[]{:S(2)}) collective-permute-start(f32[5,32,256]{2,1,0:T(8,128)S(1)} %add.58), channel_id=1, source_target_pairs={{0,32},{32,64},{64,96},{96,0},{1,33},{33,65},{65,97},{97,1},{2,34}... | collective-permute-start | bytes 491528 | tf_op jit(solution)/shard_map/ppermute | solution.py:478
  253.8 10.1 %collective-permute-start.7 = (f32[5,32,256]{2,1,0:T(8,128)}, f32[5,32,256]{2,1,0:T(8,128)S(1)}, u32[]{:S(2)}, u32[]{:S(2)}) collective-permute-start(f32[5,32,256]{2,1,0:T(8,128)} %get-tuple-element.38), channel_id=1, source_target_pairs={{0,32},{32,64},{64,96},{96,0},{1,33},{33,65},{65,97},{97,1},{2,34}... | collective-permute-start | bytes 491528 | tf_op jit(solution)/shard_map/ppermute | solution.py:478
  256.3 7.5 %collective-permute-start.9 = (f32[5,32,256]{2,1,0:T(8,128)S(1)}, f32[5,32,256]{2,1,0:T(8,128)S(1)}, u32[]{:S(2)}, u32[]{:S(2)}) collective-permute-start(f32[5,32,256]{2,1,0:T(8,128)S(1)} %add.61), channel_id=1, source_target_pairs={{0,96},{32,0},{64,32},{96,64},{1,97},{33,1},{65,33},{97,65},{2,98}... | collective-permute-start | bytes 491528 | tf_op jit(solution)/shard_map/ppermute | solution.py:478
  263.4 8.1 %collective-permute-start.6 = (f32[5,32,256]{2,1,0:T(8,128)}, f32[5,32,256]{2,1,0:T(8,128)S(1)}, u32[]{:S(2)}, u32[]{:S(2)}) collective-permute-start(f32[5,32,256]{2,1,0:T(8,128)} %add_add_fusion.1.refs_0_), channel_id=1, source_target_pairs={{0,32},{32,64},{64,96},{96,0},{1,33},{33,65},{65,97},{97,1},{2,34}... | collective-permute-start | bytes 491528 | tf_op jit(solution)/shard_map/ppermute | solution.py:478
  265.5 7.3 %collective-permute-start.12 = (f32[5,32,256]{2,1,0:T(8,128)}, f32[5,32,256]{2,1,0:T(8,128)S(1)}, u32[]{:S(2)}, u32[]{:S(2)}) collective-permute-start(f32[5,32,256]{2,1,0:T(8,128)} %add_add_fusion.refs_1_), channel_id=1, source_target_pairs={{0,96},{32,0},{64,32},{96,64},{1,97},{33,1},{65,33},{97,65},{2,98}... | collective-permute-start | bytes 491528 | tf_op jit(solution)/shard_map/ppermute | solution.py:478
  268.3 8.9 %collective-permute-start.11 = (f32[5,32,256]{2,1,0:T(8,128)}, f32[5,32,256]{2,1,0:T(8,128)}, u32[]{:S(2)}, u32[]{:S(2)}) collective-permute-start(f32[5,32,256]{2,1,0:T(8,128)} %add_add_fusion.1.refs_0_), channel_id=1, source_target_pairs={{0,96},{32,0},{64,32},{96,64},{1,97},{33,1},{65,33},{97,65},{2,98}... | collective-permute-start | bytes 491528 | tf_op jit(solution)/shard_map/ppermute | solution.py:478
  268.3 8.8 %collective-permute-start.10 = (f32[5,32,256]{2,1,0:T(8,128)}, f32[5,32,256]{2,1,0:T(8,128)}, u32[]{:S(2)}, u32[]{:S(2)}) collective-permute-start(f32[5,32,256]{2,1,0:T(8,128)} %add_add_fusion.refs_1_), channel_id=1, source_target_pairs={{0,32},{32,64},{64,96},{96,0},{1,33},{33,65},{65,97},{97,1},{2,34}... | collective-permute-start | bytes 491528 | tf_op jit(solution)/shard_map/ppermute | solution.py:478
  271.5 6.8 %copy-start.5 = (f32[5,32,256]{2,1,0:T(8,128)}, f32[5,32,256]{2,1,0:T(8,128)S(1)}, u32[]{:S(2)}) copy-start(f32[5,32,256]{2,1,0:T(8,128)S(1)} %collective-permute-done.6.rest_1_.refs_2_) | copy-start | bytes 491524
  271.5 6.6 %collective-permute-start.13 = (f32[5,32,256]{2,1,0:T(8,128)S(1)}, f32[5,32,256]{2,1,0:T(8,128)}, u32[]{:S(2)}, u32[]{:S(2)}) collective-permute-start(f32[5,32,256]{2,1,0:T(8,128)S(1)} %collective-permute-done.6.rest_1_.refs_2_), channel_id=1, source_target_pairs={{0,32},{32,64},{64,96},{96,0},{1,33},{33,65},{65,97},{97,1},{2,34}... | collective-permute-start | bytes 491528 | tf_op jit(solution)/shard_map/ppermute | solution.py:478
  272.8 5.4 %copy-start.6 = (f32[5,32,256]{2,1,0:T(8,128)}, f32[5,32,256]{2,1,0:T(8,128)S(1)}, u32[]{:S(2)}) copy-start(f32[5,32,256]{2,1,0:T(8,128)S(1)} %collective-permute-done.12.rest_4_.refs_5_) | copy-start | bytes 491524
  272.8 5.4 %collective-permute-start.14 = (f32[5,32,256]{2,1,0:T(8,128)S(1)}, f32[5,32,256]{2,1,0:T(8,128)}, u32[]{:S(2)}, u32[]{:S(2)}) collective-permute-start(f32[5,32,256]{2,1,0:T(8,128)S(1)} %collective-permute-done.12.rest_4_.refs_5_), channel_id=1, source_target_pairs={{0,96},{32,0},{64,32},{96,64},{1,97},{33,1},{65,33},{97,65},{2,98}... | collective-permute-start | bytes 491528 | tf_op jit(solution)/shard_map/ppermute | solution.py:478
  277.2 1.6 copy-start.4
  285.1 9.6 %collective-permute-start.15 = (f32[3,64,256]{2,1,0:T(8,128)}, f32[3,64,256]{2,1,0:T(8,128)S(1)}, u32[]{:S(2)}, u32[]{:S(2)}) collective-permute-start(f32[3,64,256]{2,1,0:T(8,128)} %get-tuple-element.43), channel_id=1, source_target_pairs={{0,32},{32,64},{64,96},{96,0},{1,33},{33,65},{65,97},{97,1},{2,34}... | collective-permute-start | bytes 589832 | tf_op jit(solution)/shard_map/ppermute | solution.py:478
  286.7 9.8 %collective-permute-start.16 = (f32[3,64,256]{2,1,0:T(8,128)}, f32[3,64,256]{2,1,0:T(8,128)S(1)}, u32[]{:S(2)}, u32[]{:S(2)}) collective-permute-start(f32[3,64,256]{2,1,0:T(8,128)} %get-tuple-element.44), channel_id=1, source_target_pairs={{0,64},{32,96},{64,0},{96,32},{1,65},{33,97},{65,1},{97,33},{2,66}... | collective-permute-start | bytes 589832 | tf_op jit(solution)/shard_map/ppermute | solution.py:478
  289.7 6.9 %collective-permute-start.17 = (f32[3,64,256]{2,1,0:T(8,128)}, f32[3,64,256]{2,1,0:T(8,128)S(1)}, u32[]{:S(2)}, u32[]{:S(2)}) collective-permute-start(f32[3,64,256]{2,1,0:T(8,128)} %get-tuple-element.45), channel_id=1, source_target_pairs={{0,96},{32,0},{64,32},{96,64},{1,97},{33,1},{65,33},{97,65},{2,98}... | collective-permute-start | bytes 589832 | tf_op jit(solution)/shard_map/ppermute | solution.py:478
  296.6 0.9 copy-start.1
  297.5 0.7 copy-start.3
  298.2 7.5 %collective-permute-start.20 = (f32[3,64,256]{2,1,0:T(8,128)S(1)}, f32[3,64,256]{2,1,0:T(8,128)S(1)}, u32[]{:S(2)}, u32[]{:S(2)}) collective-permute-start(f32[3,64,256]{2,1,0:T(8,128)S(1)} %add.86.refs_0_), channel_id=1, source_target_pairs={{0,96},{32,0},{64,32},{96,64},{1,97},{33,1},{65,33},{97,65},{2,98}... | collective-permute-start | bytes 589832 | tf_op jit(solution)/shard_map/ppermute | solution.py:478
  300.4 7.3 %collective-permute-start.19 = (f32[3,64,256]{2,1,0:T(8,128)S(1)}, f32[3,64,256]{2,1,0:T(8,128)S(1)}, u32[]{:S(2)}, u32[]{:S(2)}) collective-permute-start(f32[3,64,256]{2,1,0:T(8,128)S(1)} %add.86.refs_0_), channel_id=1, source_target_pairs={{0,64},{32,96},{64,0},{96,32},{1,65},{33,97},{65,1},{97,33},{2,66}... | collective-permute-start | bytes 589832 | tf_op jit(solution)/shard_map/ppermute | solution.py:478
  301.5 8.1 %collective-permute-start.18 = (f32[3,64,256]{2,1,0:T(8,128)S(1)}, f32[3,64,256]{2,1,0:T(8,128)S(1)}, u32[]{:S(2)}, u32[]{:S(2)}) collective-permute-start(f32[3,64,256]{2,1,0:T(8,128)S(1)} %add.86.refs_0_), channel_id=1, source_target_pairs={{0,32},{32,64},{64,96},{96,0},{1,33},{33,65},{65,97},{97,1},{2,34}... | collective-permute-start | bytes 589832 | tf_op jit(solution)/shard_map/ppermute | solution.py:478

commit v5 on v4

--- a/solution.py
+++ b/solution.py
@@ -16,6 +16,7 @@
 TIME_STEP = 4.0
 HIGHEST = lax.Precision.HIGHEST
 ORBS = 2
+EARLY = (1,)
 BANDS = 4
 PLANES = 8
 GROUPS = 32
@@ -271,7 +272,7 @@
     )(orbitals, potential, *first)
 
 
-def correct_kernel(n, place, received, strength, atom_ref, masked, before, after, field, coefs, updates, sems):
+def correct_kernel(n, place, received, strength, atom_ref, masked, right, before, after, field, coefs, updates, sems):
     load = pltpu.make_async_copy(before, field, sems.at[0])
     load.start()
     sums = jnp.sum(received[:, 0:16, :], axis=0)
@@ -299,19 +300,32 @@
         return carry
 
     lax.fori_loop(0, ENTRIES, step, 0, unroll=8)
+    if n in EARLY:
+        tiles = field.reshape(GROUPS * 8, 2, 2, 8, LANES)
+
+        def z_lines(index, carry):
+            at = pl.ds(index * 32, 32)
+            real, imag = ([tiles[at, c, z].reshape(SIZE, LANES) for z in range(2)] for c in range(2))
+            both = propagate_lanes(right, real, imag)
+            for c in range(2):
+                for z in range(2):
+                    tiles[at, c, z] = both[c][:, z * LANES : (z + 1) * LANES].reshape(32, 8, LANES)
+            return carry
+
+        lax.fori_loop(0, GROUPS * 8 // 32, z_lines, 0)
     store = pltpu.make_async_copy(field, after, sems.at[1])
     store.start()
     store.wait()
 
 
-def correct(n, place, received, strength, atoms, masked, before):
+def correct(n, place, received, strength, atoms, masked, right, before):
     smem = pl.BlockSpec(memory_space=pltpu.SMEM)
     vmem = pl.BlockSpec(memory_space=pltpu.VMEM)
     hbm = pl.BlockSpec(memory_space=pltpu.HBM)
     return pl.pallas_call(
         functools.partial(correct_kernel, n),
         out_shape=pltpu.HBM((GROUPS * 256, LANES), jnp.float32),
-        in_specs=[smem, vmem, vmem, vmem, vmem, hbm],
+        in_specs=[smem, vmem, vmem, vmem, vmem, vmem, hbm],
         out_specs=hbm,
         scratch_shapes=[
             pltpu.VMEM((GROUPS * 256, LANES), jnp.float32),
@@ -319,11 +333,11 @@
             pltpu.VMEM((2, ENTRIES, LANES), jnp.float32),
             pltpu.SemaphoreType.DMA((2,)),
         ],
-        input_output_aliases={5: 0},
+        input_output_aliases={6: 0},
         compiler_params=pltpu.CompilerParams(vmem_limit_bytes=24 << 20),
         cost_estimate=pl.CostEstimate(flops=5 * 10**8, bytes_accessed=20 * 10**6, transcendentals=0),
         name=f"correct{n}",
-    )(place, received, strength, atoms, masked, before)
+    )(place, received, strength, atoms, masked, right if n in EARLY else right[:, :8, :LANES], before)
 
 
 LINES_STEP = 4
@@ -332,37 +346,57 @@
 def lines_kernel(n, field, left, right, *rest):
     *chunks, half_done, turned, sems = rest[-3 - len(CHUNKS) :]
     step = pl.program_id(0)
-    for k in range(LINES_STEP):
-        real, imag = ([field[:, k, c, z].reshape(SIZE, LANES) for z in range(2)] for c in range(2))
-        both = propagate_lanes(right, real, imag)
-        y = step * LINES_STEP + k
+    last = step == pl.num_programs(0) - 1
+    rows = turned.reshape(GROUPS, 2, PLANES * 16, LANES)
+
+    def x_lines(z, y, real, imag):
+        both = propagate_rows(left, jnp.concatenate(real, axis=1), jnp.concatenate(imag, axis=1))
         for c in range(2):
+            for k in range(2):
+                for d in range(GROUPS):
+                    tile = both[c][d * 8 : d * 8 + 8, k * LANES : (k + 1) * LANES]
+                    rows[d, z, pl.ds(c * 8 + y + k, 8, stride=16), :] = tile
+
+    def copies(z):
+        begin = 0
+        for k, (chunk, planes) in enumerate(zip(chunks, CHUNKS)):
+            part = turned.at[:, z, pl.ds(begin, planes)]
+            yield pltpu.make_async_copy(part, chunk.at[:, :, n, z], sems.at[z, k])
+            begin += planes
+
+    if n in EARLY:
+        for z in range(2):
+            for k in range(0, LINES_STEP, 2):
+                parts = ([field[:, k + j, c, z].reshape(SIZE, LANES) for j in range(2)] for c in range(2))
+                x_lines(z, step * LINES_STEP + k, *parts)
+
+            @pl.when(last)
+            def _():
+                for copy in copies(z):
+                    copy.start()
+
+    else:
+        for k in range(LINES_STEP):
+            real, imag = ([field[:, k, c, z].reshape(SIZE, LANES) for z in range(2)] for c in range(2))
+            both = propagate_lanes(right, real, imag)
+            y = step * LINES_STEP + k
+            for c in range(2):
+                for z in range(2):
+                    half_done[c, z, y] = both[c][:, z * LANES : (z + 1) * LANES]
+
+        @pl.when(last)
+        def _():
             for z in range(2):
-                half_done[c, z, y] = both[c][:, z * LANES : (z + 1) * LANES]
-
-    @pl.when(step == pl.num_programs(0) - 1)
+                for y in range(0, 8, 2):
+                    x_lines(z, y, *([half_done[c, z, y + j] for j in range(2)] for c in range(2)))
+                for copy in copies(z):
+                    copy.start()
+
+    @pl.when(last)
     def _():
-        rows = turned.reshape(GROUPS, 2, PLANES * 16, LANES)
-        copies = []
         for z in range(2):
-            for y in range(0, 8, 2):
-                real, imag = (
-                    jnp.concatenate([half_done[c, z, y], half_done[c, z, y + 1]], axis=1) for c in range(2)
-                )
-                both = propagate_rows(left, real, imag)
-                for c in range(2):
-                    for k in range(2):
-                        for d in range(GROUPS):
-                            tile = both[c][d * 8 : d * 8 + 8, k * LANES : (k + 1) * LANES]
-                            rows[d, z, pl.ds(c * 8 + y + k, 8, stride=16), :] = tile
-            begin = 0
-            for k, (chunk, planes) in enumerate(zip(chunks, CHUNKS)):
-                part = turned.at[:, z, pl.ds(begin, planes)]
-                copies.append(pltpu.make_async_copy(part, chunk.at[:, :, n, z], sems.at[z, k]))
-                copies[-1].start()
-                begin += planes
-        for copy in copies:
-            copy.wait()
+            for copy in copies(z):
+                copy.wait()
 
 
 def lines(n, field, left, right, before=(), first=()):
@@ -540,7 +574,7 @@
     pencils, sent = [], ()
     for n in range(ORBS):
         shifted = shift(n, orbitals, potential, *sent)
-        fixed = correct(n, place, received, strength_atom, atoms, masked, shifted)
+        fixed = correct(n, place, received, strength_atom, atoms, masked, right, shifted)
         pencils.append(exchange(fixed.reshape(GROUPS, 256, LANES)))
         sent = (fixed,)
     mine = jnp.sum(received[:, 16:], axis=0)

time: 312 us -> 311 us (level)
  waiting for transfers between devices: 102 us -> 98.4 us
    all_to_all x4, waiting for transfers between devices: 78 us -> 74.8 us  [exchange(): lax.all_to_all(array, 'grid', split_axis=0, concat_axis=0, tiled=True)]
  transfers between devices with their start and end apart: 25 -> 25, of which waited for: 17 -> 17; matrix products, arithmetic and copies ran while one was open for 2% -> 2% of each run, Pallas kernels for 14% -> 15%
where the time goes in v5:
time: 311 us; the launch traced here: 310 us
  waiting for transfers between devices  98.4 us (32%)
  Pallas kernels  80.2 us (26%)
  blocking collectives  67.1 us (22%)
  starting transfers between devices  54.7 us (18%)
  other arithmetic  6.12 us (2%)
    all_to_all x4, waiting for transfers between devices, exchange(): lax.all_to_all(array, 'grid', split_axis=0, concat_axis=0, tiled=True)  74.8 us
    all_to_all x1, blocking collectives, exchange(): lax.all_to_all(array, 'grid', split_axis=0, concat_axis=0, tiled=True)  67.1 us
    ppermute x21, starting transfers between devices, onward(): lax.ppermute(array, 'band', [(b, (b + steps) % BANDS) for b in range(BAND...  31.2 us
    ppermute x21, waiting for transfers between devices, onward(): lax.ppermute(array, 'band', [(b, (b + steps) % BANDS) for b in range(BAND...  23.5 us
    all_to_all x4, starting transfers between devices, exchange(): lax.all_to_all(array, 'grid', split_axis=0, concat_axis=0, tiled=True)  23.4 us
    pallas_call x2, Pallas kernels, shift(): pl.pallas_call(shift_kernel, grid=(GROUPS // SHIFT_STEP,), out_shape=pltp...  16.3 us
    pallas_call x2, Pallas kernels, lines(): pl.pallas_call(functools.partial(lines_kernel, n), grid=(8 // LINES_STEP,...  15.5 us
    pallas_call x2, Pallas kernels, correct(): pl.pallas_call(functools.partial(correct_kernel, n), out_shape=pltpu.HBM(...  15.5 us
  transfers between devices with their start and end apart: 25, of which 17 were waited for; matrix products, arithmetic and copies ran while one was open for 2% of the time, Pallas kernels for 15%

profile of v5, /device:TPU:0, one launch (start us, length us, event | category | flops | bytes accessed | tf_op | source)
XLA Modules:
  0.0 309.6 jit_solution(737360363387240246)
XLA Ops:
  0.6 12.2 %project.1 = (f32[32,24,128]{2,1,0:T(8,128)}, f32[512,128]{1,0:T(8,128)}) custom-call(s32[512]{0:T(512)} %block.1, s32[512]{0:T(512)} %count.1, s32[1,512]{1,0:T(1,128)} %bitcast.12, s32[1,512]{1,0:T(1,128)} %bitcast.23, f32[4,2048,256]{2,1,0:T(8,128)} %bitcast.17, f32[2048,256]{1,0:T(8,128)} %bitcast.20, f32[4,512,128]{2,1,0:T(8,128)} %projectors_hbm.1), custom_call_target="tpu_custom_call" | custom-call | flops 1000000000 | bytes 36000000 | tf_op jit(solution)/shard_map/project/pallas_call | solution.py:215
  12.8 8.3 %all-to-all-start = ((f32[32,24,128]{2,1,0:T(8,128)}), f32[32,24,128]{2,1,0:T(8,128)S(1)}, u32[]{:S(2)}, u32[]{:S(2)}) async-start(f32[32,24,128]{2,1,0:T(8,128)} %get-tuple-element.26), calls=%async_computation | async-start | bytes 786432 | tf_op jit(solution)/shard_map/all_to_all | solution.py:557
  21.2 8.1 %shift0.1.before = f32[8192,128]{1,0:T(8,128)} custom-call(f32[2,2,8,256,256]{4,3,2,1,0:T(8,128)} %orbs.3, f32[8,256,256]{2,1,0:T(8,128)} %potential.7), custom_call_target="tpu_custom_call" | custom-call | flops 100000000 | bytes 11000000 | tf_op jit(solution)/shard_map/shift0/pallas_call | solution.py:259
  29.6 1.8 all-to-all-done.received
  31.4 6.2 %correct0.1.rest_0_ = f32[8192,128]{1,0:T(8,128)} custom-call(s32[512]{0:T(512)S(1)} %fusion.3.place, f32[32,24,128]{2,1,0:T(8,128)S(1)} %all-to-all-done.received, f32[4,128]{1,0:T(4,128)S(1)} %bitcast.15, s32[1,512]{1,0:T(1,128)S(1)} %bitcast.13, f32[512,128]{1,0:T(8,128)S(1)} %copy-done, ...), custom_call_target="tpu_custom_call", output_to_operand_aliasing={{}: (6, {})} | custom-call | flops 500000000 | bytes 20000000 | tf_op jit(solution)/shard_map/correct0/pallas_call | solution.py:325
  37.6 5.7 %all-to-all-start.2 = ((f32[32,256,128]{2,1,0:T(8,128)}), f32[32,256,128]{2,1,0:T(8,128)}, u32[]{:S(2)}, u32[]{:S(2)}) async-start(f32[32,256,128]{2,1,0:T(8,128)} %bitcast.18), calls=%async_computation.2 | async-start | bytes 8388608 | tf_op jit(solution)/shard_map/all_to_all | solution.py:557
  43.4 8.2 %shift1.1.before = f32[8192,128]{1,0:T(8,128)} custom-call(f32[2,2,8,256,256]{4,3,2,1,0:T(8,128)} %orbs.3, f32[8,256,256]{2,1,0:T(8,128)} %potential.7, f32[8192,128]{1,0:T(8,128)} %correct0.1.rest_0_), custom_call_target="tpu_custom_call" | custom-call | flops 100000000 | bytes 11000000 | tf_op jit(solution)/shard_map/shift1/pallas_call | solution.py:259
  51.6 9.3 %correct1.1 = f32[8192,128]{1,0:T(8,128)} custom-call(s32[512]{0:T(512)S(1)} %fusion.3.place, f32[32,24,128]{2,1,0:T(8,128)S(1)} %all-to-all-done.received, f32[4,128]{1,0:T(4,128)S(1)} %bitcast.16, s32[1,512]{1,0:T(1,128)S(1)} %bitcast.14, f32[512,128]{1,0:T(8,128)S(1)} %copy-done, ...), custom_call_target="tpu_custom_call", output_to_operand_aliasing={{}: (6, {})} | custom-call | flops 500000000 | bytes 20000000 | tf_op jit(solution)/shard_map/correct1/pallas_call | solution.py:325
  60.9 36.0 %all-to-all-done.2 = f32[32,256,128]{2,1,0:T(8,128)} async-done(((f32[32,256,128]{2,1,0:T(8,128)}), f32[32,256,128]{2,1,0:T(8,128)}, u32[]{:S(2)}, u32[]{:S(2)}) %all-to-all-start.2) | async-done | bytes 4194336 | tf_op jit(solution)/shard_map/all_to_all | solution.py:557
  96.8 4.9 %all-to-all-start.1 = ((f32[32,256,128]{2,1,0:T(8,128)}), f32[32,256,128]{2,1,0:T(8,128)}, u32[]{:S(2)}, u32[]{:S(2)}) async-start(f32[32,256,128]{2,1,0:T(8,128)} %bitcast.19), calls=%async_computation.1 | async-start | bytes 8388608 | tf_op jit(solution)/shard_map/all_to_all | solution.py:557
  102.0 3.3 %collective-permute-start.1 = (f32[3,16]{1,0:T(4,128)S(1)}, f32[3,16]{1,0:T(4,128)S(1)}, u32[]{:S(2)}, u32[]{:S(2)}) collective-permute-start(f32[3,16]{1,0:T(4,128)S(1)} %broadcast_multiply_fusion), channel_id=1, source_target_pairs={{0,64},{32,96},{64,0},{96,32},{1,65},{33,97},{65,1},{97,33},{2,66}... | collective-permute-start | bytes 584 | tf_op jit(solution)/shard_map/ppermute | solution.py:512
  105.2 1.1 collective-permute-start.2
  106.3 1.0 collective-permute-start
  107.3 1.6 collective-permute-done.2
  108.8 2.3 collective-permute-done
  111.7 8.5 %lines0.1 = (f32[32,5,2,2,16,128]{5,4,3,2,1,0:T(8,128)}, f32[32,3,2,2,16,128]{5,4,3,2,1,0:T(8,128)}) custom-call(f32[32,8,2,2,8,128]{5,4,3,2,1,0:T(8,128)} %bitcast.9.field, bf16[2,256,768]{2,1,0:T(8,128)(2,1)} %constant.73.clone.left, bf16[2,768,256]{2,1,0:T(8,128)(2,1)} %constant.74.clone.right), custom_call_target="tpu_custom_call" | custom-call | flops 5000000000 | bytes 10000000 | tf_op jit(solution)/shard_map/lines0/pallas_call | solution.py:404
  120.2 35.0 %all-to-all-done.1 = f32[32,256,128]{2,1,0:T(8,128)} async-done(((f32[32,256,128]{2,1,0:T(8,128)}), f32[32,256,128]{2,1,0:T(8,128)}, u32[]{:S(2)}, u32[]{:S(2)}) %all-to-all-start.1) | async-done | bytes 4194336 | tf_op jit(solution)/shard_map/all_to_all | solution.py:557
  155.2 7.0 %lines1.1 = (f32[32,5,2,2,16,128]{5,4,3,2,1,0:T(8,128)}, f32[32,3,2,2,16,128]{5,4,3,2,1,0:T(8,128)}) custom-call(f32[32,8,2,2,8,128]{5,4,3,2,1,0:T(8,128)} %bitcast.7.field, bf16[2,256,768]{2,1,0:T(8,128)(2,1)} %constant.73.clone.left, bf16[2,768,256]{2,1,0:T(8,128)(2,1)} %constant.74.clone.right, ...), custom_call_target="tpu_custom_call", output_to_operand_aliasing={{0}: (3, {}), {1}: (4, {})} | custom-call | flops 5000000000 | bytes 10000000 | tf_op jit(solution)/shard_map/lines1/pallas_call | solution.py:404
  162.2 67.1 %all_to_all.25 = f32[32,5,2,2,16,128]{5,4,3,2,1,0:T(8,128)} all-to-all(f32[32,5,2,2,16,128]{5,4,3,2,1,0:T(8,128)} %get-tuple-element.31), channel_id=1, replica_groups=mesh['band'=4,'grid'=32] {'grid'}, dimensions={0} | all-to-all | bytes 10485760 | tf_op jit(solution)/shard_map/all_to_all | solution.py:557
  229.3 4.6 %all-to-all-start.3 = ((f32[32,3,2,2,16,128]{5,4,3,2,1,0:T(8,128)}), f32[32,3,2,2,16,128]{5,4,3,2,1,0:T(8,128)S(1)}, u32[]{:S(2)}, u32[]{:S(2)}) async-start(f32[32,3,2,2,16,128]{5,4,3,2,1,0:T(8,128)} %get-tuple-element.30), calls=%async_computation.3 | async-start | bytes 6291456 | tf_op jit(solution)/shard_map/all_to_all | solution.py:557
  233.9 9.1 %finish0.1 = (f32[2,2,8,256,256]{4,3,2,1,0:T(8,128)}, f32[5,32,256]{2,1,0:T(8,128)}, f32[5,32,256]{2,1,0:T(8,128)}, f32[5,32,256]{2,1,0:T(8,128)}, f32[5,32,256]...) custom-call(s32[1]{0:T(128)} %bitcast.band, ...), custom_call_target="tpu_custom_call" | custom-call | flops 5000000000 | bytes 15000000 | tf_op jit(solution)/shard_map/finish0/pallas_call | solution.py:452
  243.0 1.6 collective-permute-start.4
  244.7 1.7 collective-permute-start.8
  246.3 1.8 collective-permute-start.3
  248.1 2.8 collective-permute-done.4
  252.3 1.6 collective-permute-start.7
  254.8 1.7 collective-permute-start.9
  256.5 3.8 %collective-permute-done.5 = f32[5,32,256]{2,1,0:T(8,128)S(1)} collective-permute-done((f32[5,32,256]{2,1,0:T(8,128)S(1)}, f32[5,32,256]{2,1,0:T(8,128)S(1)}, u32[]{:S(2)}, u32[]{:S(2)}) %collective-permute-start.5) | collective-permute-done | bytes 163872 | tf_op jit(solution)/shard_map/ppermute | solution.py:512
  260.3 1.6 add_add_fusion.1.refs_0_
  262.3 1.6 add_add_fusion.refs_1_
  264.0 2.8 collective-permute-start.12
  266.8 2.0 collective-permute-start.10
  268.8 1.2 collective-permute-done.6.rest_1_.refs_2_
  270.0 1.3 collective-permute-done.12.rest_4_.refs_5_
  271.3 2.4 collective-permute-start.14
  273.7 2.0 all-to-all-done.3
  277.3 6.3 %finish5.1 = (f32[2,2,8,256,256]{4,3,2,1,0:T(8,128)}, f32[3,64,256]{2,1,0:T(8,128)}, f32[3,64,256]{2,1,0:T(8,128)}, f32[3,64,256]{2,1,0:T(8,128)}, f32[3,64,256]{2,1,0:T(8,128)}) custom-call(s32[1]{0:T(128)} %bitcast.band, f32[32,3,2,2,2,8,128]{6,5,4,3,2,1,0:T(8,128)} %bitcast.21, f32[8,256,256]{2,1,0:T(8,128)} %potential.7, ...), custom_call_target="tpu_custom_call", output_to_operand_aliasing={{0}: (4, {})} | custom-call | flops 3000000000 | bytes 9000000 | tf_op jit(solution)/shard_map/finish5/pallas_call | solution.py:452
  283.6 1.6 collective-permute-start.15
  285.2 2.9 collective-permute-start.16
  288.1 1.3 collective-permute-start.17
  289.5 3.8 %collect0.1 = (f32[8,256,256]{2,1,0:T(8,128)}, f32[8,128]{1,0:T(8,128)}) custom-call(s32[1]{0:T(128)} %bitcast.band, f32[5,32,256]{2,1,0:T(8,128)} %add_add_fusion.1.refs_0_, f32[5,32,256]{2,1,0:T(8,128)} %add_add_fusion.refs_1_, f32[5,32,256]{2,1,0:T(8,128)} %copy-done.7, f32[5,32,256]{2,1,0:T(8,128)} %collective-permute-done.10.rest_2_.refs_3_, ...), custom_call_target="tpu_custom_call" | custom-call | bytes 3000000 | tf_op jit(solution)/shard_map/collect0/pallas_call | solution.py:488
  293.3 1.8 collective-permute-done.16.across
  296.7 2.2 collective-permute-start.20
  298.9 1.1 collective-permute-start.19
  300.8 3.4 %collective-permute-done.20.refs_3_ = f32[3,64,256]{2,1,0:T(8,128)S(1)} collective-permute-done((f32[3,64,256]{2,1,0:T(8,128)S(1)}, f32[3,64,256]{2,1,0:T(8,128)S(1)}, u32[]{:S(2)}, u32[]{:S(2)}) %collective-permute-start.20) | collective-permute-done | bytes 196640 | tf_op jit(solution)/shard_map/ppermute | solution.py:512
  304.2 1.9 collective-permute-done.19.refs_2_
  306.2 2.0 collective-permute-done.18.refs_1_
  308.2 1.5 collect5.1
  (54 shorter events, 7.9 us)
Async XLA Ops:
  12.8 18.6 %all-to-all-start = ((f32[32,24,128]{2,1,0:T(8,128)}), f32[32,24,128]{2,1,0:T(8,128)S(1)}, u32[]{:S(2)}, u32[]{:S(2)}) async-start(f32[32,24,128]{2,1,0:T(8,128)} %get-tuple-element.26), calls=%async_computation | async-start | bytes 786432 | tf_op jit(solution)/shard_map/all_to_all | solution.py:557
  21.1 8.2 %copy-start.9 = (s32[512]{0:T(512)S(1)}, s32[512]{0:T(512)}, u32[]{:S(2)}) copy-start(s32[512]{0:T(512)} %param.16) | copy-start | bytes 6148
  21.1 8.2 %copy-start.11 = (f32[512]{0:T(512)S(1)}, f32[512]{0:T(512)}, u32[]{:S(2)}) copy-start(f32[512]{0:T(512)} %param.17) | copy-start | bytes 6148
  21.1 8.4 %copy-start.10 = (s32[512]{0:T(512)S(1)}, s32[512]{0:T(512)}, u32[]{:S(2)}) copy-start(s32[512]{0:T(512)} %block.1) | copy-start | bytes 6148
  21.1 10.3 %copy-start = (f32[512,128]{1,0:T(8,128)S(1)}, f32[512,128]{1,0:T(8,128)}, u32[]{:S(2)}) copy-start(f32[512,128]{1,0:T(8,128)} %get-tuple-element.27.masked) | copy-start | bytes 786436
  21.1 10.3 %copy-start.3 = (s32[512]{0:T(512)S(1)}, s32[512]{0:T(512)}, u32[]{:S(2)}) copy-start(s32[512]{0:T(512)} %param.13) | copy-start | bytes 6148
  21.2 10.3 %copy-start.4 = (bf16[2,8,128]{2,1,0:T(8,128)(2,1)S(1)}, bf16[2,8,128]{2,1,0:T(8,128)(2,1)}, u32[]{:S(2)}) copy-start(bf16[2,8,128]{2,1,0:T(8,128)(2,1)} %constant.77.right) | copy-start | bytes 12292
  37.6 59.2 %all-to-all-start.2 = ((f32[32,256,128]{2,1,0:T(8,128)}), f32[32,256,128]{2,1,0:T(8,128)}, u32[]{:S(2)}, u32[]{:S(2)}) async-start(f32[32,256,128]{2,1,0:T(8,128)} %bitcast.18), calls=%async_computation.2 | async-start | bytes 8388608 | tf_op jit(solution)/shard_map/all_to_all | solution.py:557
  43.4 8.2 %copy-start.1 = (bf16[2,768,256]{2,1,0:T(8,128)(2,1)S(1)}, bf16[2,768,256]{2,1,0:T(8,128)(2,1)}, u32[]{:S(2)}) copy-start(bf16[2,768,256]{2,1,0:T(8,128)(2,1)} %constant.74.clone.right) | copy-start | bytes 2359300
  96.8 58.4 %all-to-all-start.1 = ((f32[32,256,128]{2,1,0:T(8,128)}), f32[32,256,128]{2,1,0:T(8,128)}, u32[]{:S(2)}, u32[]{:S(2)}) async-start(f32[32,256,128]{2,1,0:T(8,128)} %bitcast.19), calls=%async_computation.1 | async-start | bytes 8388608 | tf_op jit(solution)/shard_map/all_to_all | solution.py:557
  102.0 5.3 %collective-permute-start.1 = (f32[3,16]{1,0:T(4,128)S(1)}, f32[3,16]{1,0:T(4,128)S(1)}, u32[]{:S(2)}, u32[]{:S(2)}) collective-permute-start(f32[3,16]{1,0:T(4,128)S(1)} %broadcast_multiply_fusion), channel_id=1, source_target_pairs={{0,64},{32,96},{64,0},{96,32},{1,65},{33,97},{65,1},{97,33},{2,66}... | collective-permute-start | bytes 584 | tf_op jit(solution)/shard_map/ppermute | solution.py:512
  105.2 3.6 %collective-permute-start.2 = (f32[3,16]{1,0:T(4,128)S(1)}, f32[3,16]{1,0:T(4,128)S(1)}, u32[]{:S(2)}, u32[]{:S(2)}) collective-permute-start(f32[3,16]{1,0:T(4,128)S(1)} %broadcast_multiply_fusion), channel_id=1, source_target_pairs={{0,96},{32,0},{64,32},{96,64},{1,97},{33,1},{65,33},{97,65},{2,98}... | collective-permute-start | bytes 584 | tf_op jit(solution)/shard_map/ppermute | solution.py:512
  106.3 4.8 %collective-permute-start = (f32[3,16]{1,0:T(4,128)S(1)}, f32[3,16]{1,0:T(4,128)S(1)}, u32[]{:S(2)}, u32[]{:S(2)}) collective-permute-start(f32[3,16]{1,0:T(4,128)S(1)} %broadcast_multiply_fusion), channel_id=1, source_target_pairs={{0,32},{32,64},{64,96},{96,0},{1,33},{33,65},{65,97},{97,1},{2,34}... | collective-permute-start | bytes 584 | tf_op jit(solution)/shard_map/ppermute | solution.py:512
  229.3 46.4 %all-to-all-start.3 = ((f32[32,3,2,2,16,128]{5,4,3,2,1,0:T(8,128)}), f32[32,3,2,2,16,128]{5,4,3,2,1,0:T(8,128)S(1)}, u32[]{:S(2)}, u32[]{:S(2)}) async-start(f32[32,3,2,2,16,128]{5,4,3,2,1,0:T(8,128)} %get-tuple-element.30), calls=%async_computation.3 | async-start | bytes 6291456 | tf_op jit(solution)/shard_map/all_to_all | solution.py:557
  243.0 7.9 %collective-permute-start.4 = (f32[5,32,256]{2,1,0:T(8,128)}, f32[5,32,256]{2,1,0:T(8,128)S(1)}, u32[]{:S(2)}, u32[]{:S(2)}) collective-permute-start(f32[5,32,256]{2,1,0:T(8,128)} %get-tuple-element.36), channel_id=1, source_target_pairs={{0,32},{32,64},{64,96},{96,0},{1,33},{33,65},{65,97},{97,1},{2,34}... | collective-permute-start | bytes 491528 | tf_op jit(solution)/shard_map/ppermute | solution.py:512
  244.7 9.2 %collective-permute-start.8 = (f32[5,32,256]{2,1,0:T(8,128)}, f32[5,32,256]{2,1,0:T(8,128)S(1)}, u32[]{:S(2)}, u32[]{:S(2)}) collective-permute-start(f32[5,32,256]{2,1,0:T(8,128)} %get-tuple-element.40), channel_id=1, source_target_pairs={{0,96},{32,0},{64,32},{96,64},{1,97},{33,1},{65,33},{97,65},{2,98}... | collective-permute-start | bytes 491528 | tf_op jit(solution)/shard_map/ppermute | solution.py:512
  246.3 10.2 %collective-permute-start.3 = (f32[5,32,256]{2,1,0:T(8,128)}, f32[5,32,256]{2,1,0:T(8,128)S(1)}, u32[]{:S(2)}, u32[]{:S(2)}) collective-permute-start(f32[5,32,256]{2,1,0:T(8,128)} %get-tuple-element.34), channel_id=1, source_target_pairs={{0,96},{32,0},{64,32},{96,64},{1,97},{33,1},{65,33},{97,65},{2,98}... | collective-permute-start | bytes 491528 | tf_op jit(solution)/shard_map/ppermute | solution.py:512
  251.9 8.4 %collective-permute-start.5 = (f32[5,32,256]{2,1,0:T(8,128)S(1)}, f32[5,32,256]{2,1,0:T(8,128)S(1)}, u32[]{:S(2)}, u32[]{:S(2)}) collective-permute-start(f32[5,32,256]{2,1,0:T(8,128)S(1)} %add.58), channel_id=1, source_target_pairs={{0,32},{32,64},{64,96},{96,0},{1,33},{33,65},{65,97},{97,1},{2,34}... | collective-permute-start | bytes 491528 | tf_op jit(solution)/shard_map/ppermute | solution.py:512
  252.3 10.1 %collective-permute-start.7 = (f32[5,32,256]{2,1,0:T(8,128)}, f32[5,32,256]{2,1,0:T(8,128)S(1)}, u32[]{:S(2)}, u32[]{:S(2)}) collective-permute-start(f32[5,32,256]{2,1,0:T(8,128)} %get-tuple-element.38), channel_id=1, source_target_pairs={{0,32},{32,64},{64,96},{96,0},{1,33},{33,65},{65,97},{97,1},{2,34}... | collective-permute-start | bytes 491528 | tf_op jit(solution)/shard_map/ppermute | solution.py:512
  254.8 7.5 %collective-permute-start.9 = (f32[5,32,256]{2,1,0:T(8,128)S(1)}, f32[5,32,256]{2,1,0:T(8,128)S(1)}, u32[]{:S(2)}, u32[]{:S(2)}) collective-permute-start(f32[5,32,256]{2,1,0:T(8,128)S(1)} %add.61), channel_id=1, source_target_pairs={{0,96},{32,0},{64,32},{96,64},{1,97},{33,1},{65,33},{97,65},{2,98}... | collective-permute-start | bytes 491528 | tf_op jit(solution)/shard_map/ppermute | solution.py:512
  261.9 8.1 %collective-permute-start.6 = (f32[5,32,256]{2,1,0:T(8,128)}, f32[5,32,256]{2,1,0:T(8,128)S(1)}, u32[]{:S(2)}, u32[]{:S(2)}) collective-permute-start(f32[5,32,256]{2,1,0:T(8,128)} %add_add_fusion.1.refs_0_), channel_id=1, source_target_pairs={{0,32},{32,64},{64,96},{96,0},{1,33},{33,65},{65,97},{97,1},{2,34}... | collective-permute-start | bytes 491528 | tf_op jit(solution)/shard_map/ppermute | solution.py:512
  264.0 7.3 %collective-permute-start.12 = (f32[5,32,256]{2,1,0:T(8,128)}, f32[5,32,256]{2,1,0:T(8,128)S(1)}, u32[]{:S(2)}, u32[]{:S(2)}) collective-permute-start(f32[5,32,256]{2,1,0:T(8,128)} %add_add_fusion.refs_1_), channel_id=1, source_target_pairs={{0,96},{32,0},{64,32},{96,64},{1,97},{33,1},{65,33},{97,65},{2,98}... | collective-permute-start | bytes 491528 | tf_op jit(solution)/shard_map/ppermute | solution.py:512
  266.8 8.9 %collective-permute-start.11 = (f32[5,32,256]{2,1,0:T(8,128)}, f32[5,32,256]{2,1,0:T(8,128)}, u32[]{:S(2)}, u32[]{:S(2)}) collective-permute-start(f32[5,32,256]{2,1,0:T(8,128)} %add_add_fusion.1.refs_0_), channel_id=1, source_target_pairs={{0,96},{32,0},{64,32},{96,64},{1,97},{33,1},{65,33},{97,65},{2,98}... | collective-permute-start | bytes 491528 | tf_op jit(solution)/shard_map/ppermute | solution.py:512
  266.8 8.9 %collective-permute-start.10 = (f32[5,32,256]{2,1,0:T(8,128)}, f32[5,32,256]{2,1,0:T(8,128)}, u32[]{:S(2)}, u32[]{:S(2)}) collective-permute-start(f32[5,32,256]{2,1,0:T(8,128)} %add_add_fusion.refs_1_), channel_id=1, source_target_pairs={{0,32},{32,64},{64,96},{96,0},{1,33},{33,65},{65,97},{97,1},{2,34}... | collective-permute-start | bytes 491528 | tf_op jit(solution)/shard_map/ppermute | solution.py:512
  270.0 6.7 %copy-start.7 = (f32[5,32,256]{2,1,0:T(8,128)}, f32[5,32,256]{2,1,0:T(8,128)S(1)}, u32[]{:S(2)}) copy-start(f32[5,32,256]{2,1,0:T(8,128)S(1)} %collective-permute-done.6.rest_1_.refs_2_) | copy-start | bytes 491524
  270.0 6.6 %collective-permute-start.13 = (f32[5,32,256]{2,1,0:T(8,128)S(1)}, f32[5,32,256]{2,1,0:T(8,128)}, u32[]{:S(2)}, u32[]{:S(2)}) collective-permute-start(f32[5,32,256]{2,1,0:T(8,128)S(1)} %collective-permute-done.6.rest_1_.refs_2_), channel_id=1, source_target_pairs={{0,32},{32,64},{64,96},{96,0},{1,33},{33,65},{65,97},{97,1},{2,34}... | collective-permute-start | bytes 491528 | tf_op jit(solution)/shard_map/ppermute | solution.py:512
  271.3 5.4 %copy-start.8 = (f32[5,32,256]{2,1,0:T(8,128)}, f32[5,32,256]{2,1,0:T(8,128)S(1)}, u32[]{:S(2)}) copy-start(f32[5,32,256]{2,1,0:T(8,128)S(1)} %collective-permute-done.12.rest_4_.refs_5_) | copy-start | bytes 491524
  271.3 5.4 %collective-permute-start.14 = (f32[5,32,256]{2,1,0:T(8,128)S(1)}, f32[5,32,256]{2,1,0:T(8,128)}, u32[]{:S(2)}, u32[]{:S(2)}) collective-permute-start(f32[5,32,256]{2,1,0:T(8,128)S(1)} %collective-permute-done.12.rest_4_.refs_5_), channel_id=1, source_target_pairs={{0,96},{32,0},{64,32},{96,64},{1,97},{33,1},{65,33},{97,65},{2,98}... | collective-permute-start | bytes 491528 | tf_op jit(solution)/shard_map/ppermute | solution.py:512
  275.7 1.6 copy-start.6
  283.6 9.6 %collective-permute-start.15 = (f32[3,64,256]{2,1,0:T(8,128)}, f32[3,64,256]{2,1,0:T(8,128)S(1)}, u32[]{:S(2)}, u32[]{:S(2)}) collective-permute-start(f32[3,64,256]{2,1,0:T(8,128)} %get-tuple-element.43), channel_id=1, source_target_pairs={{0,32},{32,64},{64,96},{96,0},{1,33},{33,65},{65,97},{97,1},{2,34}... | collective-permute-start | bytes 589832 | tf_op jit(solution)/shard_map/ppermute | solution.py:512
  285.2 9.8 %collective-permute-start.16 = (f32[3,64,256]{2,1,0:T(8,128)}, f32[3,64,256]{2,1,0:T(8,128)S(1)}, u32[]{:S(2)}, u32[]{:S(2)}) collective-permute-start(f32[3,64,256]{2,1,0:T(8,128)} %get-tuple-element.44), channel_id=1, source_target_pairs={{0,64},{32,96},{64,0},{96,32},{1,65},{33,97},{65,1},{97,33},{2,66}... | collective-permute-start | bytes 589832 | tf_op jit(solution)/shard_map/ppermute | solution.py:512
  288.1 6.9 %collective-permute-start.17 = (f32[3,64,256]{2,1,0:T(8,128)}, f32[3,64,256]{2,1,0:T(8,128)S(1)}, u32[]{:S(2)}, u32[]{:S(2)}) collective-permute-start(f32[3,64,256]{2,1,0:T(8,128)} %get-tuple-element.45), channel_id=1, source_target_pairs={{0,96},{32,0},{64,32},{96,64},{1,97},{33,1},{65,33},{97,65},{2,98}... | collective-permute-start | bytes 589832 | tf_op jit(solution)/shard_map/ppermute | solution.py:512
  295.1 0.9 copy-start.2
  296.0 0.7 copy-start.5
  296.7 7.5 %collective-permute-start.20 = (f32[3,64,256]{2,1,0:T(8,128)S(1)}, f32[3,64,256]{2,1,0:T(8,128)S(1)}, u32[]{:S(2)}, u32[]{:S(2)}) collective-permute-start(f32[3,64,256]{2,1,0:T(8,128)S(1)} %add.86.refs_0_), channel_id=1, source_target_pairs={{0,96},{32,0},{64,32},{96,64},{1,97},{33,1},{65,33},{97,65},{2,98}... | collective-permute-start | bytes 589832 | tf_op jit(solution)/shard_map/ppermute | solution.py:512
  298.9 7.3 %collective-permute-start.19 = (f32[3,64,256]{2,1,0:T(8,128)S(1)}, f32[3,64,256]{2,1,0:T(8,128)S(1)}, u32[]{:S(2)}, u32[]{:S(2)}) collective-permute-start(f32[3,64,256]{2,1,0:T(8,128)S(1)} %add.86.refs_0_), channel_id=1, source_target_pairs={{0,64},{32,96},{64,0},{96,32},{1,65},{33,97},{65,1},{97,33},{2,66}... | collective-permute-start | bytes 589832 | tf_op jit(solution)/shard_map/ppermute | solution.py:512
  300.0 8.1 %collective-permute-start.18 = (f32[3,64,256]{2,1,0:T(8,128)S(1)}, f32[3,64,256]{2,1,0:T(8,128)S(1)}, u32[]{:S(2)}, u32[]{:S(2)}) collective-permute-start(f32[3,64,256]{2,1,0:T(8,128)S(1)} %add.86.refs_0_), channel_id=1, source_target_pairs={{0,32},{32,64},{64,96},{96,0},{1,33},{33,65},{65,97},{97,1},{2,34}... | collective-permute-start | bytes 589832 | tf_op jit(solution)/shard_map/ppermute | solution.py:512

commit v6 on v5

--- a/solution.py
+++ b/solution.py
@@ -148,7 +148,7 @@
         counts[pl.ds(entry, 1), :] = jnp.full((1, LANES), count[entry], jnp.int32)
         return carry
 
-    lax.fori_loop(0, ENTRIES, first, 0, unroll=8)
+    lax.fori_loop(0, ENTRIES, first, 0, unroll=32)
     cosine, sine = cos_sin((0.5 * TIME_STEP) * rows[4])
     rows[4] = cosine
     rows[5] = sine
@@ -159,7 +159,7 @@
             rows[k, pl.ds(entry, 1), :] = orbs[k, pl.ds(place(entry), 1), :]
             return carry
 
-        lax.fori_loop(0, ENTRIES, step, 0, unroll=8)
+        lax.fori_loop(0, ENTRIES, step, 0, unroll=32)
 
     projectors_copy.wait()
     piece = 64
@@ -299,7 +299,7 @@
             field[at[c], :] = both[c]
         return carry
 
-    lax.fori_loop(0, ENTRIES, step, 0, unroll=8)
+    lax.fori_loop(0, ENTRIES, step, 0, unroll=32)
     if n in EARLY:
         tiles = field.reshape(GROUPS * 8, 2, 2, 8, LANES)
 

time: 311 us -> 310 us (level)
  no operation moved by 1% of the time
where the time goes in v6:
time: 310 us; the launch traced here: 308 us
  waiting for transfers between devices  97.6 us (31%)
  Pallas kernels  79.7 us (26%)
  blocking collectives  67.1 us (22%)
  starting transfers between devices  54.7 us (18%)
  other arithmetic  6.12 us (2%)
    all_to_all x4, waiting for transfers between devices, exchange(): lax.all_to_all(array, 'grid', split_axis=0, concat_axis=0, tiled=True)  74.1 us
    all_to_all x1, blocking collectives, exchange(): lax.all_to_all(array, 'grid', split_axis=0, concat_axis=0, tiled=True)  67.1 us
    ppermute x21, starting transfers between devices, onward(): lax.ppermute(array, 'band', [(b, (b + steps) % BANDS) for b in range(BAND...  31.2 us
    ppermute x21, waiting for transfers between devices, onward(): lax.ppermute(array, 'band', [(b, (b + steps) % BANDS) for b in range(BAND...  23.5 us
    all_to_all x4, starting transfers between devices, exchange(): lax.all_to_all(array, 'grid', split_axis=0, concat_axis=0, tiled=True)  23.4 us
    pallas_call x2, Pallas kernels, shift(): pl.pallas_call(shift_kernel, grid=(GROUPS // SHIFT_STEP,), out_shape=pltp...  16.3 us
    pallas_call x2, Pallas kernels, correct(): pl.pallas_call(functools.partial(correct_kernel, n), out_shape=pltpu.HBM(...  16.1 us
    pallas_call x2, Pallas kernels, lines(): pl.pallas_call(functools.partial(lines_kernel, n), grid=(8 // LINES_STEP,...  15.5 us
  transfers between devices with their start and end apart: 25, of which 17 were waited for; matrix products, arithmetic and copies ran while one was open for 2% of the time, Pallas kernels for 15%

profile of v6, /device:TPU:0, one launch (start us, length us, event | category | flops | bytes accessed | tf_op | source)
XLA Modules:
  0.0 308.4 jit_solution(1576197989362117159)
XLA Ops:
  0.6 11.1 %project.1 = (f32[32,24,128]{2,1,0:T(8,128)}, f32[512,128]{1,0:T(8,128)}) custom-call(s32[512]{0:T(512)} %block.1, s32[512]{0:T(512)} %count.1, s32[1,512]{1,0:T(1,128)} %bitcast.12, s32[1,512]{1,0:T(1,128)} %bitcast.23, f32[4,2048,256]{2,1,0:T(8,128)} %bitcast.17, f32[2048,256]{1,0:T(8,128)} %bitcast.20, f32[4,512,128]{2,1,0:T(8,128)} %projectors_hbm.1), custom_call_target="tpu_custom_call" | custom-call | flops 1000000000 | bytes 36000000 | tf_op jit(solution)/shard_map/project/pallas_call | solution.py:215
  11.7 8.3 %all-to-all-start = ((f32[32,24,128]{2,1,0:T(8,128)}), f32[32,24,128]{2,1,0:T(8,128)S(1)}, u32[]{:S(2)}, u32[]{:S(2)}) async-start(f32[32,24,128]{2,1,0:T(8,128)} %get-tuple-element.26), calls=%async_computation | async-start | bytes 786432 | tf_op jit(solution)/shard_map/all_to_all | solution.py:557
  20.1 8.1 %shift0.1.before = f32[8192,128]{1,0:T(8,128)} custom-call(f32[2,2,8,256,256]{4,3,2,1,0:T(8,128)} %orbs.3, f32[8,256,256]{2,1,0:T(8,128)} %potential.7), custom_call_target="tpu_custom_call" | custom-call | flops 100000000 | bytes 11000000 | tf_op jit(solution)/shard_map/shift0/pallas_call | solution.py:259
  28.5 1.8 all-to-all-done.received
  30.3 6.1 %correct0.1.rest_0_ = f32[8192,128]{1,0:T(8,128)} custom-call(s32[512]{0:T(512)S(1)} %fusion.3.place, f32[32,24,128]{2,1,0:T(8,128)S(1)} %all-to-all-done.received, f32[4,128]{1,0:T(4,128)S(1)} %bitcast.15, s32[1,512]{1,0:T(1,128)S(1)} %bitcast.13, f32[512,128]{1,0:T(8,128)S(1)} %copy-done, ...), custom_call_target="tpu_custom_call", output_to_operand_aliasing={{}: (6, {})} | custom-call | flops 500000000 | bytes 20000000 | tf_op jit(solution)/shard_map/correct0/pallas_call | solution.py:325
  36.4 5.7 %all-to-all-start.2 = ((f32[32,256,128]{2,1,0:T(8,128)}), f32[32,256,128]{2,1,0:T(8,128)}, u32[]{:S(2)}, u32[]{:S(2)}) async-start(f32[32,256,128]{2,1,0:T(8,128)} %bitcast.18), calls=%async_computation.2 | async-start | bytes 8388608 | tf_op jit(solution)/shard_map/all_to_all | solution.py:557
  42.2 8.2 %shift1.1.before = f32[8192,128]{1,0:T(8,128)} custom-call(f32[2,2,8,256,256]{4,3,2,1,0:T(8,128)} %orbs.3, f32[8,256,256]{2,1,0:T(8,128)} %potential.7, f32[8192,128]{1,0:T(8,128)} %correct0.1.rest_0_), custom_call_target="tpu_custom_call" | custom-call | flops 100000000 | bytes 11000000 | tf_op jit(solution)/shard_map/shift1/pallas_call | solution.py:259
  50.4 10.0 %correct1.1 = f32[8192,128]{1,0:T(8,128)} custom-call(s32[512]{0:T(512)S(1)} %fusion.3.place, f32[32,24,128]{2,1,0:T(8,128)S(1)} %all-to-all-done.received, f32[4,128]{1,0:T(4,128)S(1)} %bitcast.16, s32[1,512]{1,0:T(1,128)S(1)} %bitcast.14, f32[512,128]{1,0:T(8,128)S(1)} %copy-done, ...), custom_call_target="tpu_custom_call", output_to_operand_aliasing={{}: (6, {})} | custom-call | flops 500000000 | bytes 20000000 | tf_op jit(solution)/shard_map/correct1/pallas_call | solution.py:325
  60.4 35.2 %all-to-all-done.2 = f32[32,256,128]{2,1,0:T(8,128)} async-done(((f32[32,256,128]{2,1,0:T(8,128)}), f32[32,256,128]{2,1,0:T(8,128)}, u32[]{:S(2)}, u32[]{:S(2)}) %all-to-all-start.2) | async-done | bytes 4194336 | tf_op jit(solution)/shard_map/all_to_all | solution.py:557
  95.6 4.9 %all-to-all-start.1 = ((f32[32,256,128]{2,1,0:T(8,128)}), f32[32,256,128]{2,1,0:T(8,128)}, u32[]{:S(2)}, u32[]{:S(2)}) async-start(f32[32,256,128]{2,1,0:T(8,128)} %bitcast.19), calls=%async_computation.1 | async-start | bytes 8388608 | tf_op jit(solution)/shard_map/all_to_all | solution.py:557
  100.8 3.3 %collective-permute-start.1 = (f32[3,16]{1,0:T(4,128)S(1)}, f32[3,16]{1,0:T(4,128)S(1)}, u32[]{:S(2)}, u32[]{:S(2)}) collective-permute-start(f32[3,16]{1,0:T(4,128)S(1)} %broadcast_multiply_fusion), channel_id=1, source_target_pairs={{0,64},{32,96},{64,0},{96,32},{1,65},{33,97},{65,1},{97,33},{2,66}... | collective-permute-start | bytes 584 | tf_op jit(solution)/shard_map/ppermute | solution.py:512
  104.0 1.1 collective-permute-start.2
  105.1 1.0 collective-permute-start
  106.1 1.6 collective-permute-done.2
  107.6 2.3 collective-permute-done
  110.5 8.5 %lines0.1 = (f32[32,5,2,2,16,128]{5,4,3,2,1,0:T(8,128)}, f32[32,3,2,2,16,128]{5,4,3,2,1,0:T(8,128)}) custom-call(f32[32,8,2,2,8,128]{5,4,3,2,1,0:T(8,128)} %bitcast.9.field, bf16[2,256,768]{2,1,0:T(8,128)(2,1)} %constant.73.clone.left, bf16[2,768,256]{2,1,0:T(8,128)(2,1)} %constant.74.clone.right), custom_call_target="tpu_custom_call" | custom-call | flops 5000000000 | bytes 10000000 | tf_op jit(solution)/shard_map/lines0/pallas_call | solution.py:404
  119.0 35.0 %all-to-all-done.1 = f32[32,256,128]{2,1,0:T(8,128)} async-done(((f32[32,256,128]{2,1,0:T(8,128)}), f32[32,256,128]{2,1,0:T(8,128)}, u32[]{:S(2)}, u32[]{:S(2)}) %all-to-all-start.1) | async-done | bytes 4194336 | tf_op jit(solution)/shard_map/all_to_all | solution.py:557
  154.0 7.0 %lines1.1 = (f32[32,5,2,2,16,128]{5,4,3,2,1,0:T(8,128)}, f32[32,3,2,2,16,128]{5,4,3,2,1,0:T(8,128)}) custom-call(f32[32,8,2,2,8,128]{5,4,3,2,1,0:T(8,128)} %bitcast.7.field, bf16[2,256,768]{2,1,0:T(8,128)(2,1)} %constant.73.clone.left, bf16[2,768,256]{2,1,0:T(8,128)(2,1)} %constant.74.clone.right, ...), custom_call_target="tpu_custom_call", output_to_operand_aliasing={{0}: (3, {}), {1}: (4, {})} | custom-call | flops 5000000000 | bytes 10000000 | tf_op jit(solution)/shard_map/lines1/pallas_call | solution.py:404
  161.0 67.1 %all_to_all.25 = f32[32,5,2,2,16,128]{5,4,3,2,1,0:T(8,128)} all-to-all(f32[32,5,2,2,16,128]{5,4,3,2,1,0:T(8,128)} %get-tuple-element.31), channel_id=1, replica_groups=mesh['band'=4,'grid'=32] {'grid'}, dimensions={0} | all-to-all | bytes 10485760 | tf_op jit(solution)/shard_map/all_to_all | solution.py:557
  228.1 4.6 %all-to-all-start.3 = ((f32[32,3,2,2,16,128]{5,4,3,2,1,0:T(8,128)}), f32[32,3,2,2,16,128]{5,4,3,2,1,0:T(8,128)S(1)}, u32[]{:S(2)}, u32[]{:S(2)}) async-start(f32[32,3,2,2,16,128]{5,4,3,2,1,0:T(8,128)} %get-tuple-element.30), calls=%async_computation.3 | async-start | bytes 6291456 | tf_op jit(solution)/shard_map/all_to_all | solution.py:557
  232.7 9.1 %finish0.1 = (f32[2,2,8,256,256]{4,3,2,1,0:T(8,128)}, f32[5,32,256]{2,1,0:T(8,128)}, f32[5,32,256]{2,1,0:T(8,128)}, f32[5,32,256]{2,1,0:T(8,128)}, f32[5,32,256]...) custom-call(s32[1]{0:T(128)} %bitcast.band, ...), custom_call_target="tpu_custom_call" | custom-call | flops 5000000000 | bytes 15000000 | tf_op jit(solution)/shard_map/finish0/pallas_call | solution.py:452
  241.8 1.6 collective-permute-start.4
  243.5 1.7 collective-permute-start.8
  245.1 1.8 collective-permute-start.3
  246.9 2.8 collective-permute-done.4
  251.1 1.6 collective-permute-start.7
  253.6 1.7 collective-permute-start.9
  255.3 3.8 %collective-permute-done.5 = f32[5,32,256]{2,1,0:T(8,128)S(1)} collective-permute-done((f32[5,32,256]{2,1,0:T(8,128)S(1)}, f32[5,32,256]{2,1,0:T(8,128)S(1)}, u32[]{:S(2)}, u32[]{:S(2)}) %collective-permute-start.5) | collective-permute-done | bytes 163872 | tf_op jit(solution)/shard_map/ppermute | solution.py:512
  259.1 1.6 add_add_fusion.1.refs_0_
  261.1 1.6 add_add_fusion.refs_1_
  262.7 2.8 collective-permute-start.12
  265.6 2.0 collective-permute-start.10
  267.6 1.2 collective-permute-done.6.rest_1_.refs_2_
  268.8 1.3 collective-permute-done.12.rest_4_.refs_5_
  270.1 2.4 collective-permute-start.14
  272.4 2.0 all-to-all-done.3
  276.1 6.3 %finish5.1 = (f32[2,2,8,256,256]{4,3,2,1,0:T(8,128)}, f32[3,64,256]{2,1,0:T(8,128)}, f32[3,64,256]{2,1,0:T(8,128)}, f32[3,64,256]{2,1,0:T(8,128)}, f32[3,64,256]{2,1,0:T(8,128)}) custom-call(s32[1]{0:T(128)} %bitcast.band, f32[32,3,2,2,2,8,128]{6,5,4,3,2,1,0:T(8,128)} %bitcast.21, f32[8,256,256]{2,1,0:T(8,128)} %potential.7, ...), custom_call_target="tpu_custom_call", output_to_operand_aliasing={{0}: (4, {})} | custom-call | flops 3000000000 | bytes 9000000 | tf_op jit(solution)/shard_map/finish5/pallas_call | solution.py:452
  282.4 1.6 collective-permute-start.15
  284.0 2.9 collective-permute-start.16
  286.9 1.3 collective-permute-start.17
  288.3 3.8 %collect0.1 = (f32[8,256,256]{2,1,0:T(8,128)}, f32[8,128]{1,0:T(8,128)}) custom-call(s32[1]{0:T(128)} %bitcast.band, f32[5,32,256]{2,1,0:T(8,128)} %add_add_fusion.1.refs_0_, f32[5,32,256]{2,1,0:T(8,128)} %add_add_fusion.refs_1_, f32[5,32,256]{2,1,0:T(8,128)} %copy-done.7, f32[5,32,256]{2,1,0:T(8,128)} %collective-permute-done.10.rest_2_.refs_3_, ...), custom_call_target="tpu_custom_call" | custom-call | bytes 3000000 | tf_op jit(solution)/shard_map/collect0/pallas_call | solution.py:488
  292.0 1.8 collective-permute-done.16.across
  295.5 2.2 collective-permute-start.20
  297.7 1.1 collective-permute-start.19
  299.6 3.4 %collective-permute-done.20.refs_3_ = f32[3,64,256]{2,1,0:T(8,128)S(1)} collective-permute-done((f32[3,64,256]{2,1,0:T(8,128)S(1)}, f32[3,64,256]{2,1,0:T(8,128)S(1)}, u32[]{:S(2)}, u32[]{:S(2)}) %collective-permute-start.20) | collective-permute-done | bytes 196640 | tf_op jit(solution)/shard_map/ppermute | solution.py:512
  303.0 1.9 collective-permute-done.19.refs_2_
  305.0 2.0 collective-permute-done.18.refs_1_
  307.0 1.5 collect5.1
  (54 shorter events, 7.9 us)
Async XLA Ops:
  11.7 18.6 %all-to-all-start = ((f32[32,24,128]{2,1,0:T(8,128)}), f32[32,24,128]{2,1,0:T(8,128)S(1)}, u32[]{:S(2)}, u32[]{:S(2)}) async-start(f32[32,24,128]{2,1,0:T(8,128)} %get-tuple-element.26), calls=%async_computation | async-start | bytes 786432 | tf_op jit(solution)/shard_map/all_to_all | solution.py:557
  20.0 8.2 %copy-start.9 = (s32[512]{0:T(512)S(1)}, s32[512]{0:T(512)}, u32[]{:S(2)}) copy-start(s32[512]{0:T(512)} %param.16) | copy-start | bytes 6148
  20.0 8.2 %copy-start.11 = (f32[512]{0:T(512)S(1)}, f32[512]{0:T(512)}, u32[]{:S(2)}) copy-start(f32[512]{0:T(512)} %param.17) | copy-start | bytes 6148
  20.0 8.4 %copy-start.10 = (s32[512]{0:T(512)S(1)}, s32[512]{0:T(512)}, u32[]{:S(2)}) copy-start(s32[512]{0:T(512)} %block.1) | copy-start | bytes 6148
  20.1 10.3 %copy-start = (f32[512,128]{1,0:T(8,128)S(1)}, f32[512,128]{1,0:T(8,128)}, u32[]{:S(2)}) copy-start(f32[512,128]{1,0:T(8,128)} %get-tuple-element.27.masked) | copy-start | bytes 786436
  20.1 10.3 %copy-start.3 = (s32[512]{0:T(512)S(1)}, s32[512]{0:T(512)}, u32[]{:S(2)}) copy-start(s32[512]{0:T(512)} %param.13) | copy-start | bytes 6148
  20.1 10.3 %copy-start.4 = (bf16[2,8,128]{2,1,0:T(8,128)(2,1)S(1)}, bf16[2,8,128]{2,1,0:T(8,128)(2,1)}, u32[]{:S(2)}) copy-start(bf16[2,8,128]{2,1,0:T(8,128)(2,1)} %constant.77.right) | copy-start | bytes 12292
  36.4 59.2 %all-to-all-start.2 = ((f32[32,256,128]{2,1,0:T(8,128)}), f32[32,256,128]{2,1,0:T(8,128)}, u32[]{:S(2)}, u32[]{:S(2)}) async-start(f32[32,256,128]{2,1,0:T(8,128)} %bitcast.18), calls=%async_computation.2 | async-start | bytes 8388608 | tf_op jit(solution)/shard_map/all_to_all | solution.py:557
  42.1 8.2 %copy-start.1 = (bf16[2,768,256]{2,1,0:T(8,128)(2,1)S(1)}, bf16[2,768,256]{2,1,0:T(8,128)(2,1)}, u32[]{:S(2)}) copy-start(bf16[2,768,256]{2,1,0:T(8,128)(2,1)} %constant.74.clone.right) | copy-start | bytes 2359300
  95.6 58.4 %all-to-all-start.1 = ((f32[32,256,128]{2,1,0:T(8,128)}), f32[32,256,128]{2,1,0:T(8,128)}, u32[]{:S(2)}, u32[]{:S(2)}) async-start(f32[32,256,128]{2,1,0:T(8,128)} %bitcast.19), calls=%async_computation.1 | async-start | bytes 8388608 | tf_op jit(solution)/shard_map/all_to_all | solution.py:557
  100.8 5.3 %collective-permute-start.1 = (f32[3,16]{1,0:T(4,128)S(1)}, f32[3,16]{1,0:T(4,128)S(1)}, u32[]{:S(2)}, u32[]{:S(2)}) collective-permute-start(f32[3,16]{1,0:T(4,128)S(1)} %broadcast_multiply_fusion), channel_id=1, source_target_pairs={{0,64},{32,96},{64,0},{96,32},{1,65},{33,97},{65,1},{97,33},{2,66}... | collective-permute-start | bytes 584 | tf_op jit(solution)/shard_map/ppermute | solution.py:512
  104.0 3.6 %collective-permute-start.2 = (f32[3,16]{1,0:T(4,128)S(1)}, f32[3,16]{1,0:T(4,128)S(1)}, u32[]{:S(2)}, u32[]{:S(2)}) collective-permute-start(f32[3,16]{1,0:T(4,128)S(1)} %broadcast_multiply_fusion), channel_id=1, source_target_pairs={{0,96},{32,0},{64,32},{96,64},{1,97},{33,1},{65,33},{97,65},{2,98}... | collective-permute-start | bytes 584 | tf_op jit(solution)/shard_map/ppermute | solution.py:512
  105.1 4.8 %collective-permute-start = (f32[3,16]{1,0:T(4,128)S(1)}, f32[3,16]{1,0:T(4,128)S(1)}, u32[]{:S(2)}, u32[]{:S(2)}) collective-permute-start(f32[3,16]{1,0:T(4,128)S(1)} %broadcast_multiply_fusion), channel_id=1, source_target_pairs={{0,32},{32,64},{64,96},{96,0},{1,33},{33,65},{65,97},{97,1},{2,34}... | collective-permute-start | bytes 584 | tf_op jit(solution)/shard_map/ppermute | solution.py:512
  228.1 46.4 %all-to-all-start.3 = ((f32[32,3,2,2,16,128]{5,4,3,2,1,0:T(8,128)}), f32[32,3,2,2,16,128]{5,4,3,2,1,0:T(8,128)S(1)}, u32[]{:S(2)}, u32[]{:S(2)}) async-start(f32[32,3,2,2,16,128]{5,4,3,2,1,0:T(8,128)} %get-tuple-element.30), calls=%async_computation.3 | async-start | bytes 6291456 | tf_op jit(solution)/shard_map/all_to_all | solution.py:557
  241.8 7.9 %collective-permute-start.4 = (f32[5,32,256]{2,1,0:T(8,128)}, f32[5,32,256]{2,1,0:T(8,128)S(1)}, u32[]{:S(2)}, u32[]{:S(2)}) collective-permute-start(f32[5,32,256]{2,1,0:T(8,128)} %get-tuple-element.36), channel_id=1, source_target_pairs={{0,32},{32,64},{64,96},{96,0},{1,33},{33,65},{65,97},{97,1},{2,34}... | collective-permute-start | bytes 491528 | tf_op jit(solution)/shard_map/ppermute | solution.py:512
  243.5 9.2 %collective-permute-start.8 = (f32[5,32,256]{2,1,0:T(8,128)}, f32[5,32,256]{2,1,0:T(8,128)S(1)}, u32[]{:S(2)}, u32[]{:S(2)}) collective-permute-start(f32[5,32,256]{2,1,0:T(8,128)} %get-tuple-element.40), channel_id=1, source_target_pairs={{0,96},{32,0},{64,32},{96,64},{1,97},{33,1},{65,33},{97,65},{2,98}... | collective-permute-start | bytes 491528 | tf_op jit(solution)/shard_map/ppermute | solution.py:512
  245.1 10.2 %collective-permute-start.3 = (f32[5,32,256]{2,1,0:T(8,128)}, f32[5,32,256]{2,1,0:T(8,128)S(1)}, u32[]{:S(2)}, u32[]{:S(2)}) collective-permute-start(f32[5,32,256]{2,1,0:T(8,128)} %get-tuple-element.34), channel_id=1, source_target_pairs={{0,96},{32,0},{64,32},{96,64},{1,97},{33,1},{65,33},{97,65},{2,98}... | collective-permute-start | bytes 491528 | tf_op jit(solution)/shard_map/ppermute | solution.py:512
  250.7 8.4 %collective-permute-start.5 = (f32[5,32,256]{2,1,0:T(8,128)S(1)}, f32[5,32,256]{2,1,0:T(8,128)S(1)}, u32[]{:S(2)}, u32[]{:S(2)}) collective-permute-start(f32[5,32,256]{2,1,0:T(8,128)S(1)} %add.58), channel_id=1, source_target_pairs={{0,32},{32,64},{64,96},{96,0},{1,33},{33,65},{65,97},{97,1},{2,34}... | collective-permute-start | bytes 491528 | tf_op jit(solution)/shard_map/ppermute | solution.py:512
  251.1 10.1 %collective-permute-start.7 = (f32[5,32,256]{2,1,0:T(8,128)}, f32[5,32,256]{2,1,0:T(8,128)S(1)}, u32[]{:S(2)}, u32[]{:S(2)}) collective-permute-start(f32[5,32,256]{2,1,0:T(8,128)} %get-tuple-element.38), channel_id=1, source_target_pairs={{0,32},{32,64},{64,96},{96,0},{1,33},{33,65},{65,97},{97,1},{2,34}... | collective-permute-start | bytes 491528 | tf_op jit(solution)/shard_map/ppermute | solution.py:512
  253.6 7.5 %collective-permute-start.9 = (f32[5,32,256]{2,1,0:T(8,128)S(1)}, f32[5,32,256]{2,1,0:T(8,128)S(1)}, u32[]{:S(2)}, u32[]{:S(2)}) collective-permute-start(f32[5,32,256]{2,1,0:T(8,128)S(1)} %add.61), channel_id=1, source_target_pairs={{0,96},{32,0},{64,32},{96,64},{1,97},{33,1},{65,33},{97,65},{2,98}... | collective-permute-start | bytes 491528 | tf_op jit(solution)/shard_map/ppermute | solution.py:512
  260.7 8.1 %collective-permute-start.6 = (f32[5,32,256]{2,1,0:T(8,128)}, f32[5,32,256]{2,1,0:T(8,128)S(1)}, u32[]{:S(2)}, u32[]{:S(2)}) collective-permute-start(f32[5,32,256]{2,1,0:T(8,128)} %add_add_fusion.1.refs_0_), channel_id=1, source_target_pairs={{0,32},{32,64},{64,96},{96,0},{1,33},{33,65},{65,97},{97,1},{2,34}... | collective-permute-start | bytes 491528 | tf_op jit(solution)/shard_map/ppermute | solution.py:512
  262.7 7.3 %collective-permute-start.12 = (f32[5,32,256]{2,1,0:T(8,128)}, f32[5,32,256]{2,1,0:T(8,128)S(1)}, u32[]{:S(2)}, u32[]{:S(2)}) collective-permute-start(f32[5,32,256]{2,1,0:T(8,128)} %add_add_fusion.refs_1_), channel_id=1, source_target_pairs={{0,96},{32,0},{64,32},{96,64},{1,97},{33,1},{65,33},{97,65},{2,98}... | collective-permute-start | bytes 491528 | tf_op jit(solution)/shard_map/ppermute | solution.py:512
  265.6 8.9 %collective-permute-start.11 = (f32[5,32,256]{2,1,0:T(8,128)}, f32[5,32,256]{2,1,0:T(8,128)}, u32[]{:S(2)}, u32[]{:S(2)}) collective-permute-start(f32[5,32,256]{2,1,0:T(8,128)} %add_add_fusion.1.refs_0_), channel_id=1, source_target_pairs={{0,96},{32,0},{64,32},{96,64},{1,97},{33,1},{65,33},{97,65},{2,98}... | collective-permute-start | bytes 491528 | tf_op jit(solution)/shard_map/ppermute | solution.py:512
  265.6 8.9 %collective-permute-start.10 = (f32[5,32,256]{2,1,0:T(8,128)}, f32[5,32,256]{2,1,0:T(8,128)}, u32[]{:S(2)}, u32[]{:S(2)}) collective-permute-start(f32[5,32,256]{2,1,0:T(8,128)} %add_add_fusion.refs_1_), channel_id=1, source_target_pairs={{0,32},{32,64},{64,96},{96,0},{1,33},{33,65},{65,97},{97,1},{2,34}... | collective-permute-start | bytes 491528 | tf_op jit(solution)/shard_map/ppermute | solution.py:512
  268.8 6.7 %copy-start.7 = (f32[5,32,256]{2,1,0:T(8,128)}, f32[5,32,256]{2,1,0:T(8,128)S(1)}, u32[]{:S(2)}) copy-start(f32[5,32,256]{2,1,0:T(8,128)S(1)} %collective-permute-done.6.rest_1_.refs_2_) | copy-start | bytes 491524
  268.8 6.6 %collective-permute-start.13 = (f32[5,32,256]{2,1,0:T(8,128)S(1)}, f32[5,32,256]{2,1,0:T(8,128)}, u32[]{:S(2)}, u32[]{:S(2)}) collective-permute-start(f32[5,32,256]{2,1,0:T(8,128)S(1)} %collective-permute-done.6.rest_1_.refs_2_), channel_id=1, source_target_pairs={{0,32},{32,64},{64,96},{96,0},{1,33},{33,65},{65,97},{97,1},{2,34}... | collective-permute-start | bytes 491528 | tf_op jit(solution)/shard_map/ppermute | solution.py:512
  270.1 5.4 %copy-start.8 = (f32[5,32,256]{2,1,0:T(8,128)}, f32[5,32,256]{2,1,0:T(8,128)S(1)}, u32[]{:S(2)}) copy-start(f32[5,32,256]{2,1,0:T(8,128)S(1)} %collective-permute-done.12.rest_4_.refs_5_) | copy-start | bytes 491524
  270.1 5.4 %collective-permute-start.14 = (f32[5,32,256]{2,1,0:T(8,128)S(1)}, f32[5,32,256]{2,1,0:T(8,128)}, u32[]{:S(2)}, u32[]{:S(2)}) collective-permute-start(f32[5,32,256]{2,1,0:T(8,128)S(1)} %collective-permute-done.12.rest_4_.refs_5_), channel_id=1, source_target_pairs={{0,96},{32,0},{64,32},{96,64},{1,97},{33,1},{65,33},{97,65},{2,98}... | collective-permute-start | bytes 491528 | tf_op jit(solution)/shard_map/ppermute | solution.py:512
  274.5 1.6 copy-start.6
  282.4 9.6 %collective-permute-start.15 = (f32[3,64,256]{2,1,0:T(8,128)}, f32[3,64,256]{2,1,0:T(8,128)S(1)}, u32[]{:S(2)}, u32[]{:S(2)}) collective-permute-start(f32[3,64,256]{2,1,0:T(8,128)} %get-tuple-element.43), channel_id=1, source_target_pairs={{0,32},{32,64},{64,96},{96,0},{1,33},{33,65},{65,97},{97,1},{2,34}... | collective-permute-start | bytes 589832 | tf_op jit(solution)/shard_map/ppermute | solution.py:512
  284.0 9.8 %collective-permute-start.16 = (f32[3,64,256]{2,1,0:T(8,128)}, f32[3,64,256]{2,1,0:T(8,128)S(1)}, u32[]{:S(2)}, u32[]{:S(2)}) collective-permute-start(f32[3,64,256]{2,1,0:T(8,128)} %get-tuple-element.44), channel_id=1, source_target_pairs={{0,64},{32,96},{64,0},{96,32},{1,65},{33,97},{65,1},{97,33},{2,66}... | collective-permute-start | bytes 589832 | tf_op jit(solution)/shard_map/ppermute | solution.py:512
  286.9 6.9 %collective-permute-start.17 = (f32[3,64,256]{2,1,0:T(8,128)}, f32[3,64,256]{2,1,0:T(8,128)S(1)}, u32[]{:S(2)}, u32[]{:S(2)}) collective-permute-start(f32[3,64,256]{2,1,0:T(8,128)} %get-tuple-element.45), channel_id=1, source_target_pairs={{0,96},{32,0},{64,32},{96,64},{1,97},{33,1},{65,33},{97,65},{2,98}... | collective-permute-start | bytes 589832 | tf_op jit(solution)/shard_map/ppermute | solution.py:512
  293.8 0.9 copy-start.2
  294.8 0.7 copy-start.5
  295.5 7.5 %collective-permute-start.20 = (f32[3,64,256]{2,1,0:T(8,128)S(1)}, f32[3,64,256]{2,1,0:T(8,128)S(1)}, u32[]{:S(2)}, u32[]{:S(2)}) collective-permute-start(f32[3,64,256]{2,1,0:T(8,128)S(1)} %add.86.refs_0_), channel_id=1, source_target_pairs={{0,96},{32,0},{64,32},{96,64},{1,97},{33,1},{65,33},{97,65},{2,98}... | collective-permute-start | bytes 589832 | tf_op jit(solution)/shard_map/ppermute | solution.py:512
  297.7 7.3 %collective-permute-start.19 = (f32[3,64,256]{2,1,0:T(8,128)S(1)}, f32[3,64,256]{2,1,0:T(8,128)S(1)}, u32[]{:S(2)}, u32[]{:S(2)}) collective-permute-start(f32[3,64,256]{2,1,0:T(8,128)S(1)} %add.86.refs_0_), channel_id=1, source_target_pairs={{0,64},{32,96},{64,0},{96,32},{1,65},{33,97},{65,1},{97,33},{2,66}... | collective-permute-start | bytes 589832 | tf_op jit(solution)/shard_map/ppermute | solution.py:512
  298.8 8.1 %collective-permute-start.18 = (f32[3,64,256]{2,1,0:T(8,128)S(1)}, f32[3,64,256]{2,1,0:T(8,128)S(1)}, u32[]{:S(2)}, u32[]{:S(2)}) collective-permute-start(f32[3,64,256]{2,1,0:T(8,128)S(1)} %add.86.refs_0_), channel_id=1, source_target_pairs={{0,32},{32,64},{64,96},{96,0},{1,33},{33,65},{65,97},{97,1},{2,34}... | collective-permute-start | bytes 589832 | tf_op jit(solution)/shard_map/ppermute | solution.py:512

commit v7 on v6

--- a/solution.py
+++ b/solution.py
@@ -184,7 +184,7 @@
         table[at, :] = out
         return carry
 
-    lax.fori_loop(0, ENTRIES // piece, reduce, 0)
+    lax.fori_loop(0, ENTRIES // piece, reduce, 0, unroll=2)
     turned = jnp.transpose(table[...])[:16]
     sums = lax.dot_general(
         three_parts(turned), atom_matrix(atom_ref), (((1,), (1,)), ((), ())), preferred_element_type=jnp.float32

time: 310 us -> 309 us (level)
  no operation moved by 1% of the time
where the time goes in v7:
time: 309 us; the launch traced here: 308 us
  waiting for transfers between devices  97.6 us (32%)
  Pallas kernels  79.4 us (26%)
  blocking collectives  67.1 us (22%)
  starting transfers between devices  54.7 us (18%)
  other arithmetic  6.12 us (2%)
    all_to_all x4, waiting for transfers between devices, exchange(): lax.all_to_all(array, 'grid', split_axis=0, concat_axis=0, tiled=True)  74.1 us
    all_to_all x1, blocking collectives, exchange(): lax.all_to_all(array, 'grid', split_axis=0, concat_axis=0, tiled=True)  67.1 us
    ppermute x21, starting transfers between devices, onward(): lax.ppermute(array, 'band', [(b, (b + steps) % BANDS) for b in range(BAND...  31.2 us
    ppermute x21, waiting for transfers between devices, onward(): lax.ppermute(array, 'band', [(b, (b + steps) % BANDS) for b in range(BAND...  23.5 us
    all_to_all x4, starting transfers between devices, exchange(): lax.all_to_all(array, 'grid', split_axis=0, concat_axis=0, tiled=True)  23.4 us
    pallas_call x2, Pallas kernels, shift(): pl.pallas_call(shift_kernel, grid=(GROUPS // SHIFT_STEP,), out_shape=pltp...  16.3 us
    pallas_call x2, Pallas kernels, correct(): pl.pallas_call(functools.partial(correct_kernel, n), out_shape=pltpu.HBM(...  16.1 us
    pallas_call x2, Pallas kernels, lines(): pl.pallas_call(functools.partial(lines_kernel, n), grid=(8 // LINES_STEP,...  15.5 us
  transfers between devices with their start and end apart: 25, of which 17 were waited for; matrix products, arithmetic and copies ran while one was open for 2% of the time, Pallas kernels for 15%

profile of v7, /device:TPU:0, one launch (start us, length us, event | category | flops | bytes accessed | tf_op | source)
XLA Modules:
  0.0 308.1 jit_solution(12366078016569089651)
XLA Ops:
  0.6 10.8 %project.1 = (f32[32,24,128]{2,1,0:T(8,128)}, f32[512,128]{1,0:T(8,128)}) custom-call(s32[512]{0:T(512)} %block.1, s32[512]{0:T(512)} %count.1, s32[1,512]{1,0:T(1,128)} %bitcast.12, s32[1,512]{1,0:T(1,128)} %bitcast.23, f32[4,2048,256]{2,1,0:T(8,128)} %bitcast.17, f32[2048,256]{1,0:T(8,128)} %bitcast.20, f32[4,512,128]{2,1,0:T(8,128)} %projectors_hbm.1), custom_call_target="tpu_custom_call" | custom-call | flops 1000000000 | bytes 36000000 | tf_op jit(solution)/shard_map/project/pallas_call | solution.py:215
  11.4 8.3 %all-to-all-start = ((f32[32,24,128]{2,1,0:T(8,128)}), f32[32,24,128]{2,1,0:T(8,128)S(1)}, u32[]{:S(2)}, u32[]{:S(2)}) async-start(f32[32,24,128]{2,1,0:T(8,128)} %get-tuple-element.26), calls=%async_computation | async-start | bytes 786432 | tf_op jit(solution)/shard_map/all_to_all | solution.py:557
  19.8 8.1 %shift0.1.before = f32[8192,128]{1,0:T(8,128)} custom-call(f32[2,2,8,256,256]{4,3,2,1,0:T(8,128)} %orbs.3, f32[8,256,256]{2,1,0:T(8,128)} %potential.7), custom_call_target="tpu_custom_call" | custom-call | flops 100000000 | bytes 11000000 | tf_op jit(solution)/shard_map/shift0/pallas_call | solution.py:259
  28.2 1.8 all-to-all-done.received
  30.0 6.1 %correct0.1.rest_0_ = f32[8192,128]{1,0:T(8,128)} custom-call(s32[512]{0:T(512)S(1)} %fusion.3.place, f32[32,24,128]{2,1,0:T(8,128)S(1)} %all-to-all-done.received, f32[4,128]{1,0:T(4,128)S(1)} %bitcast.15, s32[1,512]{1,0:T(1,128)S(1)} %bitcast.13, f32[512,128]{1,0:T(8,128)S(1)} %copy-done, ...), custom_call_target="tpu_custom_call", output_to_operand_aliasing={{}: (6, {})} | custom-call | flops 500000000 | bytes 20000000 | tf_op jit(solution)/shard_map/correct0/pallas_call | solution.py:325
  36.1 5.7 %all-to-all-start.2 = ((f32[32,256,128]{2,1,0:T(8,128)}), f32[32,256,128]{2,1,0:T(8,128)}, u32[]{:S(2)}, u32[]{:S(2)}) async-start(f32[32,256,128]{2,1,0:T(8,128)} %bitcast.18), calls=%async_computation.2 | async-start | bytes 8388608 | tf_op jit(solution)/shard_map/all_to_all | solution.py:557
  41.8 8.2 %shift1.1.before = f32[8192,128]{1,0:T(8,128)} custom-call(f32[2,2,8,256,256]{4,3,2,1,0:T(8,128)} %orbs.3, f32[8,256,256]{2,1,0:T(8,128)} %potential.7, f32[8192,128]{1,0:T(8,128)} %correct0.1.rest_0_), custom_call_target="tpu_custom_call" | custom-call | flops 100000000 | bytes 11000000 | tf_op jit(solution)/shard_map/shift1/pallas_call | solution.py:259
  50.0 10.0 %correct1.1 = f32[8192,128]{1,0:T(8,128)} custom-call(s32[512]{0:T(512)S(1)} %fusion.3.place, f32[32,24,128]{2,1,0:T(8,128)S(1)} %all-to-all-done.received, f32[4,128]{1,0:T(4,128)S(1)} %bitcast.16, s32[1,512]{1,0:T(1,128)S(1)} %bitcast.14, f32[512,128]{1,0:T(8,128)S(1)} %copy-done, ...), custom_call_target="tpu_custom_call", output_to_operand_aliasing={{}: (6, {})} | custom-call | flops 500000000 | bytes 20000000 | tf_op jit(solution)/shard_map/correct1/pallas_call | solution.py:325
  60.1 35.2 %all-to-all-done.2 = f32[32,256,128]{2,1,0:T(8,128)} async-done(((f32[32,256,128]{2,1,0:T(8,128)}), f32[32,256,128]{2,1,0:T(8,128)}, u32[]{:S(2)}, u32[]{:S(2)}) %all-to-all-start.2) | async-done | bytes 4194336 | tf_op jit(solution)/shard_map/all_to_all | solution.py:557
  95.3 4.9 %all-to-all-start.1 = ((f32[32,256,128]{2,1,0:T(8,128)}), f32[32,256,128]{2,1,0:T(8,128)}, u32[]{:S(2)}, u32[]{:S(2)}) async-start(f32[32,256,128]{2,1,0:T(8,128)} %bitcast.19), calls=%async_computation.1 | async-start | bytes 8388608 | tf_op jit(solution)/shard_map/all_to_all | solution.py:557
  100.4 3.3 %collective-permute-start.1 = (f32[3,16]{1,0:T(4,128)S(1)}, f32[3,16]{1,0:T(4,128)S(1)}, u32[]{:S(2)}, u32[]{:S(2)}) collective-permute-start(f32[3,16]{1,0:T(4,128)S(1)} %broadcast_multiply_fusion), channel_id=1, source_target_pairs={{0,64},{32,96},{64,0},{96,32},{1,65},{33,97},{65,1},{97,33},{2,66}... | collective-permute-start | bytes 584 | tf_op jit(solution)/shard_map/ppermute | solution.py:512
  103.7 1.1 collective-permute-start.2
  104.7 1.0 collective-permute-start
  105.7 1.6 collective-permute-done.2
  107.3 2.3 collective-permute-done
  110.1 8.5 %lines0.1 = (f32[32,5,2,2,16,128]{5,4,3,2,1,0:T(8,128)}, f32[32,3,2,2,16,128]{5,4,3,2,1,0:T(8,128)}) custom-call(f32[32,8,2,2,8,128]{5,4,3,2,1,0:T(8,128)} %bitcast.9.field, bf16[2,256,768]{2,1,0:T(8,128)(2,1)} %constant.73.clone.left, bf16[2,768,256]{2,1,0:T(8,128)(2,1)} %constant.74.clone.right), custom_call_target="tpu_custom_call" | custom-call | flops 5000000000 | bytes 10000000 | tf_op jit(solution)/shard_map/lines0/pallas_call | solution.py:404
  118.6 35.0 %all-to-all-done.1 = f32[32,256,128]{2,1,0:T(8,128)} async-done(((f32[32,256,128]{2,1,0:T(8,128)}), f32[32,256,128]{2,1,0:T(8,128)}, u32[]{:S(2)}, u32[]{:S(2)}) %all-to-all-start.1) | async-done | bytes 4194336 | tf_op jit(solution)/shard_map/all_to_all | solution.py:557
  153.7 7.0 %lines1.1 = (f32[32,5,2,2,16,128]{5,4,3,2,1,0:T(8,128)}, f32[32,3,2,2,16,128]{5,4,3,2,1,0:T(8,128)}) custom-call(f32[32,8,2,2,8,128]{5,4,3,2,1,0:T(8,128)} %bitcast.7.field, bf16[2,256,768]{2,1,0:T(8,128)(2,1)} %constant.73.clone.left, bf16[2,768,256]{2,1,0:T(8,128)(2,1)} %constant.74.clone.right, ...), custom_call_target="tpu_custom_call", output_to_operand_aliasing={{0}: (3, {}), {1}: (4, {})} | custom-call | flops 5000000000 | bytes 10000000 | tf_op jit(solution)/shard_map/lines1/pallas_call | solution.py:404
  160.7 67.1 %all_to_all.25 = f32[32,5,2,2,16,128]{5,4,3,2,1,0:T(8,128)} all-to-all(f32[32,5,2,2,16,128]{5,4,3,2,1,0:T(8,128)} %get-tuple-element.31), channel_id=1, replica_groups=mesh['band'=4,'grid'=32] {'grid'}, dimensions={0} | all-to-all | bytes 10485760 | tf_op jit(solution)/shard_map/all_to_all | solution.py:557
  227.8 4.6 %all-to-all-start.3 = ((f32[32,3,2,2,16,128]{5,4,3,2,1,0:T(8,128)}), f32[32,3,2,2,16,128]{5,4,3,2,1,0:T(8,128)S(1)}, u32[]{:S(2)}, u32[]{:S(2)}) async-start(f32[32,3,2,2,16,128]{5,4,3,2,1,0:T(8,128)} %get-tuple-element.30), calls=%async_computation.3 | async-start | bytes 6291456 | tf_op jit(solution)/shard_map/all_to_all | solution.py:557
  232.4 9.1 %finish0.1 = (f32[2,2,8,256,256]{4,3,2,1,0:T(8,128)}, f32[5,32,256]{2,1,0:T(8,128)}, f32[5,32,256]{2,1,0:T(8,128)}, f32[5,32,256]{2,1,0:T(8,128)}, f32[5,32,256]...) custom-call(s32[1]{0:T(128)} %bitcast.band, ...), custom_call_target="tpu_custom_call" | custom-call | flops 5000000000 | bytes 15000000 | tf_op jit(solution)/shard_map/finish0/pallas_call | solution.py:452
  241.5 1.6 collective-permute-start.4
  243.1 1.7 collective-permute-start.8
  244.8 1.8 collective-permute-start.3
  246.6 2.8 collective-permute-done.4
  250.7 1.6 collective-permute-start.7
  253.3 1.7 collective-permute-start.9
  255.0 3.8 %collective-permute-done.5 = f32[5,32,256]{2,1,0:T(8,128)S(1)} collective-permute-done((f32[5,32,256]{2,1,0:T(8,128)S(1)}, f32[5,32,256]{2,1,0:T(8,128)S(1)}, u32[]{:S(2)}, u32[]{:S(2)}) %collective-permute-start.5) | collective-permute-done | bytes 163872 | tf_op jit(solution)/shard_map/ppermute | solution.py:512
  258.8 1.6 add_add_fusion.1.refs_0_
  260.8 1.6 add_add_fusion.refs_1_
  262.4 2.8 collective-permute-start.12
  265.3 2.0 collective-permute-start.10
  267.3 1.2 collective-permute-done.6.rest_1_.refs_2_
  268.5 1.3 collective-permute-done.12.rest_4_.refs_5_
  269.8 2.4 collective-permute-start.14
  272.1 2.0 all-to-all-done.3
  275.8 6.3 %finish5.1 = (f32[2,2,8,256,256]{4,3,2,1,0:T(8,128)}, f32[3,64,256]{2,1,0:T(8,128)}, f32[3,64,256]{2,1,0:T(8,128)}, f32[3,64,256]{2,1,0:T(8,128)}, f32[3,64,256]{2,1,0:T(8,128)}) custom-call(s32[1]{0:T(128)} %bitcast.band, f32[32,3,2,2,2,8,128]{6,5,4,3,2,1,0:T(8,128)} %bitcast.21, f32[8,256,256]{2,1,0:T(8,128)} %potential.7, ...), custom_call_target="tpu_custom_call", output_to_operand_aliasing={{0}: (4, {})} | custom-call | flops 3000000000 | bytes 9000000 | tf_op jit(solution)/shard_map/finish5/pallas_call | solution.py:452
  282.1 1.6 collective-permute-start.15
  283.7 2.9 collective-permute-start.16
  286.6 1.3 collective-permute-start.17
  287.9 3.8 %collect0.1 = (f32[8,256,256]{2,1,0:T(8,128)}, f32[8,128]{1,0:T(8,128)}) custom-call(s32[1]{0:T(128)} %bitcast.band, f32[5,32,256]{2,1,0:T(8,128)} %add_add_fusion.1.refs_0_, f32[5,32,256]{2,1,0:T(8,128)} %add_add_fusion.refs_1_, f32[5,32,256]{2,1,0:T(8,128)} %copy-done.7, f32[5,32,256]{2,1,0:T(8,128)} %collective-permute-done.10.rest_2_.refs_3_, ...), custom_call_target="tpu_custom_call" | custom-call | bytes 3000000 | tf_op jit(solution)/shard_map/collect0/pallas_call | solution.py:488
  291.7 1.8 collective-permute-done.16.across
  295.2 2.2 collective-permute-start.20
  297.3 1.1 collective-permute-start.19
  299.2 3.4 %collective-permute-done.20.refs_3_ = f32[3,64,256]{2,1,0:T(8,128)S(1)} collective-permute-done((f32[3,64,256]{2,1,0:T(8,128)S(1)}, f32[3,64,256]{2,1,0:T(8,128)S(1)}, u32[]{:S(2)}, u32[]{:S(2)}) %collective-permute-start.20) | collective-permute-done | bytes 196640 | tf_op jit(solution)/shard_map/ppermute | solution.py:512
  302.7 1.9 collective-permute-done.19.refs_2_
  304.6 2.0 collective-permute-done.18.refs_1_
  306.6 1.5 collect5.1
  (54 shorter events, 7.9 us)
Async XLA Ops:
  11.4 18.6 %all-to-all-start = ((f32[32,24,128]{2,1,0:T(8,128)}), f32[32,24,128]{2,1,0:T(8,128)S(1)}, u32[]{:S(2)}, u32[]{:S(2)}) async-start(f32[32,24,128]{2,1,0:T(8,128)} %get-tuple-element.26), calls=%async_computation | async-start | bytes 786432 | tf_op jit(solution)/shard_map/all_to_all | solution.py:557
  19.7 8.2 %copy-start.9 = (s32[512]{0:T(512)S(1)}, s32[512]{0:T(512)}, u32[]{:S(2)}) copy-start(s32[512]{0:T(512)} %param.16) | copy-start | bytes 6148
  19.7 8.2 %copy-start.11 = (f32[512]{0:T(512)S(1)}, f32[512]{0:T(512)}, u32[]{:S(2)}) copy-start(f32[512]{0:T(512)} %param.17) | copy-start | bytes 6148
  19.7 8.4 %copy-start.10 = (s32[512]{0:T(512)S(1)}, s32[512]{0:T(512)}, u32[]{:S(2)}) copy-start(s32[512]{0:T(512)} %block.1) | copy-start | bytes 6148
  19.7 10.3 %copy-start = (f32[512,128]{1,0:T(8,128)S(1)}, f32[512,128]{1,0:T(8,128)}, u32[]{:S(2)}) copy-start(f32[512,128]{1,0:T(8,128)} %get-tuple-element.27.masked) | copy-start | bytes 786436
  19.7 10.3 %copy-start.3 = (s32[512]{0:T(512)S(1)}, s32[512]{0:T(512)}, u32[]{:S(2)}) copy-start(s32[512]{0:T(512)} %param.13) | copy-start | bytes 6148
  19.7 10.3 %copy-start.4 = (bf16[2,8,128]{2,1,0:T(8,128)(2,1)S(1)}, bf16[2,8,128]{2,1,0:T(8,128)(2,1)}, u32[]{:S(2)}) copy-start(bf16[2,8,128]{2,1,0:T(8,128)(2,1)} %constant.77.right) | copy-start | bytes 12292
  36.1 59.2 %all-to-all-start.2 = ((f32[32,256,128]{2,1,0:T(8,128)}), f32[32,256,128]{2,1,0:T(8,128)}, u32[]{:S(2)}, u32[]{:S(2)}) async-start(f32[32,256,128]{2,1,0:T(8,128)} %bitcast.18), calls=%async_computation.2 | async-start | bytes 8388608 | tf_op jit(solution)/shard_map/all_to_all | solution.py:557
  41.8 8.2 %copy-start.1 = (bf16[2,768,256]{2,1,0:T(8,128)(2,1)S(1)}, bf16[2,768,256]{2,1,0:T(8,128)(2,1)}, u32[]{:S(2)}) copy-start(bf16[2,768,256]{2,1,0:T(8,128)(2,1)} %constant.74.clone.right) | copy-start | bytes 2359300
  95.3 58.4 %all-to-all-start.1 = ((f32[32,256,128]{2,1,0:T(8,128)}), f32[32,256,128]{2,1,0:T(8,128)}, u32[]{:S(2)}, u32[]{:S(2)}) async-start(f32[32,256,128]{2,1,0:T(8,128)} %bitcast.19), calls=%async_computation.1 | async-start | bytes 8388608 | tf_op jit(solution)/shard_map/all_to_all | solution.py:557
  100.4 5.3 %collective-permute-start.1 = (f32[3,16]{1,0:T(4,128)S(1)}, f32[3,16]{1,0:T(4,128)S(1)}, u32[]{:S(2)}, u32[]{:S(2)}) collective-permute-start(f32[3,16]{1,0:T(4,128)S(1)} %broadcast_multiply_fusion), channel_id=1, source_target_pairs={{0,64},{32,96},{64,0},{96,32},{1,65},{33,97},{65,1},{97,33},{2,66}... | collective-permute-start | bytes 584 | tf_op jit(solution)/shard_map/ppermute | solution.py:512
  103.7 3.6 %collective-permute-start.2 = (f32[3,16]{1,0:T(4,128)S(1)}, f32[3,16]{1,0:T(4,128)S(1)}, u32[]{:S(2)}, u32[]{:S(2)}) collective-permute-start(f32[3,16]{1,0:T(4,128)S(1)} %broadcast_multiply_fusion), channel_id=1, source_target_pairs={{0,96},{32,0},{64,32},{96,64},{1,97},{33,1},{65,33},{97,65},{2,98}... | collective-permute-start | bytes 584 | tf_op jit(solution)/shard_map/ppermute | solution.py:512
  104.7 4.8 %collective-permute-start = (f32[3,16]{1,0:T(4,128)S(1)}, f32[3,16]{1,0:T(4,128)S(1)}, u32[]{:S(2)}, u32[]{:S(2)}) collective-permute-start(f32[3,16]{1,0:T(4,128)S(1)} %broadcast_multiply_fusion), channel_id=1, source_target_pairs={{0,32},{32,64},{64,96},{96,0},{1,33},{33,65},{65,97},{97,1},{2,34}... | collective-permute-start | bytes 584 | tf_op jit(solution)/shard_map/ppermute | solution.py:512
  227.8 46.4 %all-to-all-start.3 = ((f32[32,3,2,2,16,128]{5,4,3,2,1,0:T(8,128)}), f32[32,3,2,2,16,128]{5,4,3,2,1,0:T(8,128)S(1)}, u32[]{:S(2)}, u32[]{:S(2)}) async-start(f32[32,3,2,2,16,128]{5,4,3,2,1,0:T(8,128)} %get-tuple-element.30), calls=%async_computation.3 | async-start | bytes 6291456 | tf_op jit(solution)/shard_map/all_to_all | solution.py:557
  241.5 7.9 %collective-permute-start.4 = (f32[5,32,256]{2,1,0:T(8,128)}, f32[5,32,256]{2,1,0:T(8,128)S(1)}, u32[]{:S(2)}, u32[]{:S(2)}) collective-permute-start(f32[5,32,256]{2,1,0:T(8,128)} %get-tuple-element.36), channel_id=1, source_target_pairs={{0,32},{32,64},{64,96},{96,0},{1,33},{33,65},{65,97},{97,1},{2,34}... | collective-permute-start | bytes 491528 | tf_op jit(solution)/shard_map/ppermute | solution.py:512
  243.1 9.2 %collective-permute-start.8 = (f32[5,32,256]{2,1,0:T(8,128)}, f32[5,32,256]{2,1,0:T(8,128)S(1)}, u32[]{:S(2)}, u32[]{:S(2)}) collective-permute-start(f32[5,32,256]{2,1,0:T(8,128)} %get-tuple-element.40), channel_id=1, source_target_pairs={{0,96},{32,0},{64,32},{96,64},{1,97},{33,1},{65,33},{97,65},{2,98}... | collective-permute-start | bytes 491528 | tf_op jit(solution)/shard_map/ppermute | solution.py:512
  244.8 10.2 %collective-permute-start.3 = (f32[5,32,256]{2,1,0:T(8,128)}, f32[5,32,256]{2,1,0:T(8,128)S(1)}, u32[]{:S(2)}, u32[]{:S(2)}) collective-permute-start(f32[5,32,256]{2,1,0:T(8,128)} %get-tuple-element.34), channel_id=1, source_target_pairs={{0,96},{32,0},{64,32},{96,64},{1,97},{33,1},{65,33},{97,65},{2,98}... | collective-permute-start | bytes 491528 | tf_op jit(solution)/shard_map/ppermute | solution.py:512
  250.4 8.4 %collective-permute-start.5 = (f32[5,32,256]{2,1,0:T(8,128)S(1)}, f32[5,32,256]{2,1,0:T(8,128)S(1)}, u32[]{:S(2)}, u32[]{:S(2)}) collective-permute-start(f32[5,32,256]{2,1,0:T(8,128)S(1)} %add.58), channel_id=1, source_target_pairs={{0,32},{32,64},{64,96},{96,0},{1,33},{33,65},{65,97},{97,1},{2,34}... | collective-permute-start | bytes 491528 | tf_op jit(solution)/shard_map/ppermute | solution.py:512
  250.7 10.1 %collective-permute-start.7 = (f32[5,32,256]{2,1,0:T(8,128)}, f32[5,32,256]{2,1,0:T(8,128)S(1)}, u32[]{:S(2)}, u32[]{:S(2)}) collective-permute-start(f32[5,32,256]{2,1,0:T(8,128)} %get-tuple-element.38), channel_id=1, source_target_pairs={{0,32},{32,64},{64,96},{96,0},{1,33},{33,65},{65,97},{97,1},{2,34}... | collective-permute-start | bytes 491528 | tf_op jit(solution)/shard_map/ppermute | solution.py:512
  253.3 7.5 %collective-permute-start.9 = (f32[5,32,256]{2,1,0:T(8,128)S(1)}, f32[5,32,256]{2,1,0:T(8,128)S(1)}, u32[]{:S(2)}, u32[]{:S(2)}) collective-permute-start(f32[5,32,256]{2,1,0:T(8,128)S(1)} %add.61), channel_id=1, source_target_pairs={{0,96},{32,0},{64,32},{96,64},{1,97},{33,1},{65,33},{97,65},{2,98}... | collective-permute-start | bytes 491528 | tf_op jit(solution)/shard_map/ppermute | solution.py:512
  260.4 8.1 %collective-permute-start.6 = (f32[5,32,256]{2,1,0:T(8,128)}, f32[5,32,256]{2,1,0:T(8,128)S(1)}, u32[]{:S(2)}, u32[]{:S(2)}) collective-permute-start(f32[5,32,256]{2,1,0:T(8,128)} %add_add_fusion.1.refs_0_), channel_id=1, source_target_pairs={{0,32},{32,64},{64,96},{96,0},{1,33},{33,65},{65,97},{97,1},{2,34}... | collective-permute-start | bytes 491528 | tf_op jit(solution)/shard_map/ppermute | solution.py:512
  262.4 7.3 %collective-permute-start.12 = (f32[5,32,256]{2,1,0:T(8,128)}, f32[5,32,256]{2,1,0:T(8,128)S(1)}, u32[]{:S(2)}, u32[]{:S(2)}) collective-permute-start(f32[5,32,256]{2,1,0:T(8,128)} %add_add_fusion.refs_1_), channel_id=1, source_target_pairs={{0,96},{32,0},{64,32},{96,64},{1,97},{33,1},{65,33},{97,65},{2,98}... | collective-permute-start | bytes 491528 | tf_op jit(solution)/shard_map/ppermute | solution.py:512
  265.3 8.9 %collective-permute-start.11 = (f32[5,32,256]{2,1,0:T(8,128)}, f32[5,32,256]{2,1,0:T(8,128)}, u32[]{:S(2)}, u32[]{:S(2)}) collective-permute-start(f32[5,32,256]{2,1,0:T(8,128)} %add_add_fusion.1.refs_0_), channel_id=1, source_target_pairs={{0,96},{32,0},{64,32},{96,64},{1,97},{33,1},{65,33},{97,65},{2,98}... | collective-permute-start | bytes 491528 | tf_op jit(solution)/shard_map/ppermute | solution.py:512
  265.3 8.9 %collective-permute-start.10 = (f32[5,32,256]{2,1,0:T(8,128)}, f32[5,32,256]{2,1,0:T(8,128)}, u32[]{:S(2)}, u32[]{:S(2)}) collective-permute-start(f32[5,32,256]{2,1,0:T(8,128)} %add_add_fusion.refs_1_), channel_id=1, source_target_pairs={{0,32},{32,64},{64,96},{96,0},{1,33},{33,65},{65,97},{97,1},{2,34}... | collective-permute-start | bytes 491528 | tf_op jit(solution)/shard_map/ppermute | solution.py:512
  268.5 6.7 %copy-start.7 = (f32[5,32,256]{2,1,0:T(8,128)}, f32[5,32,256]{2,1,0:T(8,128)S(1)}, u32[]{:S(2)}) copy-start(f32[5,32,256]{2,1,0:T(8,128)S(1)} %collective-permute-done.6.rest_1_.refs_2_) | copy-start | bytes 491524
  268.5 6.6 %collective-permute-start.13 = (f32[5,32,256]{2,1,0:T(8,128)S(1)}, f32[5,32,256]{2,1,0:T(8,128)}, u32[]{:S(2)}, u32[]{:S(2)}) collective-permute-start(f32[5,32,256]{2,1,0:T(8,128)S(1)} %collective-permute-done.6.rest_1_.refs_2_), channel_id=1, source_target_pairs={{0,32},{32,64},{64,96},{96,0},{1,33},{33,65},{65,97},{97,1},{2,34}... | collective-permute-start | bytes 491528 | tf_op jit(solution)/shard_map/ppermute | solution.py:512
  269.8 5.4 %copy-start.8 = (f32[5,32,256]{2,1,0:T(8,128)}, f32[5,32,256]{2,1,0:T(8,128)S(1)}, u32[]{:S(2)}) copy-start(f32[5,32,256]{2,1,0:T(8,128)S(1)} %collective-permute-done.12.rest_4_.refs_5_) | copy-start | bytes 491524
  269.8 5.4 %collective-permute-start.14 = (f32[5,32,256]{2,1,0:T(8,128)S(1)}, f32[5,32,256]{2,1,0:T(8,128)}, u32[]{:S(2)}, u32[]{:S(2)}) collective-permute-start(f32[5,32,256]{2,1,0:T(8,128)S(1)} %collective-permute-done.12.rest_4_.refs_5_), channel_id=1, source_target_pairs={{0,96},{32,0},{64,32},{96,64},{1,97},{33,1},{65,33},{97,65},{2,98}... | collective-permute-start | bytes 491528 | tf_op jit(solution)/shard_map/ppermute | solution.py:512
  274.2 1.6 copy-start.6
  282.1 9.6 %collective-permute-start.15 = (f32[3,64,256]{2,1,0:T(8,128)}, f32[3,64,256]{2,1,0:T(8,128)S(1)}, u32[]{:S(2)}, u32[]{:S(2)}) collective-permute-start(f32[3,64,256]{2,1,0:T(8,128)} %get-tuple-element.43), channel_id=1, source_target_pairs={{0,32},{32,64},{64,96},{96,0},{1,33},{33,65},{65,97},{97,1},{2,34}... | collective-permute-start | bytes 589832 | tf_op jit(solution)/shard_map/ppermute | solution.py:512
  283.7 9.8 %collective-permute-start.16 = (f32[3,64,256]{2,1,0:T(8,128)}, f32[3,64,256]{2,1,0:T(8,128)S(1)}, u32[]{:S(2)}, u32[]{:S(2)}) collective-permute-start(f32[3,64,256]{2,1,0:T(8,128)} %get-tuple-element.44), channel_id=1, source_target_pairs={{0,64},{32,96},{64,0},{96,32},{1,65},{33,97},{65,1},{97,33},{2,66}... | collective-permute-start | bytes 589832 | tf_op jit(solution)/shard_map/ppermute | solution.py:512
  286.6 6.9 %collective-permute-start.17 = (f32[3,64,256]{2,1,0:T(8,128)}, f32[3,64,256]{2,1,0:T(8,128)S(1)}, u32[]{:S(2)}, u32[]{:S(2)}) collective-permute-start(f32[3,64,256]{2,1,0:T(8,128)} %get-tuple-element.45), channel_id=1, source_target_pairs={{0,96},{32,0},{64,32},{96,64},{1,97},{33,1},{65,33},{97,65},{2,98}... | collective-permute-start | bytes 589832 | tf_op jit(solution)/shard_map/ppermute | solution.py:512
  293.5 0.9 copy-start.2
  294.4 0.7 copy-start.5
  295.2 7.5 %collective-permute-start.20 = (f32[3,64,256]{2,1,0:T(8,128)S(1)}, f32[3,64,256]{2,1,0:T(8,128)S(1)}, u32[]{:S(2)}, u32[]{:S(2)}) collective-permute-start(f32[3,64,256]{2,1,0:T(8,128)S(1)} %add.86.refs_0_), channel_id=1, source_target_pairs={{0,96},{32,0},{64,32},{96,64},{1,97},{33,1},{65,33},{97,65},{2,98}... | collective-permute-start | bytes 589832 | tf_op jit(solution)/shard_map/ppermute | solution.py:512
  297.3 7.3 %collective-permute-start.19 = (f32[3,64,256]{2,1,0:T(8,128)S(1)}, f32[3,64,256]{2,1,0:T(8,128)S(1)}, u32[]{:S(2)}, u32[]{:S(2)}) collective-permute-start(f32[3,64,256]{2,1,0:T(8,128)S(1)} %add.86.refs_0_), channel_id=1, source_target_pairs={{0,64},{32,96},{64,0},{96,32},{1,65},{33,97},{65,1},{97,33},{2,66}... | collective-permute-start | bytes 589832 | tf_op jit(solution)/shard_map/ppermute | solution.py:512
  298.5 8.1 %collective-permute-start.18 = (f32[3,64,256]{2,1,0:T(8,128)S(1)}, f32[3,64,256]{2,1,0:T(8,128)S(1)}, u32[]{:S(2)}, u32[]{:S(2)}) collective-permute-start(f32[3,64,256]{2,1,0:T(8,128)S(1)} %add.86.refs_0_), channel_id=1, source_target_pairs={{0,32},{32,64},{64,96},{96,0},{1,33},{33,65},{65,97},{97,1},{2,34}... | collective-permute-start | bytes 589832 | tf_op jit(solution)/shard_map/ppermute | solution.py:512
